TPU v7x, 32 devices: a whole 2x2x4 slice. The times are simulated.
32 devices in a mesh: groups: 2 (over y), gx: 16 (over z, x, core).
Axes of the slice: x: 2, y: 2, z: 4, core: 2. Of those that a mesh axis runs over, the one named last changes fastest.
Arguments:
- tokens: bfloat16 [2, 32, 18432], P(None, ('groups', 'gx')), parts along dimension 1, may hold values from -6 to 6
- norm_gain: float32 [18432], replicated, may hold values from 0.1 to 1.9
- w_query: bfloat16 [6144, 18432], P('gx'), may hold values from -0.046875 to 0.046875
- w_keyval: bfloat16 [512, 18432], P('gx'), may hold values from -0.046875 to 0.046875
- w_gate: bfloat16 [9216, 18432], P('gx'), may hold values from -0.046875 to 0.046875
- w_up: bfloat16 [9216, 18432], P('gx'), may hold values from -0.046875 to 0.046875
- w_out: bfloat16 [6144, 18432], P('gx'), may hold values from -0.078125 to 0.078125
- w_down: bfloat16 [9216, 18432], P('gx'), may hold values from -0.0625 to 0.0625
- cache_keys: bfloat16 [32, 1024, 256], P(('groups', 'gx')), parts along dimension 0
- cache_values: bfloat16 [32, 1024, 256], P(('groups', 'gx')), parts along dimension 0, may hold values from -6 to 6
- lengths: int32 [32], P(('groups', 'gx')), parts along dimension 0, may hold values from 128 to 1024, as said below
- positions: int32 [32], P(('groups', 'gx')), parts along dimension 0, may hold values from 1024 to 4095
Outputs:
- layer_out: bfloat16 [2, 32, 18432], P(None, ('groups', 'gx')), parts along dimension 1
There are 2 independent parts, one for each index of `groups`. A program takes and returns all parts, laid end to end along the dimension named above; an argument that names none is the same for every part. Nothing has to cross between parts.
Inputs may be any that keep to these rules, and one draw needn't show every extreme that they name: `lengths`: some row has all 1024 slots live.
All inputs are finite; a program needn't handle non-finite values.
Results may differ from a plain program's by a relative error of at most 0.012.
The roundings to bfloat16 on the way count: a program that leaves them out, or rounds other values in their place, can miss the bound.
Values may be sent and summed in bfloat16 or wider, within the bound.
No kernel may reach another device: no remote copies, remote signals or barrier semaphores. Data moves between devices by JAX's collectives and lax.ppermute only.
A program may use at most 320 MiB of HBM per device.

v0:
```python
import math

import jax
import jax.numpy as jnp
from jax import lax
from jax.sharding import PartitionSpec as P


def layer_norm(tokens, norm_gain):
    values = tokens.astype(jnp.float32)
    center = jnp.mean(values, axis=-1, keepdims=True)
    spread = jnp.mean((values - center) ** 2, axis=-1, keepdims=True)
    return ((values - center) / jnp.sqrt(spread + 1e-05) * norm_gain).astype(jnp.bfloat16)


def rotate(vector, angle_pos):
    half = vector.shape[-1] // 2
    freq = jnp.exp(-math.log(10000.0) * jnp.arange(half, dtype=jnp.float32) / half)
    angle = angle_pos[..., None] * freq
    first = vector[..., :half]
    second = vector[..., half:]
    return jnp.concatenate(
        [
            first * jnp.cos(angle) - second * jnp.sin(angle),
            second * jnp.cos(angle) + first * jnp.sin(angle),
        ],
        axis=-1,
    )


def attend(queries, extra_keys, extra_values, cache_keys, cache_values, lengths):
    scale = 1.0 / math.sqrt(queries.shape[-1])
    cached = (
        jnp.einsum("rhd,rld->rhl", queries, cache_keys, preferred_element_type=jnp.float32) * scale
    )
    live = jnp.arange(cache_keys.shape[1])[None, None, :] < lengths[:, None, None]
    cached = jnp.where(live, cached, -1e30)
    fresh = (
        jnp.einsum("rhd,red->rhe", queries, extra_keys, preferred_element_type=jnp.float32) * scale
    )
    top = jnp.maximum(jnp.max(cached, axis=-1), jnp.max(fresh, axis=-1))
    cached_exp = jnp.exp(cached - top[..., None])
    fresh_exp = jnp.exp(fresh - top[..., None])
    total = jnp.sum(cached_exp, axis=-1) + jnp.sum(fresh_exp, axis=-1)
    cached_w = (cached_exp / total[..., None]).astype(jnp.bfloat16)
    fresh_w = (fresh_exp / total[..., None]).astype(jnp.bfloat16)
    result = jnp.einsum("rhl,rld->rhd", cached_w, cache_values, preferred_element_type=jnp.float32)
    result = result + jnp.einsum(
        "rhe,red->rhd", fresh_w, extra_values, preferred_element_type=jnp.float32
    )
    return result.astype(jnp.bfloat16).reshape(queries.shape[0], -1)


def run_steps(
    normed,
    tokens,
    first,
    new_keys,
    new_values,
    weights,
    out_cols,
    cache_keys,
    cache_values,
    lengths,
    positions,
):
    w_query, w_keyval, w_gate, w_up, w_out, w_down = weights
    query_cols = w_query.shape[0]
    keyval_cols = w_keyval.shape[0]
    hidden_cols = w_gate.shape[0]
    rows_local = normed.shape[1]
    piece = lax.all_gather(normed, "gx", axis=1, tiled=True)
    projected = jnp.concatenate(
        [
            jnp.einsum("snd,cd->snc", piece, weight, preferred_element_type=jnp.float32)
            for weight in (w_query, w_keyval, w_gate, w_up)
        ],
        axis=2,
    )
    query_part = projected[:, :, :query_cols]
    keyval_part = projected[:, :, query_cols : query_cols + keyval_cols]
    gate = projected[:, :, query_cols + keyval_cols : query_cols + keyval_cols + hidden_cols]
    upward = projected[:, :, query_cols + keyval_cols + hidden_cols :]
    hidden = (jax.nn.silu(gate) * upward).astype(jnp.bfloat16)
    queries, keyvals = (
        lax.all_to_all(query_part, "gx", split_axis=1, concat_axis=2, tiled=True),
        lax.all_to_all(keyval_part, "gx", split_axis=1, concat_axis=2, tiled=True),
    )
    head = keyvals.shape[2] // 2
    attended = []
    angle_pos = (positions + first + 0).astype(jnp.float32)
    rotated = rotate(queries[0].reshape(rows_local, -1, head), angle_pos[:, None]).astype(
        jnp.bfloat16
    )
    new_keys = new_keys + [rotate(keyvals[0, :, :head], angle_pos).astype(jnp.bfloat16)]
    new_values = new_values + [keyvals[0, :, head:].astype(jnp.bfloat16)]
    attended.append(
        attend(
            rotated,
            jnp.stack(new_keys, axis=1),
            jnp.stack(new_values, axis=1),
            cache_keys,
            cache_values,
            lengths,
        )
    )
    attended = jnp.stack(attended)
    out_by_col, down_by_col = out_cols
    from_attn = jnp.einsum(
        "srq,qd->srd",
        lax.all_gather(attended, "gx", axis=1, tiled=True),
        out_by_col,
        preferred_element_type=jnp.float32,
    )
    from_hidden = jnp.einsum(
        "srf,fd->srd",
        lax.all_gather(hidden, "gx", axis=2, tiled=True),
        down_by_col,
        preferred_element_type=jnp.float32,
    )
    summed = lax.all_to_all(from_attn + from_hidden, "gx", split_axis=1, concat_axis=2, tiled=True)
    result = (tokens.astype(jnp.float32) + summed).astype(jnp.bfloat16)
    return (result, new_keys, new_values)


def local(
    tokens,
    norm_gain,
    w_query,
    w_keyval,
    w_gate,
    w_up,
    w_out,
    w_down,
    cache_keys,
    cache_values,
    lengths,
    positions,
):
    normed = layer_norm(tokens, norm_gain)
    weights = (w_query, w_keyval, w_gate, w_up, w_out, w_down)
    out_cols = (
        lax.all_to_all(w_out, "gx", split_axis=1, concat_axis=0, tiled=True),
        lax.all_to_all(w_down, "gx", split_axis=1, concat_axis=0, tiled=True),
    )
    first_out, kept_keys, kept_values = run_steps(
        normed[0:1],
        tokens[0:1],
        0,
        [],
        [],
        weights,
        out_cols,
        cache_keys,
        cache_values,
        lengths,
        positions,
    )
    second_out, kept_keys, kept_values = run_steps(
        normed[1:2],
        tokens[1:2],
        1,
        kept_keys,
        kept_values,
        weights,
        out_cols,
        cache_keys,
        cache_values,
        lengths,
        positions,
    )
    return jnp.concatenate([first_out, second_out], axis=0)


def solution(mesh):
    in_specs = (
        P(None, ("groups", "gx"), None),
        P(),
        P("gx", None),
        P("gx", None),
        P("gx", None),
        P("gx", None),
        P("gx", None),
        P("gx", None),
        P(("groups", "gx"), None, None),
        P(("groups", "gx"), None, None),
        P(("groups", "gx")),
        P(("groups", "gx")),
    )
    out_specs = P(None, ("groups", "gx"), None)
    return jax.shard_map(local, mesh=mesh, in_specs=in_specs, out_specs=out_specs, check_vma=False)
```

profile of v0, /device:TPU:0, one launch (start us, length us, event | category | flops | bytes accessed | tf_op | source)
XLA Modules:
  0.0 1046.1 jit_solution(6507867284019978116)
XLA Ops:
  0.0 1.2 convert_reduce_fusion
  1.3 1.2 fusion.38
  2.5 1.1 fusion.37
  3.6 0.1 fusion.79
  3.7 26.4 %all_gather.18 = bf16[1,16,18432]{2,0,1:T(2,128)(2,1)S(1)} all-gather(bf16[1,1,18432]{2,0,1:T(2,128)(2,1)S(1)} %get-tuple-element.7), channel_id=1, replica_groups=mesh['groups'=2,'gx'=16] {'gx'}, dimensions={1}, use_global_device_ids=true | all-gather | bytes 626688 | tf_op jit(solution)/shard_map/all_gather | solution.py:72
  30.1 0.3 copy.58
  30.4 1.0 fusion.20
  31.4 3.5 all-to-all-start.1
  34.9 25.1 %all_gather.21 = bf16[1,16,18432]{2,0,1:T(2,128)(2,1)S(1)} all-gather(bf16[1,1,18432]{2,0,1:T(2,128)(2,1)S(1)} %get-tuple-element.8), channel_id=1, replica_groups=mesh['groups'=2,'gx'=16] {'gx'}, dimensions={1}, use_global_device_ids=true | all-gather | bytes 626688 | tf_op jit(solution)/shard_map/all_gather | solution.py:72
  60.0 0.3 copy.60
  60.3 1.0 fusion.14
  61.4 3.5 all-to-all-start.6
  64.9 7.0 convolution_bitcast_fusion.1
  71.8 0.7 copy.43
  72.5 6.0 all-to-all-start
  78.5 7.0 convolution_bitcast_fusion
  85.4 0.6 copy.52
  86.1 6.0 all-to-all-start.5
  92.1 18.6 %copy.46 = bf16[384,18432]{0,1:T(8,128)(2,1)} copy(bf16[384,18432]{1,0:T(8,128)(2,1)} %param.18) | data formatting | bytes 28311552 | tf_op args[6]
  110.7 6.1 all-to-all-start.2
  116.8 15.2 %copy.72 = bf16[72,16,8,1152]{3,2,0,1:T(8,128)(2,1)} copy(bf16[72,16,8,1152]{3,2,1,0:T(8,128)(2,1)} %bitcast.148) | data formatting | bytes 42467328 | tf_op jit(solution)/shard_map/all_to_all | solution.py:144
  131.9 236.0 %all-to-all-done.2 = bf16[384,16,1152]{0,2,1:T(8,128)(2,1)} async-done(((bf16[384,16,1152]{0,2,1:T(8,128)(2,1)}), bf16[384,16,1152]{0,2,1:T(8,128)(2,1)}, u32[]{:S(2)}, u32[]{:S(2)}) %all-to-all-start.2) | async-done | bytes 14155808 | tf_op jit(solution)/shard_map/all_to_all | solution.py:143
  367.9 59.7 %all-to-all-start.3 = ((bf16[576,16,1152]{2,0,1:T(8,128)(2,1)}), bf16[576,16,1152]{2,0,1:T(8,128)(2,1)}, u32[]{:S(2)}, u32[]{:S(2)}) async-start(bf16[576,16,1152]{2,0,1:T(8,128)(2,1)} %bitcast.146), calls=%async_computation.3 | async-start | bytes 42467328 | tf_op jit(solution)/shard_map/all_to_all | solution.py:144
  428.9 9.9 fusion.18
  438.8 9.9 fusion.7
  448.7 386.2 %all-gather.2 = bf16[16,576,16]{1,2,0:T(8,128)(2,1)S(1)} all-gather(bf16[1,576,16]{1,2,0:T(8,128)(2,1)S(1)} %fusion.7), channel_id=2, replica_groups=mesh['groups'=2,'gx'=16] {'gx'}, dimensions={0}, use_global_device_ids=true | all-gather | bytes 313344 | tf_op jit(solution)/shard_map/all_gather | solution.py:117
  834.9 0.1 copy.48
  835.0 0.3 reshape.466
  835.2 9.9 fusion.12
  845.1 10.0 fusion.6
  855.1 82.5 %all-gather.3 = bf16[16,576,16]{1,2,0:T(8,128)(2,1)S(1)} all-gather(bf16[1,576,16]{1,2,0:T(8,128)(2,1)S(1)} %fusion.6), channel_id=3, replica_groups=mesh['groups'=2,'gx'=16] {'gx'}, dimensions={0}, use_global_device_ids=true | all-gather | bytes 313344 | tf_op jit(solution)/shard_map/all_gather | solution.py:117
  937.6 0.1 copy.55
  937.7 0.3 reshape.468
  937.9 0.1 fusion.70
  938.1 0.5 broadcast.188
  938.6 0.6 reduce.23
  939.2 0.1 all_to_all.80
  939.4 0.6 reduce.22
  940.1 0.1 all_to_all.93
  940.2 0.1 reduce.14
  940.3 0.4 fusion.80
  940.7 0.1 fusion.81
  940.8 0.2 fusion.39
  941.0 0.2 fusion.9
  941.3 0.1 reduce.16
  941.4 0.1 fusion.83
  941.5 0.4 fusion.82
  941.9 0.2 fusion.40
  942.2 0.2 fusion.23
  942.4 0.2 fusion.8
  942.6 18.5 %all_gather.19 = bf16[1,16,6144]{2,0,1:T(2,128)(2,1)S(1)} all-gather(bf16[1,1,6144]{2,0,1:T(2,128)(2,1)S(1)} %bitcast.151), channel_id=1, replica_groups=mesh['groups'=2,'gx'=16] {'gx'}, dimensions={1}, use_global_device_ids=true | all-gather | bytes 208896 | tf_op jit(solution)/shard_map/all_gather | solution.py:111
  961.1 19.9 %all_gather.22 = bf16[1,16,6144]{2,0,1:T(2,128)(2,1)S(1)} all-gather(bf16[1,1,6144]{2,0,1:T(2,128)(2,1)S(1)} %bitcast.152), channel_id=1, replica_groups=mesh['groups'=2,'gx'=16] {'gx'}, dimensions={1}, use_global_device_ids=true | all-gather | bytes 208896 | tf_op jit(solution)/shard_map/all_gather | solution.py:111
  981.0 18.8 %copy.47 = bf16[16,384,1152]{2,1,0:T(8,128)(2,1)} copy(bf16[16,384,1152]{1,2,0:T(8,128)(2,1)} %bitcast.16) | data formatting | bytes 28311552 | tf_op jit(solution)/shard_map/all_to_all | solution.py:143
  999.8 7.1 fusion.28
  1006.9 1.9 copy-done.2
  1008.9 1.9 fusion.31
  1010.8 8.5 fusion.1
  1019.4 0.7 copy.56
  1020.1 3.5 all-to-all-start.7
  1023.6 8.6 fusion
  1032.3 0.1 copy.50
  1032.4 12.8 %all_to_all.104 = f32[1,16,1152]{2,0,1:T(1,128)S(1)} all-to-all(f32[1,16,1152]{2,0,1:T(1,128)S(1)} %copy.50), channel_id=1, replica_groups=mesh['groups'=2,'gx'=16] {'gx'}, dimensions={1} | all-to-all | bytes 147456 | tf_op jit(solution)/shard_map/all_to_all | solution.py:121
  1045.1 0.2 add_convert_fusion.1
  1045.3 0.8 pad_maximum_fusion
  (39 shorter events, 0.4 us)
Async XLA Ops:
  0.0 30.4 %copy-start = (bf16[32,18432]{1,0:T(8,128)(2,1)S(1)}, bf16[32,18432]{1,0:T(8,128)(2,1)}, u32[]{:S(2)}) copy-start(bf16[32,18432]{1,0:T(8,128)(2,1)} %param.15) | copy-start | bytes 3538948
  31.4 29.9 %all-to-all-start.1 = ((f32[1,16,32]{2,0,1:T(1,128)}), f32[1,16,32]{2,0,1:T(1,128)S(1)}, u32[]{:S(2)}, u32[]{:S(2)}) async-start(f32[1,16,32]{2,0,1:T(1,128)} %bitcast.7), calls=%async_computation.1 | async-start | bytes 16384 | tf_op jit(solution)/shard_map/all_to_all | solution.py:87
  61.4 11.1 %all-to-all-start.6 = ((f32[1,16,32]{2,0,1:T(1,128)}), f32[1,16,32]{2,0,1:T(1,128)S(1)}, u32[]{:S(2)}, u32[]{:S(2)}) async-start(f32[1,16,32]{2,0,1:T(1,128)} %bitcast.32), calls=%async_computation.6 | async-start | bytes 16384 | tf_op jit(solution)/shard_map/all_to_all | solution.py:87
  72.5 13.6 %all-to-all-start = ((f32[1,16,384]{2,0,1:T(1,128)}), f32[1,16,384]{2,0,1:T(1,128)S(1)}, u32[]{:S(2)}, u32[]{:S(2)}) async-start(f32[1,16,384]{2,0,1:T(1,128)} %copy.43), calls=%async_computation | async-start | bytes 49152 | tf_op jit(solution)/shard_map/all_to_all | solution.py:86
  86.1 24.7 %all-to-all-start.5 = ((f32[1,16,384]{2,0,1:T(1,128)}), f32[1,16,384]{2,0,1:T(1,128)S(1)}, u32[]{:S(2)}, u32[]{:S(2)}) async-start(f32[1,16,384]{2,0,1:T(1,128)} %copy.52), calls=%async_computation.5 | async-start | bytes 49152 | tf_op jit(solution)/shard_map/all_to_all | solution.py:86
  110.7 257.2 %all-to-all-start.2 = ((bf16[384,16,1152]{0,2,1:T(8,128)(2,1)}), bf16[384,16,1152]{0,2,1:T(8,128)(2,1)}, u32[]{:S(2)}, u32[]{:S(2)}) async-start(bf16[384,16,1152]{0,2,1:T(8,128)(2,1)} %bitcast.147), calls=%async_computation.2 | async-start | bytes 28311552 | tf_op jit(solution)/shard_map/all_to_all | solution.py:143
  367.9 642.9 %all-to-all-start.3 = ((bf16[576,16,1152]{2,0,1:T(8,128)(2,1)}), bf16[576,16,1152]{2,0,1:T(8,128)(2,1)}, u32[]{:S(2)}, u32[]{:S(2)}) async-start(bf16[576,16,1152]{2,0,1:T(8,128)(2,1)} %bitcast.146), calls=%async_computation.3 | async-start | bytes 42467328 | tf_op jit(solution)/shard_map/all_to_all | solution.py:144
  845.1 95.2 %copy-start.3 = (bf16[1,1024,256]{2,1,0:T(8,128)(2,1)S(1)}, bf16[1,1024,256]{2,1,0:T(8,128)(2,1)}, u32[]{:S(2)}) copy-start(bf16[1,1024,256]{2,1,0:T(8,128)(2,1)} %param.20) | copy-start | bytes 1572868
  845.1 95.9 %copy-start.5 = (bf16[1,1024,256]{2,1,0:T(8,128)(2,1)S(1)}, bf16[1,1024,256]{2,1,0:T(8,128)(2,1)}, u32[]{:S(2)}) copy-start(bf16[1,1024,256]{2,1,0:T(8,128)(2,1)} %param.21) | copy-start | bytes 1572868
  999.8 9.1 copy-start.2
  1020.1 12.3 %all-to-all-start.7 = ((f32[1,16,1152]{2,0,1:T(1,128)}), f32[1,16,1152]{2,0,1:T(1,128)S(1)}, u32[]{:S(2)}, u32[]{:S(2)}) async-start(f32[1,16,1152]{2,0,1:T(1,128)} %copy.56), calls=%async_computation.7 | async-start | bytes 147456 | tf_op jit(solution)/shard_map/all_to_all | solution.py:121
  1023.6 21.5 %copy-start.4 = (bf16[2,1,18432]{2,0,1:T(2,128)(2,1)S(1)}, bf16[2,1,18432]{2,0,1:T(2,128)(2,1)}, u32[]{:S(2)}) copy-start(bf16[2,1,18432]{2,0,1:T(2,128)(2,1)} %param.12) | copy-start | bytes 221188
  1023.6 22.5 %copy-start.1 = (bf16[32,18432]{1,0:T(8,128)(2,1)S(1)}, bf16[32,18432]{1,0:T(8,128)(2,1)}, u32[]{:S(2)}) copy-start(bf16[32,18432]{1,0:T(8,128)(2,1)} %param.15) | copy-start | bytes 3538948
where the time goes:
time: 1050 us
  blocking collectives  571 us (54%)
  waiting for transfers between devices  236 us (22%)
  starting transfers between devices  88.2 us (8%)
  matrix products  83.5 us (8%)
  local copies, waits for them, and re-layouts  58.8 us (6%)
    all_gather x2, blocking collectives, run_steps(): lax.all_gather(hidden, 'gx', axis=2, tiled=True)  469 us
    all_to_all x1, waiting for transfers between devices, local(): lax.all_to_all(w_out, 'gx', split_axis=1, concat_axis=0, tiled=True)  236 us
    all_to_all x1, starting transfers between devices, local(): lax.all_to_all(w_down, 'gx', split_axis=1, concat_axis=0, tiled=True)  59.7 us
    dot_general x8, matrix products, run_steps(): jnp.einsum('snd,cd->snc', piece, weight, preferred_element_type=jnp.float32)  55.6 us
    all_gather x2, blocking collectives, run_steps(): piece = lax.all_gather(normed, 'gx', axis=1, tiled=True)  51.4 us
    all_gather x2, blocking collectives, run_steps(): lax.all_gather(attended, 'gx', axis=1, tiled=True)  38.4 us
    unnamed x17, local copies, waits for them, and re-layouts  21.8 us
  transfers between devices with their start and end apart: 7, of which 1 were waited for; matrix products, arithmetic and copies ran while one was open for 13% of the time, Pallas kernels for 0%

commit v1 on v0

v1 whole, which is shorter than its diff:
```python
import math

import jax
import jax.numpy as jnp
from jax import lax
from jax.sharding import PartitionSpec as P


def layer_norm(tokens, norm_gain):
    values = tokens.astype(jnp.float32)
    center = jnp.mean(values, axis=-1, keepdims=True)
    spread = jnp.mean((values - center) ** 2, axis=-1, keepdims=True)
    return ((values - center) / jnp.sqrt(spread + 1e-05) * norm_gain).astype(jnp.bfloat16)


def rotate(vector, angle_pos):
    half = vector.shape[-1] // 2
    freq = jnp.exp(-math.log(10000.0) * jnp.arange(half, dtype=jnp.float32) / half)
    angle = angle_pos[..., None] * freq
    first = vector[..., :half]
    second = vector[..., half:]
    return jnp.concatenate(
        [
            first * jnp.cos(angle) - second * jnp.sin(angle),
            second * jnp.cos(angle) + first * jnp.sin(angle),
        ],
        axis=-1,
    )


def attend(queries, new_keys, new_values, cache_keys, cache_values, lengths):
    steps = queries.shape[1]
    scale = 1.0 / math.sqrt(queries.shape[-1])
    cached = (
        jnp.einsum("rthd,rld->rthl", queries, cache_keys, preferred_element_type=jnp.float32)
        * scale
    )
    live = jnp.arange(cache_keys.shape[1])[None, None, None, :] < lengths[:, None, None, None]
    cached = jnp.where(live, cached, -1e30)
    fresh = (
        jnp.einsum("rthd,red->rthe", queries, new_keys, preferred_element_type=jnp.float32) * scale
    )
    known = jnp.arange(steps)[None, :] <= jnp.arange(steps)[:, None]
    fresh = jnp.where(known[None, :, None, :], fresh, -1e30)
    top = jnp.maximum(jnp.max(cached, axis=-1), jnp.max(fresh, axis=-1))
    cached_exp = jnp.exp(cached - top[..., None])
    fresh_exp = jnp.exp(fresh - top[..., None])
    total = jnp.sum(cached_exp, axis=-1) + jnp.sum(fresh_exp, axis=-1)
    cached_w = (cached_exp / total[..., None]).astype(jnp.bfloat16)
    fresh_w = (fresh_exp / total[..., None]).astype(jnp.bfloat16)
    result = jnp.einsum(
        "rthl,rld->rthd", cached_w, cache_values, preferred_element_type=jnp.float32
    )
    result = result + jnp.einsum(
        "rthe,red->rthd", fresh_w, new_values, preferred_element_type=jnp.float32
    )
    return result.astype(jnp.bfloat16)


def local(
    tokens,
    norm_gain,
    w_query,
    w_keyval,
    w_gate,
    w_up,
    w_out,
    w_down,
    cache_keys,
    cache_values,
    lengths,
    positions,
):
    steps, rows, width = tokens.shape
    head = cache_keys.shape[2]
    query_cols = w_query.shape[0]
    devices = lax.axis_size("gx")
    normed = layer_norm(tokens, norm_gain)
    everyone = lax.all_gather(normed, "gx", axis=0, tiled=False).reshape(-1, width)

    def project(weight):
        return jnp.einsum("nd,cd->nc", everyone, weight, preferred_element_type=jnp.float32)

    attention_in = jnp.concatenate([project(w_query), project(w_keyval)], axis=1)
    attention_in = attention_in.reshape(devices, steps * rows, -1)
    arrived = lax.all_to_all(attention_in, "gx", split_axis=0, concat_axis=0, tiled=True)
    arrived = arrived.reshape(devices, steps, rows, -1).transpose(2, 1, 0, 3)
    query = arrived[..., :query_cols].reshape(rows, steps, -1, head)
    keyval = arrived[..., query_cols:].reshape(rows, steps, 2 * head)
    hidden = (jax.nn.silu(project(w_gate)) * project(w_up)).astype(jnp.bfloat16)

    angle_pos = (positions[:, None] + jnp.arange(steps)[None, :]).astype(jnp.float32)
    rotated = rotate(query, angle_pos[:, :, None]).astype(jnp.bfloat16)
    new_keys = rotate(keyval[..., :head], angle_pos).astype(jnp.bfloat16)
    new_values = keyval[..., head:].astype(jnp.bfloat16)
    attended = attend(rotated, new_keys, new_values, cache_keys, cache_values, lengths)
    attended = attended.reshape(rows, steps, devices, -1).transpose(2, 1, 0, 3)
    attended = lax.all_to_all(attended, "gx", split_axis=0, concat_axis=0, tiled=True)
    attended = attended.reshape(devices * steps * rows, -1)

    branch = jnp.dot(attended, w_out, preferred_element_type=jnp.float32)
    branch = branch + jnp.dot(hidden, w_down, preferred_element_type=jnp.float32)
    branch = lax.psum_scatter(
        branch.reshape(devices, steps * rows, width), "gx", scatter_dimension=0, tiled=True
    )
    branch = branch.reshape(steps, rows, width)
    return (tokens.astype(jnp.float32) + branch).astype(jnp.bfloat16)


def solution(mesh):
    in_specs = (
        P(None, ("groups", "gx"), None),
        P(),
        P("gx", None),
        P("gx", None),
        P("gx", None),
        P("gx", None),
        P("gx", None),
        P("gx", None),
        P(("groups", "gx"), None, None),
        P(("groups", "gx"), None, None),
        P(("groups", "gx")),
        P(("groups", "gx")),
    )
    out_specs = P(None, ("groups", "gx"), None)
    return jax.shard_map(local, mesh=mesh, in_specs=in_specs, out_specs=out_specs, check_vma=False)
```

time: 1050 us -> 240 us (0.23)
  blocking collectives: 571 us -> 0 us
  waiting for transfers between devices: 236 us -> 150 us
  starting transfers between devices: 88.2 us -> 7.23 us
  local copies, waits for them, and re-layouts: 58.8 us -> 11.2 us
  matrix products: 83.5 us -> 51.1 us
  between operations: 1.67 us -> 14.9 us
    all_gather x6 -> x0, blocking collectives: 558 us -> none  [the longest x2 469 us: run_steps(): lax.all_gather(hidden, 'gx', axis=2, tiled=True)]
    all_to_all x7 -> x2, waiting for transfers between devices: 236 us -> 6.87 us  [the longest x1 6.87 us: local(): lax.all_to_all(attention_in, 'gx', split_axis=0, concat_axis=0, tiled=True)]
    unnamed x0 -> x3, waiting for transfers between devices: none -> 99.5 us
    all_to_all x7 -> x2, starting transfers between devices: 88.2 us -> 7 us  [the longest x1 3.5 us: local(): lax.all_to_all(attention_in, 'gx', split_axis=0, concat_axis=0, tiled=True)]
    all_gather x0 -> x1, waiting for transfers between devices: none -> 43.7 us  [local(): lax.all_gather(normed, 'gx', axis=0, tiled=False).reshape(-1, width)]
    all_to_all x5 -> x0, local copies, waits for them, and re-layouts: 34.7 us -> none  [the longest x1 18.8 us: local(): lax.all_to_all(w_out, 'gx', split_axis=1, concat_axis=0, tiled=True)]
    dot_general x19 -> x9, matrix products: 83.5 us -> 51.1 us  [the longest x1 23 us: local(): jnp.dot(hidden, w_down, preferred_element_type=jnp.float32)]
    unnamed x17 -> x15, local copies, waits for them, and re-layouts: 21.8 us -> 5.15 us
  transfers between devices with their start and end apart: 7 -> 4, of which waited for: 1 -> 3; matrix products, arithmetic and copies ran while one was open for 13% -> 5% of each run, Pallas kernels for 0% -> 0%
where the time goes in v1:
time: 240 us; the launch traced here: 239 us
  waiting for transfers between devices  150 us (62%)
  matrix products  51.1 us (21%)
  between operations  14.9 us (6%)
  local copies, waits for them, and re-layouts  11.2 us (5%)
  starting transfers between devices  7.23 us (3%)
  other arithmetic  4.97 us (2%)
    unnamed x3, waiting for transfers between devices  99.5 us
    all_gather x1, waiting for transfers between devices, local(): lax.all_gather(normed, 'gx', axis=0, tiled=False).reshape(-1, width)  43.7 us
    dot_general x1, matrix products, local(): jnp.dot(hidden, w_down, preferred_element_type=jnp.float32)  23 us
    dot_general x3, matrix products, project(): jnp.einsum('nd,cd->nc', everyone, weight, preferred_element_type=jnp.floa...  18.2 us
    dot_general x1, matrix products, local(): branch = jnp.dot(attended, w_out, preferred_element_type=jnp.float32)  8.96 us
    all_to_all x1, waiting for transfers between devices, local(): lax.all_to_all(attention_in, 'gx', split_axis=0, concat_axis=0, tiled=True)  6.87 us
    unnamed x15, local copies, waits for them, and re-layouts  5.15 us
  transfers between devices with their start and end apart: 4, of which 3 were waited for; matrix products, arithmetic and copies ran while one was open for 5% of the time, Pallas kernels for 0%

profile of v1, /device:TPU:0, one launch (start us, length us, event | category | flops | bytes accessed | tf_op | source)
XLA Modules:
  0.0 239.5 jit_solution(15065781644227757842)
XLA Ops:
  6.5 0.0 copy-start
  6.5 0.0 all-gather.3.cloned.1.call-start
  6.5 1.3 fusion.24
  7.8 1.3 multiply_reduce_fusion
  9.1 1.7 multiply_convert_fusion
  10.9 0.0 all-gather.3.cloned.1.call-update
  12.2 0.1 multiply_cosine_fusion.1
  12.3 43.7 %all-gather.3.cloned.1.call-done = bf16[32,1,18432]{2,1,0:T(2,128)(2,1)} async-done(((bf16[2,1,18432]{2,1,0:T(2,128)(2,1)}), bf16[32,1,18432]{2,1,0:T(2,128)(2,1)}) %all-gather.3.cloned.1.call-update) | async-done | bytes 1179664 | tf_op jit(solution)/shard_map/all_gather | solution.py:79
  56.1 2.4 copy.28
  58.4 7.4 %fusion.6 = f32[32,384]{1,0:T(8,128)S(1)} fusion(bf16[384,18432]{1,0:T(8,128)(2,1)} %param.14, bf16[32,1,18432]{2,0,1:T(8,128)(2,1)S(1)} %copy.28), kind=kOutput, calls=%fused_computation.7 | convolution fusion | flops 452984832 | bytes 15384576 | tf_op jit(solution)/shard_map/nd,cd->nc/dot_general | solution.py:82
  65.8 0.0 copy-done
  65.8 0.0 copy-start.3
  65.8 0.0 copy-start.4
  65.8 0.4 fusion.4
  66.3 0.7 reshape.362
  67.0 3.5 %all-to-all-start = ((f32[16,2,416]{2,1,0:T(2,128)}), f32[16,2,416]{2,1,0:T(2,128)S(1)}, u32[]{:S(2)}, u32[]{:S(2)}) async-start(f32[16,2,416]{2,1,0:T(2,128)} %reshape.362), calls=%async_computation | async-start | bytes 131072 | tf_op jit(solution)/shard_map/all_to_all | solution.py:86
  70.5 6.9 %all-to-all-done = f32[16,2,416]{2,1,0:T(2,128)S(1)} async-done(((f32[16,2,416]{2,1,0:T(2,128)}), f32[16,2,416]{2,1,0:T(2,128)S(1)}, u32[]{:S(2)}, u32[]{:S(2)}) %all-to-all-start) | async-done | bytes 53280 | tf_op jit(solution)/shard_map/all_to_all | solution.py:86
  77.4 0.1 reshape.366
  77.5 0.1 fusion.42
  77.6 0.0 copy-done.3
  77.7 0.4 fusion.47
  78.0 0.2 fusion.48
  78.2 0.2 fusion.20
  78.4 0.0 copy-done.4
  78.4 0.3 fusion.17
  78.7 0.2 fusion.15
  78.9 0.6 copy.38
  79.5 3.5 %all-to-all-start.1 = ((bf16[16,2,1,384]{3,1,2,0:T(2,128)(2,1)}), bf16[16,2,1,384]{3,1,2,0:T(2,128)(2,1)S(1)}, u32[]{:S(2)}, u32[]{:S(2)}) async-start(bf16[16,2,1,384]{3,1,2,0:T(2,128)(2,1)} %bitcast.70), calls=%async_computation.1 | async-start | bytes 49152 | tf_op jit(solution)/shard_map/all_to_all | solution.py:98
  83.1 0.2 all-reduce.3.cloned.1.call-start
  83.3 10.4 %fusion.2 = f32[32,576]{1,0:T(8,128)S(1)} fusion(bf16[576,18432]{1,0:T(8,128)(2,1)} %param.16, bf16[32,1,18432]{2,0,1:T(8,128)(2,1)S(1)} %copy.28), kind=kOutput, calls=%fused_computation.3 | convolution fusion | flops 679477248 | bytes 22487040 | tf_op jit(solution)/shard_map/nd,cd->nc/dot_general | solution.py:82
  93.7 0.0 all-to-all-done.1
  93.7 9.0 %fusion.49 = f32[32,18432]{1,0:T(8,128)} fusion(bf16[32,384]{1,0:T(8,128)(2,1)S(1)} %reshape.370, bf16[384,18432]{1,0:T(8,128)(2,1)} %param.18), kind=kOutput, calls=%fused_computation.73 | convolution fusion | flops 452984832 | bytes 16539648 | tf_op jit(solution)/shard_map/dot_general | solution.py:101
  102.7 23.0 %convolution_add_fusion = f32[32,18432]{1,0:T(8,128)} fusion(f32[32,18432]{1,0:T(8,128)} %fusion.49, bf16[576,18432]{1,0:T(8,128)(2,1)} %param.19, bf16[576,18432]{1,0:T(8,128)(2,1)} %param.17, bf16[32,1,18432]{2,0,1:T(8,128)(2,1)S(1)} %copy.28, f32[32,576]{1,0:T(8,128)S(1)} %fusion.2), kind=kOutput, calls=%fused_computation | convolution fusion | flops 1359654912 | bytes 48439296 | tf_op jit(solution)/shard_map/dot_general | solution.py:102
  125.6 0.0 copy-start.1
  125.6 3.8 %reshape.371 = f32[16,2,18432]{2,1,0:T(2,128)} reshape(f32[32,18432]{1,0:T(8,128)} %convolution_add_fusion) | data formatting | bytes 4718592 | tf_op jit(solution)/shard_map/reshape | solution.py:104
  129.5 0.0 copy-start.5
  129.5 0.0 copy-start.2
  129.5 0.0 all-reduce.3.cloned.1.call-update
  129.5 0.6 copy-done.5
  130.1 0.6 dynamic-slice
  130.7 99.4 %all-reduce.3.cloned.1.call-done = f32[16,2,18432]{2,1,0:T(2,128)} async-done(((f32[16,2,18432]{2,1,0:T(2,128)}), f32[16,2,18432]{2,1,0:T(2,128)}) %all-reduce.3.cloned.1.call-update) | async-done | bytes 2359312
  230.2 1.6 constant_dynamic-slice_fusion
  231.7 0.0 copy-done.2
  231.7 0.2 add_convert_fusion
  231.9 0.7 copy.27
  232.6 0.0 copy-done.1
  (18 shorter events, 0.2 us)
Async XLA Ops:
  6.5 59.3 %copy-start = (bf16[32,18432]{1,0:T(8,128)(2,1)S(1)}, bf16[32,18432]{1,0:T(8,128)(2,1)}, u32[]{:S(2)}) copy-start(bf16[32,18432]{1,0:T(8,128)(2,1)} %param.15) | copy-start | bytes 3538948
  6.5 49.5 %all-gather.3.cloned.1.call-start = ((), (), s32[]{:S(2)}) async-start(), calls=%async_computation.2 | async-start | bytes 2506752 | tf_op jit(solution)/shard_map/all_gather | solution.py:79
  65.8 11.8 %copy-start.3 = (bf16[1,1024,256]{2,1,0:T(8,128)(2,1)S(1)}, bf16[1,1024,256]{2,1,0:T(8,128)(2,1)}, u32[]{:S(2)}) copy-start(bf16[1,1024,256]{2,1,0:T(8,128)(2,1)} %param.20) | copy-start | bytes 1572868
  65.8 12.6 %copy-start.4 = (bf16[1,1024,256]{2,1,0:T(8,128)(2,1)S(1)}, bf16[1,1024,256]{2,1,0:T(8,128)(2,1)}, u32[]{:S(2)}) copy-start(bf16[1,1024,256]{2,1,0:T(8,128)(2,1)} %param.21) | copy-start | bytes 1572868
  67.0 10.4 %all-to-all-start = ((f32[16,2,416]{2,1,0:T(2,128)}), f32[16,2,416]{2,1,0:T(2,128)S(1)}, u32[]{:S(2)}, u32[]{:S(2)}) async-start(f32[16,2,416]{2,1,0:T(2,128)} %reshape.362), calls=%async_computation | async-start | bytes 131072 | tf_op jit(solution)/shard_map/all_to_all | solution.py:86
  79.5 14.1 %all-to-all-start.1 = ((bf16[16,2,1,384]{3,1,2,0:T(2,128)(2,1)}), bf16[16,2,1,384]{3,1,2,0:T(2,128)(2,1)S(1)}, u32[]{:S(2)}, u32[]{:S(2)}) async-start(bf16[16,2,1,384]{3,1,2,0:T(2,128)(2,1)} %bitcast.70), calls=%async_computation.1 | async-start | bytes 49152 | tf_op jit(solution)/shard_map/all_to_all | solution.py:98
  83.1 147.1 %all-reduce.3.cloned.1.call-start = ((), (), s32[]{:S(2)}) async-start(), calls=%async_computation.3 | async-start | bytes 4718592
  125.6 107.0 %copy-start.1 = (bf16[32,18432]{1,0:T(8,128)(2,1)S(1)}, bf16[32,18432]{1,0:T(8,128)(2,1)}, u32[]{:S(2)}) copy-start(bf16[32,18432]{1,0:T(8,128)(2,1)} %param.15) | copy-start | bytes 3538948
  129.5 0.7 copy-start.5
  129.5 102.3 %copy-start.2 = (bf16[2,1,18432]{2,0,1:T(2,128)(2,1)S(1)}, bf16[2,1,18432]{2,0,1:T(2,128)(2,1)}, u32[]{:S(2)}) copy-start(bf16[2,1,18432]{2,0,1:T(2,128)(2,1)} %param.12) | copy-start | bytes 221188
Sparse Core Ops, SparseCore 0:
  11.0 45.0 all-gather.2
  129.6 100.4 all-reduce.2

commit v2 on v1

v2 whole, which is shorter than its diff:
```python
import functools
import math

import jax
import jax.numpy as jnp
from jax import lax
from jax.experimental import pallas as pl
from jax.experimental.pallas import tpu as pltpu
from jax.sharding import PartitionSpec as P

F32 = jnp.float32
BF16 = jnp.bfloat16
NT = (((1,), (1,)), ((), ()))
ANY = pl.BlockSpec(memory_space=pl.ANY)
VMEM = pl.BlockSpec(memory_space=pltpu.VMEM)
SMEM = pl.BlockSpec(memory_space=pltpu.SMEM)


def params(mib):
    return pltpu.CompilerParams(vmem_limit_bytes=mib << 20)


def cost(rows, *weights):
    size = sum(math.prod(w.shape) for w in weights)
    return pl.CostEstimate(flops=2 * rows * size, bytes_accessed=2 * size, transcendentals=0)


def slot_at(place, half):
    return 2 * place if place < half else 2 * (place - half) + 1


def cuts(width):
    for count in (8, 9, 6, 4, 3, 2):
        if width % (128 * count) == 0:
            return count
    return 1


def norm_kernel(tokens_ref, gain_ref, out_ref):
    values = tokens_ref[...].astype(F32)
    centered = values - jnp.mean(values, axis=-1, keepdims=True)
    spread = jnp.mean(centered * centered, axis=-1, keepdims=True)
    out_ref[...] = (centered / jnp.sqrt(spread + 1e-05) * gain_ref[...]).astype(BF16)


def layer_norm(tokens, norm_gain):
    return pl.pallas_call(
        norm_kernel, out_shape=jax.ShapeDtypeStruct(tokens.shape, BF16)
    )(tokens, norm_gain.reshape(1, -1))


def attention_in_kernel(
    chunks, me_ref, mine_ref, other_ref, wq_ref, wk_ref, out_ref, rows_ref,
    pieces, spread, rows, wq, wk, acc_q, acc_k, piece_sem, q_sem, k_sem, rows_sem,
):
    half, steps, width = mine_ref.shape
    step = width // chunks

    def cols(c):
        return pl.ds(c * step, step)

    piece_copies = [
        pltpu.make_async_copy(mine_ref, pieces.at[pl.ds(0, half)], piece_sem.at[0]),
        pltpu.make_async_copy(other_ref, pieces.at[pl.ds(half, half)], piece_sem.at[1]),
    ]
    q_copies = [
        pltpu.make_async_copy(wq_ref.at[:, cols(c)], wq.at[c], q_sem.at[c]) for c in range(chunks)
    ]
    k_copies = [
        pltpu.make_async_copy(wk_ref.at[:, cols(c)], wk.at[c], k_sem.at[c]) for c in range(chunks)
    ]
    row_copies = [
        pltpu.make_async_copy(rows.at[:, cols(c)], rows_ref.at[:, cols(c)], rows_sem.at[c])
        for c in range(chunks)
    ]
    for copy in piece_copies:
        copy.start()
    for c in range(chunks):
        q_copies[c].start()
        k_copies[c].start()
    acc_q[...] = jnp.zeros_like(acc_q)
    acc_k[...] = jnp.zeros_like(acc_k)
    for copy in piece_copies:
        copy.wait()
    for c in range(chunks):
        part = slice(c * step, (c + 1) * step)
        for p in range(2 * half):
            spread[p * steps : (p + 1) * steps, :] = pieces[p, :, part].astype(F32)
        block = spread[...].astype(BF16)
        rows[:, part] = block
        row_copies[c].start()
        q_copies[c].wait()
        acc_q[...] += lax.dot_general(block, wq[c], NT, preferred_element_type=F32)
        k_copies[c].wait()
        acc_k[...] += lax.dot_general(block, wk[c], NT, preferred_element_type=F32)
    split = acc_q.shape[1]
    for p in range(2 * half):
        owner = lax.bitwise_xor(me_ref[0], slot_at(p, half))
        out_ref[owner, :, :split] = acc_q[p * steps : (p + 1) * steps, :]
        out_ref[owner, :, split:] = acc_k[p * steps : (p + 1) * steps, :]
    for copy in row_copies:
        copy.wait()


def attention_in(me, mine, other, w_query, w_keyval):
    half, steps, width = mine.shape
    n = 2 * half * steps
    chunks = cuts(width)
    step = width // chunks
    q_cols, k_cols = w_query.shape[0], w_keyval.shape[0]
    return pl.pallas_call(
        functools.partial(attention_in_kernel, chunks),
        in_specs=[SMEM, ANY, ANY, ANY, ANY],
        out_specs=[VMEM, ANY],
        out_shape=[
            jax.ShapeDtypeStruct((2 * half, steps, q_cols + k_cols), F32),
            jax.ShapeDtypeStruct((n, width), BF16),
        ],
        scratch_shapes=[
            pltpu.VMEM((2 * half, steps, width), BF16),
            pltpu.VMEM((n, step), F32),
            pltpu.VMEM((n, width), BF16),
            pltpu.VMEM((chunks, q_cols, step), BF16),
            pltpu.VMEM((chunks, k_cols, step), BF16),
            pltpu.VMEM((n, q_cols), F32),
            pltpu.VMEM((n, k_cols), F32),
            pltpu.SemaphoreType.DMA((2,)),
            pltpu.SemaphoreType.DMA((chunks,)),
            pltpu.SemaphoreType.DMA((chunks,)),
            pltpu.SemaphoreType.DMA((chunks,)),
        ],
        compiler_params=params(52),
        cost_estimate=cost(n, w_query, w_keyval),
    )(me, mine, other, w_query, w_keyval)


def hidden_kernel(
    chunks, rows_ref, wg_ref, wu_ref, out_ref, rows, wg, wu, acc_g, acc_u, row_sem, g_sem, u_sem
):
    step = rows_ref.shape[1] // chunks

    def cols(c):
        return pl.ds(c * step, step)

    row_copy = pltpu.make_async_copy(rows_ref, rows, row_sem)
    copies = [
        (
            pltpu.make_async_copy(wg_ref.at[:, cols(c)], wg.at[c], g_sem.at[c]),
            pltpu.make_async_copy(wu_ref.at[:, cols(c)], wu.at[c], u_sem.at[c]),
        )
        for c in range(chunks)
    ]
    row_copy.start()
    for gate_copy, up_copy in copies:
        gate_copy.start()
        up_copy.start()
    acc_g[...] = jnp.zeros_like(acc_g)
    acc_u[...] = jnp.zeros_like(acc_u)
    row_copy.wait()
    for c in range(chunks):
        block = rows[:, c * step : (c + 1) * step]
        copies[c][0].wait()
        acc_g[...] += lax.dot_general(block, wg[c], NT, preferred_element_type=F32)
        copies[c][1].wait()
        acc_u[...] += lax.dot_general(block, wu[c], NT, preferred_element_type=F32)
    gate = acc_g[...]
    out_ref[...] = (jax.nn.silu(gate) * acc_u[...]).astype(BF16)


def hidden_units(rows, w_gate, w_up):
    n, width = rows.shape
    units = w_gate.shape[0]
    chunks = cuts(width)
    step = width // chunks
    return pl.pallas_call(
        functools.partial(hidden_kernel, chunks),
        in_specs=[ANY, ANY, ANY],
        out_specs=VMEM,
        out_shape=jax.ShapeDtypeStruct((n, units), BF16),
        scratch_shapes=[
            pltpu.VMEM((n, width), BF16),
            pltpu.VMEM((chunks, units, step), BF16),
            pltpu.VMEM((chunks, units, step), BF16),
            pltpu.VMEM((n, units), F32),
            pltpu.VMEM((n, units), F32),
            pltpu.SemaphoreType.DMA,
            pltpu.SemaphoreType.DMA((chunks,)),
            pltpu.SemaphoreType.DMA((chunks,)),
        ],
        compiler_params=params(56),
        cost_estimate=cost(n, w_gate, w_up),
    )(rows, w_gate, w_up)


def down_kernel(chunks, hidden_ref, w_ref, out_ref, w, out, w_sem, out_sem):
    step = w_ref.shape[1] // chunks

    def cols(c):
        return pl.ds(c * step, step)

    copies = [
        pltpu.make_async_copy(w_ref.at[:, cols(c)], w.at[c], w_sem.at[c]) for c in range(chunks)
    ]
    out_copies = [
        pltpu.make_async_copy(out.at[c], out_ref.at[:, cols(c)], out_sem.at[c])
        for c in range(chunks)
    ]
    for copy in copies:
        copy.start()
    for c in range(chunks):
        copies[c].wait()
        out[c] = jnp.dot(hidden_ref[...], w[c], preferred_element_type=F32)
        out_copies[c].start()
    for copy in out_copies:
        copy.wait()


def down_part(hidden, w_down):
    n, units = hidden.shape
    width = w_down.shape[1]
    chunks = cuts(width)
    step = width // chunks
    return pl.pallas_call(
        functools.partial(down_kernel, chunks),
        in_specs=[VMEM, ANY],
        out_specs=ANY,
        out_shape=jax.ShapeDtypeStruct((n, width), F32),
        scratch_shapes=[
            pltpu.VMEM((chunks, units, step), BF16),
            pltpu.VMEM((chunks, n, step), F32),
            pltpu.SemaphoreType.DMA((chunks,)),
            pltpu.SemaphoreType.DMA((chunks,)),
        ],
        compiler_params=params(40),
        cost_estimate=cost(n, w_down),
    )(hidden, w_down)


def branch_kernel(
    chunks, me_ref, attended_ref, part_ref, w_ref, keep_ref, send_ref,
    spread, w, part, keep, send, w_sem, part_sem, keep_sem, send_sem,
):
    slots, steps, _ = attended_ref.shape
    half = keep_ref.shape[0]
    step = w_ref.shape[1] // chunks

    def cols(c):
        return pl.ds(c * step, step)

    copies = [
        (
            pltpu.make_async_copy(w_ref.at[:, cols(c)], w.at[c], w_sem.at[c]),
            pltpu.make_async_copy(part_ref.at[:, cols(c)], part.at[c], part_sem.at[c]),
        )
        for c in range(chunks)
    ]
    out_copies = [
        (
            pltpu.make_async_copy(keep.at[c], keep_ref.at[:, cols(c)], keep_sem.at[c]),
            pltpu.make_async_copy(send.at[c], send_ref.at[:, cols(c)], send_sem.at[c]),
        )
        for c in range(chunks)
    ]
    for w_copy, part_copy in copies:
        w_copy.start()
        part_copy.start()
    for p in range(slots):
        owner = lax.bitwise_xor(me_ref[0], slot_at(p, slots // 2))
        spread[p * steps : (p + 1) * steps, :] = attended_ref[owner].astype(F32)
    attended = spread[...].astype(BF16)
    for c in range(chunks):
        for copy in copies[c]:
            copy.wait()
        total = part[c] + jnp.dot(attended, w[c], preferred_element_type=F32)
        keep[c] = total[:half]
        send[c] = total[half:].astype(BF16)
        for copy in out_copies[c]:
            copy.start()
    for pair in out_copies:
        for copy in pair:
            copy.wait()


def branch_parts(me, attended, part, w_out):
    slots, steps, features = attended.shape
    n, width = part.shape
    half = n // 2
    chunks = cuts(width)
    step = width // chunks
    return pl.pallas_call(
        functools.partial(branch_kernel, chunks),
        in_specs=[SMEM, VMEM, ANY, ANY],
        out_specs=[ANY, ANY],
        out_shape=[
            jax.ShapeDtypeStruct((half, width), F32),
            jax.ShapeDtypeStruct((half, width), BF16),
        ],
        scratch_shapes=[
            pltpu.VMEM((n, features), F32),
            pltpu.VMEM((chunks, features, step), BF16),
            pltpu.VMEM((chunks, n, step), F32),
            pltpu.VMEM((chunks, half, step), F32),
            pltpu.VMEM((chunks, half, step), BF16),
            pltpu.SemaphoreType.DMA((chunks,)),
            pltpu.SemaphoreType.DMA((chunks,)),
            pltpu.SemaphoreType.DMA((chunks,)),
            pltpu.SemaphoreType.DMA((chunks,)),
        ],
        compiler_params=params(40),
        cost_estimate=cost(n, w_out),
    )(me, attended, part, w_out)


def cut_kernel(keep_ref, came_ref, own_ref, *send_refs):
    steps = own_ref.shape[0]
    total = keep_ref[...] + came_ref[...].astype(F32)
    own_ref[...] = total[:steps]
    for p, send_ref in enumerate(send_refs):
        send_ref[...] = total[(p + 1) * steps : (p + 2) * steps].astype(BF16)


def cut_parts(keep, came, steps):
    half, width = keep.shape
    slots = half // steps
    chunks = 3 if width % 384 == 0 else 1
    step = width // chunks
    whole = pl.BlockSpec((half, step), lambda c: (0, c))
    piece = pl.BlockSpec((steps, step), lambda c: (0, c))
    return pl.pallas_call(
        cut_kernel,
        grid=(chunks,),
        in_specs=[whole, whole],
        out_specs=[piece] * slots,
        out_shape=[jax.ShapeDtypeStruct((steps, width), F32)]
        + [jax.ShapeDtypeStruct((steps, width), BF16)] * (slots - 1),
        compiler_params=params(32),
        cost_estimate=pl.CostEstimate(
            flops=2 * half * width, bytes_accessed=8 * half * width, transcendentals=0
        ),
    )(keep, came)


def rotate(vector, angle_pos):
    half = vector.shape[-1] // 2
    freq = jnp.exp(-math.log(10000.0) * jnp.arange(half, dtype=F32) / half)
    angle = angle_pos[..., None] * freq
    first = vector[..., :half]
    second = vector[..., half:]
    return jnp.concatenate(
        [
            first * jnp.cos(angle) - second * jnp.sin(angle),
            second * jnp.cos(angle) + first * jnp.sin(angle),
        ],
        axis=-1,
    )


def attend(queries, new_keys, new_values, cache_keys, cache_values, lengths):
    steps = queries.shape[1]
    scale = 1.0 / math.sqrt(queries.shape[-1])
    cached = jnp.einsum("rthd,rld->rthl", queries, cache_keys, preferred_element_type=F32) * scale
    live = jnp.arange(cache_keys.shape[1])[None, None, None, :] < lengths[:, None, None, None]
    cached = jnp.where(live, cached, -1e30)
    fresh = jnp.einsum("rthd,red->rthe", queries, new_keys, preferred_element_type=F32) * scale
    known = jnp.arange(steps)[None, :] <= jnp.arange(steps)[:, None]
    fresh = jnp.where(known[None, :, None, :], fresh, -1e30)
    top = jnp.maximum(jnp.max(cached, axis=-1), jnp.max(fresh, axis=-1))
    cached_exp = jnp.exp(cached - top[..., None])
    fresh_exp = jnp.exp(fresh - top[..., None])
    total = jnp.sum(cached_exp, axis=-1) + jnp.sum(fresh_exp, axis=-1)
    cached_w = (cached_exp / total[..., None]).astype(BF16)
    fresh_w = (fresh_exp / total[..., None]).astype(BF16)
    result = jnp.einsum("rthl,rld->rthd", cached_w, cache_values, preferred_element_type=F32)
    result = result + jnp.einsum("rthe,red->rthd", fresh_w, new_values, preferred_element_type=F32)
    return result.astype(BF16)


def swap(value, bits, devices):
    return lax.ppermute(value, "gx", [(i, i ^ bits) for i in range(devices)])


def gather_rows(piece, devices):
    outer = min(4, devices // 2)
    inner = devices // (2 * outer)
    near = [piece] + [swap(piece, 2 * inner * a, devices) for a in range(1, outer)]
    far = [near] + [[swap(p, 2 * b, devices) for p in near] for b in range(1, inner)]
    even = jnp.stack([far[b][a] for a in range(outer) for b in range(inner)])
    return even, swap(even, 1, devices)


def local(
    tokens,
    norm_gain,
    w_query,
    w_keyval,
    w_gate,
    w_up,
    w_out,
    w_down,
    cache_keys,
    cache_values,
    lengths,
    positions,
):
    steps, rows, width = tokens.shape
    head = cache_keys.shape[2]
    query_cols = w_query.shape[0]
    devices = lax.axis_size("gx")
    batch = steps * rows
    me = lax.axis_index("gx").astype(jnp.int32).reshape(1)

    own_tokens = tokens.reshape(batch, width)
    even, odd = gather_rows(layer_norm(own_tokens, norm_gain), devices)
    projected, everyone = attention_in(me, even, odd, w_query, w_keyval)

    arrived = lax.all_to_all(projected, "gx", split_axis=0, concat_axis=0, tiled=True)
    arrived = arrived.reshape(devices, steps, rows, -1).transpose(2, 1, 0, 3)
    query = arrived[..., :query_cols].reshape(rows, steps, -1, head)
    keyval = arrived[..., query_cols:].reshape(rows, steps, 2 * head)
    hidden = hidden_units(everyone, w_gate, w_up)

    angle_pos = (positions[:, None] + jnp.arange(steps)[None, :]).astype(F32)
    rotated = rotate(query, angle_pos[:, :, None]).astype(BF16)
    new_keys = rotate(keyval[..., :head], angle_pos).astype(BF16)
    new_values = keyval[..., head:].astype(BF16)
    attended = attend(rotated, new_keys, new_values, cache_keys, cache_values, lengths)
    attended = attended.reshape(rows, steps, devices, -1).transpose(2, 1, 0, 3)
    attended = attended.reshape(devices, batch, -1)
    attended = lax.all_to_all(attended, "gx", split_axis=0, concat_axis=0, tiled=True)

    part = down_part(hidden, w_down)
    keep, send = branch_parts(me, attended, part, w_out)
    pieces = cut_parts(keep, swap(send, 1, devices), batch)
    branch = pieces[0]
    for place in range(1, devices // 2):
        branch = branch + swap(pieces[place], 2 * place, devices).astype(F32)
    result = (own_tokens.astype(F32) + branch).astype(BF16)
    return result.reshape(tokens.shape)


def solution(mesh):
    in_specs = (
        P(None, ("groups", "gx"), None),
        P(),
        P("gx", None),
        P("gx", None),
        P("gx", None),
        P("gx", None),
        P("gx", None),
        P("gx", None),
        P(("groups", "gx"), None, None),
        P(("groups", "gx"), None, None),
        P(("groups", "gx")),
        P(("groups", "gx")),
    )
    out_specs = P(None, ("groups", "gx"), None)
    return jax.shard_map(local, mesh=mesh, in_specs=in_specs, out_specs=out_specs, check_vma=False)
```

time: 240 us -> 109 us (0.45)
  waiting for transfers between devices: 150 us -> 14.8 us
  Pallas kernels: 0 us -> 53.5 us
  matrix products: 51.1 us -> 0.98 us
  starting transfers between devices: 7.23 us -> 32.9 us
  between operations: 14.9 us -> 1.56 us
  local copies, waits for them, and re-layouts: 11.2 us -> 3.01 us
  other arithmetic: 4.97 us -> 1.45 us
    unnamed x3 -> x0, waiting for transfers between devices: 99.5 us -> none
    pallas_call x0 -> x6, Pallas kernels: none -> 53.5 us  [the longest x1 27 us: hidden_units(): pl.pallas_call(functools.partial(hidden_kernel, chunks), in_specs=[ANY, A...]
    dot_general x6 -> x1, matrix products: 50.3 us -> 0.18 us  [attend(): jnp.einsum('rthd,red->rthe', queries, new_keys, preferred_element_type=F32)]
    all_gather x1 -> x0, waiting for transfers between devices: 43.7 us -> none  [local(): lax.all_gather(normed, 'gx', axis=0, tiled=False).reshape(-1, width)]
    ppermute x0 -> x16, starting transfers between devices: none -> 22.7 us  [swap(): return lax.ppermute(value, 'gx', [(i, i ^ bits) for i in range(devices)])]
    ppermute x0 -> x16, waiting for transfers between devices: none -> 14.8 us  [swap(): return lax.ppermute(value, 'gx', [(i, i ^ bits) for i in range(devices)])]
    all_to_all x1, waiting for transfers between devices: 6.87 us -> 0.01 us  [local(): lax.all_to_all(projected, 'gx', split_axis=0, concat_axis=0, tiled=True)]
    reshape x3 -> x0, local copies, waits for them, and re-layouts: 4.52 us -> none  [the longest x1 3.83 us: local(): branch.reshape(devices, steps * rows, width)]
  transfers between devices with their start and end apart: 4 -> 18, of which waited for: 3 -> 5; matrix products, arithmetic and copies ran while one was open for 5% -> 1% of each run, Pallas kernels for 0% -> 32%
where the time goes in v2:
time: 109 us; the launch traced here: 108 us
  Pallas kernels  53.5 us (49%)
  starting transfers between devices  32.9 us (30%)
  waiting for transfers between devices  14.8 us (14%)
  local copies, waits for them, and re-layouts  3.01 us (3%)
  between operations  1.56 us (1%)
  other arithmetic  1.45 us (1%)
    pallas_call x1, Pallas kernels, hidden_units(): pl.pallas_call(functools.partial(hidden_kernel, chunks), in_specs=[ANY, A...  27 us
    ppermute x16, starting transfers between devices, swap(): return lax.ppermute(value, 'gx', [(i, i ^ bits) for i in range(devices)])  22.7 us
    ppermute x16, waiting for transfers between devices, swap(): return lax.ppermute(value, 'gx', [(i, i ^ bits) for i in range(devices)])  14.8 us
    pallas_call x1, Pallas kernels, attention_in(): pl.pallas_call(functools.partial(attention_in_kernel, chunks), in_specs=[...  9.83 us
    pallas_call x1, Pallas kernels, down_part(): pl.pallas_call(functools.partial(down_kernel, chunks), in_specs=[VMEM, AN...  7.87 us
    pallas_call x1, Pallas kernels, branch_parts(): pl.pallas_call(functools.partial(branch_kernel, chunks), in_specs=[SMEM,...  6.19 us
    all_to_all x1, starting transfers between devices, local(): lax.all_to_all(attended, 'gx', split_axis=0, concat_axis=0, tiled=True)  6 us
    all_to_all x1, starting transfers between devices, local(): lax.all_to_all(projected, 'gx', split_axis=0, concat_axis=0, tiled=True)  4.26 us
  transfers between devices with their start and end apart: 18, of which 5 were waited for; matrix products, arithmetic and copies ran while one was open for 1% of the time, Pallas kernels for 32%

profile of v2, /device:TPU:0, one launch (start us, length us, event | category | flops | bytes accessed | tf_op | source)
XLA Modules:
  0.0 108.2 jit_solution(16239667188662418794)
XLA Ops:
  0.0 2.2 %shard_map.118 = bf16[2,18432]{1,0:T(2,128)(2,1)} custom-call(bf16[2,18432]{1,0:T(2,128)(2,1)} %bitcast.65, f32[1,18432]{1,0:T(1,128)} %bitcast.68), custom_call_target="tpu_custom_call" | custom-call | tf_op jit(solution)/shard_map/pallas_call | solution.py:47
  2.2 5.0 %collective-permute-start.5 = (bf16[2,18432]{1,0:T(2,128)(2,1)}, bf16[2,18432]{1,0:T(2,128)(2,1)S(1)}, u32[]{:S(2)}, u32[]{:S(2)}) collective-permute-start(bf16[2,18432]{1,0:T(2,128)(2,1)} %shard_map.118), channel_id=1, source_target_pairs={{0,12},{1,13},{2,14},{3,15},{4,8},{5,9},{6,10},{7,11},{8,4},{9,5},... | collective-permute-start | bytes 221192 | tf_op jit(solution)/shard_map/ppermute | solution.py:379
  7.2 0.0 collective-permute-start.3
  7.2 0.6 collective-permute-start.1
  7.8 1.7 %collective-permute-start = (bf16[2,18432]{1,0:T(2,128)(2,1)}, bf16[2,18432]{1,0:T(2,128)(2,1)S(1)}, u32[]{:S(2)}, u32[]{:S(2)}) collective-permute-start(bf16[2,18432]{1,0:T(2,128)(2,1)} %shard_map.118), channel_id=1, source_target_pairs={{0,2},{1,3},{2,0},{3,1},{4,6},{5,7},{6,4},{7,5},{8,10},{9,11},{10,... | collective-permute-start | bytes 221192 | tf_op jit(solution)/shard_map/ppermute | solution.py:379
  9.5 1.0 bitcast_dynamic-update-slice_fusion.7
  10.5 0.0 collective-permute-done.5
  10.5 1.6 %collective-permute-start.6 = (bf16[2,18432]{1,0:T(2,128)(2,1)S(1)}, bf16[2,18432]{1,0:T(2,128)(2,1)S(1)}, u32[]{:S(2)}, u32[]{:S(2)}) collective-permute-start(bf16[2,18432]{1,0:T(2,128)(2,1)S(1)} %collective-permute-done.5), channel_id=1, source_target_pairs={{0,2},{1,3},{2,0},{3,1},{4,6},{5,7},{6,4},{7,5},{8,10},{9,11},{10,... | collective-permute-start | bytes 221192 | tf_op jit(solution)/shard_map/ppermute | solution.py:379
  12.0 1.6 %collective-permute-done.3 = bf16[2,18432]{1,0:T(2,128)(2,1)S(1)} collective-permute-done((bf16[2,18432]{1,0:T(2,128)(2,1)}, bf16[2,18432]{1,0:T(2,128)(2,1)S(1)}, u32[]{:S(2)}, u32[]{:S(2)}) %collective-permute-start.3) | collective-permute-done | bytes 73760 | tf_op jit(solution)/shard_map/ppermute | solution.py:379
  13.6 1.5 %collective-permute-start.4 = (bf16[2,18432]{1,0:T(2,128)(2,1)S(1)}, bf16[2,18432]{1,0:T(2,128)(2,1)S(1)}, u32[]{:S(2)}, u32[]{:S(2)}) collective-permute-start(bf16[2,18432]{1,0:T(2,128)(2,1)S(1)} %collective-permute-done.3), channel_id=1, source_target_pairs={{0,2},{1,3},{2,0},{3,1},{4,6},{5,7},{6,4},{7,5},{8,10},{9,11},{10,... | collective-permute-start | bytes 221192 | tf_op jit(solution)/shard_map/ppermute | solution.py:379
  15.1 0.0 collective-permute-done.1
  15.1 0.5 collective-permute-start.2
  15.7 0.0 collective-permute-done
  15.7 0.1 bitcast_dynamic-update-slice_fusion.6
  15.7 0.1 bitcast_dynamic-update-slice_fusion.5
  15.8 3.7 %collective-permute-done.2 = bf16[2,18432]{1,0:T(2,128)(2,1)S(1)} collective-permute-done((bf16[2,18432]{1,0:T(2,128)(2,1)S(1)}, bf16[2,18432]{1,0:T(2,128)(2,1)S(1)}, u32[]{:S(2)}, u32[]{:S(2)}) %collective-permute-start.2) | collective-permute-done | bytes 73760 | tf_op jit(solution)/shard_map/ppermute | solution.py:379
  19.5 0.1 bitcast_dynamic-update-slice_fusion.4
  19.6 0.1 bitcast_dynamic-update-slice_fusion.3
  19.6 0.0 collective-permute-done.4
  19.6 0.1 bitcast_dynamic-update-slice_fusion.2
  19.7 0.1 bitcast_dynamic-update-slice_fusion.1
  19.8 0.0 collective-permute-done.6
  19.8 0.1 bitcast_dynamic-update-slice_fusion.mine_ref
  19.9 0.1 collective-permute-start.7
  21.3 0.1 multiply_cosine_fusion.1
  21.4 0.5 collective-permute-done.7.other_ref
  21.9 9.8 %shard_map.119 = (f32[16,2,416]{2,1,0:T(2,128)}, bf16[32,18432]{1,0:T(8,128)(2,1)}) custom-call(s32[1]{0:T(128)} %bitcast.1.me_ref, bf16[8,2,18432]{2,1,0:T(2,128)(2,1)S(1)} %bitcast_dynamic-update-slice_fusion.mine_ref, bf16[8,2,18432]{2,1,0:T(2,128)(2,1)S(1)} %collective-permute-done.7.other_ref, bf16[384,18432]{1,0:T(8,128)(2,1)} %wq_ref.1, ...), custom_call_target="tpu_custom_call" | custom-call | flops 490733568 | bytes 15335424 | tf_op jit(solution)/shard_map/pallas_call | solution.py:111
  31.8 4.3 %all-to-all-start = ((f32[16,2,416]{2,1,0:T(2,128)}), f32[16,2,416]{2,1,0:T(2,128)S(1)}, u32[]{:S(2)}, u32[]{:S(2)}) async-start(f32[16,2,416]{2,1,0:T(2,128)} %get-tuple-element.17), calls=%async_computation | async-start | bytes 131072 | tf_op jit(solution)/shard_map/all_to_all | solution.py:416
  36.0 0.0 copy-start.3
  36.0 27.0 %shard_map.120.hidden_ref = bf16[32,576]{1,0:T(8,128)(2,1)} custom-call(bf16[32,18432]{1,0:T(8,128)(2,1)} %get-tuple-element.18.rows_ref, bf16[576,18432]{1,0:T(8,128)(2,1)} %wg_ref.1, bf16[576,18432]{1,0:T(8,128)(2,1)} %wu_ref.1), custom_call_target="tpu_custom_call" | custom-call | flops 1358954496 | bytes 42467328 | tf_op jit(solution)/shard_map/pallas_call | solution.py:175
  63.1 0.0 all-to-all-done
  63.2 0.1 reshape.342
  63.2 0.1 fusion.27
  63.4 0.0 copy-done
  63.4 0.4 fusion.31
  63.7 0.2 fusion.32
  64.0 0.2 fusion.6
  64.2 0.3 fusion.3
  64.4 0.2 fusion.1
  64.6 0.6 copy.17
  65.3 6.0 %all-to-all-start.1 = ((bf16[16,2,384]{2,1,0:T(2,128)(2,1)}), bf16[16,2,384]{2,1,0:T(2,128)(2,1)S(1)}, u32[]{:S(2)}, u32[]{:S(2)}) async-start(bf16[16,2,384]{2,1,0:T(2,128)(2,1)} %bitcast.62), calls=%async_computation.1 | async-start | bytes 49152 | tf_op jit(solution)/shard_map/all_to_all | solution.py:429
  71.3 0.8 copy-done.1
  72.1 7.9 %shard_map.121.part_ref = f32[32,18432]{1,0:T(8,128)S(1)} custom-call(bf16[32,576]{1,0:T(8,128)(2,1)S(1)} %copy-done.1, bf16[576,18432]{1,0:T(8,128)(2,1)} %w_ref.2), custom_call_target="tpu_custom_call" | custom-call | flops 679477248 | bytes 21233664 | tf_op jit(solution)/shard_map/pallas_call | solution.py:223
  79.9 0.0 copy-start.2
  80.0 0.0 all-to-all-done.1.attended_ref
  80.0 6.2 %shard_map.122 = (f32[16,18432]{1,0:T(8,128)S(1)}, bf16[16,18432]{1,0:T(8,128)(2,1)S(1)}) custom-call(s32[1]{0:T(128)} %bitcast.1.me_ref, bf16[16,2,384]{2,1,0:T(2,128)(2,1)S(1)} %all-to-all-done.1.attended_ref, f32[32,18432]{1,0:T(8,128)S(1)} %shard_map.121.part_ref, bf16[384,18432]{1,0:T(8,128)(2,1)} %w_ref.3), custom_call_target="tpu_custom_call" | custom-call | flops 452984832 | bytes 14155776 | tf_op jit(solution)/shard_map/pallas_call | solution.py:290
  86.2 0.5 collective-permute-start.8
  86.6 1.6 %collective-permute-done.8.came_ref = bf16[16,18432]{1,0:T(8,128)(2,1)S(1)} collective-permute-done((bf16[16,18432]{1,0:T(8,128)(2,1)S(1)}, bf16[16,18432]{1,0:T(8,128)(2,1)S(1)}, u32[]{:S(2)}, u32[]{:S(2)}) %collective-permute-start.8) | collective-permute-done | bytes 589856 | tf_op jit(solution)/shard_map/ppermute | solution.py:379
  88.3 0.4 shard_map.123
  88.7 2.0 %collective-permute-start.9 = (bf16[2,18432]{1,0:T(2,128)(2,1)S(1)}, bf16[2,18432]{1,0:T(2,128)(2,1)S(1)}, u32[]{:S(2)}, u32[]{:S(2)}) collective-permute-start(bf16[2,18432]{1,0:T(2,128)(2,1)S(1)} %get-tuple-element.22), channel_id=1, source_target_pairs={{0,2},{1,3},{2,0},{3,1},{4,6},{5,7},{6,4},{7,5},{8,10},{9,11},{10,... | collective-permute-start | bytes 221192 | tf_op jit(solution)/shard_map/ppermute | solution.py:379
  90.6 1.5 %collective-permute-start.10 = (bf16[2,18432]{1,0:T(2,128)(2,1)S(1)}, bf16[2,18432]{1,0:T(2,128)(2,1)S(1)}, u32[]{:S(2)}, u32[]{:S(2)}) collective-permute-start(bf16[2,18432]{1,0:T(2,128)(2,1)S(1)} %get-tuple-element.23), channel_id=1, source_target_pairs={{0,4},{1,5},{2,6},{3,7},{4,0},{5,1},{6,2},{7,3},{8,12},{9,13},{10,... | collective-permute-start | bytes 221192 | tf_op jit(solution)/shard_map/ppermute | solution.py:379
  92.1 0.1 collective-permute-start.11
  92.2 2.8 %collective-permute-start.12 = (bf16[2,18432]{1,0:T(2,128)(2,1)S(1)}, bf16[2,18432]{1,0:T(2,128)(2,1)S(1)}, u32[]{:S(2)}, u32[]{:S(2)}) collective-permute-start(bf16[2,18432]{1,0:T(2,128)(2,1)S(1)} %get-tuple-element.25), channel_id=1, source_target_pairs={{0,8},{1,9},{2,10},{3,11},{4,12},{5,13},{6,14},{7,15},{8,0},{9,1},... | collective-permute-start | bytes 221192 | tf_op jit(solution)/shard_map/ppermute | solution.py:379
  95.0 1.5 %collective-permute-start.13 = (bf16[2,18432]{1,0:T(2,128)(2,1)S(1)}, bf16[2,18432]{1,0:T(2,128)(2,1)S(1)}, u32[]{:S(2)}, u32[]{:S(2)}) collective-permute-start(bf16[2,18432]{1,0:T(2,128)(2,1)S(1)} %get-tuple-element.26), channel_id=1, source_target_pairs={{0,10},{1,11},{2,8},{3,9},{4,14},{5,15},{6,12},{7,13},{8,2},{9,3},... | collective-permute-start | bytes 221192 | tf_op jit(solution)/shard_map/ppermute | solution.py:379
  96.5 0.0 collective-permute-done.9
  96.5 3.3 %collective-permute-start.14 = (bf16[2,18432]{1,0:T(2,128)(2,1)S(1)}, bf16[2,18432]{1,0:T(2,128)(2,1)S(1)}, u32[]{:S(2)}, u32[]{:S(2)}) collective-permute-start(bf16[2,18432]{1,0:T(2,128)(2,1)S(1)} %get-tuple-element.27), channel_id=1, source_target_pairs={{0,12},{1,13},{2,14},{3,15},{4,8},{5,9},{6,10},{7,11},{8,4},{9,5},... | collective-permute-start | bytes 221192 | tf_op jit(solution)/shard_map/ppermute | solution.py:379
  99.8 0.0 collective-permute-done.10
  99.8 0.1 collective-permute-start.15
  99.9 0.0 collective-permute-done.11
  99.9 0.0 collective-permute-done.12
  99.9 7.3 %collective-permute-done.13 = bf16[2,18432]{1,0:T(2,128)(2,1)S(1)} collective-permute-done((bf16[2,18432]{1,0:T(2,128)(2,1)S(1)}, bf16[2,18432]{1,0:T(2,128)(2,1)S(1)}, u32[]{:S(2)}, u32[]{:S(2)}) %collective-permute-start.13) | collective-permute-done | bytes 73760 | tf_op jit(solution)/shard_map/ppermute | solution.py:379
  107.2 0.0 collective-permute-done.14
  107.2 0.0 collective-permute-done.15
  107.2 1.0 fusion.9
  (18 shorter events, 0.2 us)
Async XLA Ops:
  0.0 63.4 %copy-start = (bf16[1,1024,256]{2,1,0:T(8,128)(2,1)S(1)}, bf16[1,1024,256]{2,1,0:T(8,128)(2,1)}, u32[]{:S(2)}) copy-start(bf16[1,1024,256]{2,1,0:T(8,128)(2,1)} %param.20) | copy-start | bytes 1572868
  2.2 8.3 %collective-permute-start.5 = (bf16[2,18432]{1,0:T(2,128)(2,1)}, bf16[2,18432]{1,0:T(2,128)(2,1)S(1)}, u32[]{:S(2)}, u32[]{:S(2)}) collective-permute-start(bf16[2,18432]{1,0:T(2,128)(2,1)} %shard_map.118), channel_id=1, source_target_pairs={{0,12},{1,13},{2,14},{3,15},{4,8},{5,9},{6,10},{7,11},{8,4},{9,5},... | collective-permute-start | bytes 221192 | tf_op jit(solution)/shard_map/ppermute | solution.py:379
  7.2 6.4 %collective-permute-start.3 = (bf16[2,18432]{1,0:T(2,128)(2,1)}, bf16[2,18432]{1,0:T(2,128)(2,1)S(1)}, u32[]{:S(2)}, u32[]{:S(2)}) collective-permute-start(bf16[2,18432]{1,0:T(2,128)(2,1)} %shard_map.118), channel_id=1, source_target_pairs={{0,8},{1,9},{2,10},{3,11},{4,12},{5,13},{6,14},{7,15},{8,0},{9,1},... | collective-permute-start | bytes 221192 | tf_op jit(solution)/shard_map/ppermute | solution.py:379
  7.2 7.9 %collective-permute-start.1 = (bf16[2,18432]{1,0:T(2,128)(2,1)}, bf16[2,18432]{1,0:T(2,128)(2,1)S(1)}, u32[]{:S(2)}, u32[]{:S(2)}) collective-permute-start(bf16[2,18432]{1,0:T(2,128)(2,1)} %shard_map.118), channel_id=1, source_target_pairs={{0,4},{1,5},{2,6},{3,7},{4,0},{5,1},{6,2},{7,3},{8,12},{9,13},{10,... | collective-permute-start | bytes 221192 | tf_op jit(solution)/shard_map/ppermute | solution.py:379
  7.8 7.9 %collective-permute-start = (bf16[2,18432]{1,0:T(2,128)(2,1)}, bf16[2,18432]{1,0:T(2,128)(2,1)S(1)}, u32[]{:S(2)}, u32[]{:S(2)}) collective-permute-start(bf16[2,18432]{1,0:T(2,128)(2,1)} %shard_map.118), channel_id=1, source_target_pairs={{0,2},{1,3},{2,0},{3,1},{4,6},{5,7},{6,4},{7,5},{8,10},{9,11},{10,... | collective-permute-start | bytes 221192 | tf_op jit(solution)/shard_map/ppermute | solution.py:379
  10.5 9.3 %collective-permute-start.6 = (bf16[2,18432]{1,0:T(2,128)(2,1)S(1)}, bf16[2,18432]{1,0:T(2,128)(2,1)S(1)}, u32[]{:S(2)}, u32[]{:S(2)}) collective-permute-start(bf16[2,18432]{1,0:T(2,128)(2,1)S(1)} %collective-permute-done.5), channel_id=1, source_target_pairs={{0,2},{1,3},{2,0},{3,1},{4,6},{5,7},{6,4},{7,5},{8,10},{9,11},{10,... | collective-permute-start | bytes 221192 | tf_op jit(solution)/shard_map/ppermute | solution.py:379
  13.6 6.0 %collective-permute-start.4 = (bf16[2,18432]{1,0:T(2,128)(2,1)S(1)}, bf16[2,18432]{1,0:T(2,128)(2,1)S(1)}, u32[]{:S(2)}, u32[]{:S(2)}) collective-permute-start(bf16[2,18432]{1,0:T(2,128)(2,1)S(1)} %collective-permute-done.3), channel_id=1, source_target_pairs={{0,2},{1,3},{2,0},{3,1},{4,6},{5,7},{6,4},{7,5},{8,10},{9,11},{10,... | collective-permute-start | bytes 221192 | tf_op jit(solution)/shard_map/ppermute | solution.py:379
  15.1 4.4 %collective-permute-start.2 = (bf16[2,18432]{1,0:T(2,128)(2,1)S(1)}, bf16[2,18432]{1,0:T(2,128)(2,1)S(1)}, u32[]{:S(2)}, u32[]{:S(2)}) collective-permute-start(bf16[2,18432]{1,0:T(2,128)(2,1)S(1)} %collective-permute-done.1), channel_id=1, source_target_pairs={{0,2},{1,3},{2,0},{3,1},{4,6},{5,7},{6,4},{7,5},{8,10},{9,11},{10,... | collective-permute-start | bytes 221192 | tf_op jit(solution)/shard_map/ppermute | solution.py:379
  19.9 2.1 %collective-permute-start.7 = (bf16[8,2,18432]{2,1,0:T(2,128)(2,1)S(1)}, bf16[8,2,18432]{2,1,0:T(2,128)(2,1)S(1)}, u32[]{:S(2)}, u32[]{:S(2)}) collective-permute-start(bf16[8,2,18432]{2,1,0:T(2,128)(2,1)S(1)} %bitcast_dynamic-update-slice_fusion.mine_ref), channel_id=1, source_target_pairs={{0,1},{1,0},{2,3},{3,2},{4,5},{5,4},{6,7},{7,6},{8,9},{9,8},{10,11... | collective-permute-start | bytes 1769480 | tf_op jit(solution)/shard_map/ppermute | solution.py:379
  31.8 31.3 %all-to-all-start = ((f32[16,2,416]{2,1,0:T(2,128)}), f32[16,2,416]{2,1,0:T(2,128)S(1)}, u32[]{:S(2)}, u32[]{:S(2)}) async-start(f32[16,2,416]{2,1,0:T(2,128)} %get-tuple-element.17), calls=%async_computation | async-start | bytes 131072 | tf_op jit(solution)/shard_map/all_to_all | solution.py:416
  36.0 28.1 %copy-start.3 = (bf16[1,1024,256]{2,1,0:T(8,128)(2,1)S(1)}, bf16[1,1024,256]{2,1,0:T(8,128)(2,1)}, u32[]{:S(2)}) copy-start(bf16[1,1024,256]{2,1,0:T(8,128)(2,1)} %param.21) | copy-start | bytes 1572868
  65.3 14.7 %all-to-all-start.1 = ((bf16[16,2,384]{2,1,0:T(2,128)(2,1)}), bf16[16,2,384]{2,1,0:T(2,128)(2,1)S(1)}, u32[]{:S(2)}, u32[]{:S(2)}) async-start(bf16[16,2,384]{2,1,0:T(2,128)(2,1)} %bitcast.62), calls=%async_computation.1 | async-start | bytes 49152 | tf_op jit(solution)/shard_map/all_to_all | solution.py:429
  71.3 0.8 copy-start.1
  79.9 27.3 %copy-start.2 = (bf16[2,1,18432]{2,0,1:T(2,128)(2,1)S(1)}, bf16[2,1,18432]{2,0,1:T(2,128)(2,1)}, u32[]{:S(2)}) copy-start(bf16[2,1,18432]{2,0,1:T(2,128)(2,1)} %param.12) | copy-start | bytes 221188
  86.2 2.1 %collective-permute-start.8 = (bf16[16,18432]{1,0:T(8,128)(2,1)S(1)}, bf16[16,18432]{1,0:T(8,128)(2,1)S(1)}, u32[]{:S(2)}, u32[]{:S(2)}) collective-permute-start(bf16[16,18432]{1,0:T(8,128)(2,1)S(1)} %get-tuple-element.20), channel_id=1, source_target_pairs={{0,1},{1,0},{2,3},{3,2},{4,5},{5,4},{6,7},{7,6},{8,9},{9,8},{10,11... | collective-permute-start | bytes 1769480 | tf_op jit(solution)/shard_map/ppermute | solution.py:379
  88.7 7.8 %collective-permute-start.9 = (bf16[2,18432]{1,0:T(2,128)(2,1)S(1)}, bf16[2,18432]{1,0:T(2,128)(2,1)S(1)}, u32[]{:S(2)}, u32[]{:S(2)}) collective-permute-start(bf16[2,18432]{1,0:T(2,128)(2,1)S(1)} %get-tuple-element.22), channel_id=1, source_target_pairs={{0,2},{1,3},{2,0},{3,1},{4,6},{5,7},{6,4},{7,5},{8,10},{9,11},{10,... | collective-permute-start | bytes 221192 | tf_op jit(solution)/shard_map/ppermute | solution.py:379
  90.6 9.1 %collective-permute-start.10 = (bf16[2,18432]{1,0:T(2,128)(2,1)S(1)}, bf16[2,18432]{1,0:T(2,128)(2,1)S(1)}, u32[]{:S(2)}, u32[]{:S(2)}) collective-permute-start(bf16[2,18432]{1,0:T(2,128)(2,1)S(1)} %get-tuple-element.23), channel_id=1, source_target_pairs={{0,4},{1,5},{2,6},{3,7},{4,0},{5,1},{6,2},{7,3},{8,12},{9,13},{10,... | collective-permute-start | bytes 221192 | tf_op jit(solution)/shard_map/ppermute | solution.py:379
  92.1 7.8 %collective-permute-start.11 = (bf16[2,18432]{1,0:T(2,128)(2,1)S(1)}, bf16[2,18432]{1,0:T(2,128)(2,1)S(1)}, u32[]{:S(2)}, u32[]{:S(2)}) collective-permute-start(bf16[2,18432]{1,0:T(2,128)(2,1)S(1)} %get-tuple-element.24), channel_id=1, source_target_pairs={{0,6},{1,7},{2,4},{3,5},{4,2},{5,3},{6,0},{7,1},{8,14},{9,15},{10,... | collective-permute-start | bytes 221192 | tf_op jit(solution)/shard_map/ppermute | solution.py:379
  92.2 7.7 %collective-permute-start.12 = (bf16[2,18432]{1,0:T(2,128)(2,1)S(1)}, bf16[2,18432]{1,0:T(2,128)(2,1)S(1)}, u32[]{:S(2)}, u32[]{:S(2)}) collective-permute-start(bf16[2,18432]{1,0:T(2,128)(2,1)S(1)} %get-tuple-element.25), channel_id=1, source_target_pairs={{0,8},{1,9},{2,10},{3,11},{4,12},{5,13},{6,14},{7,15},{8,0},{9,1},... | collective-permute-start | bytes 221192 | tf_op jit(solution)/shard_map/ppermute | solution.py:379
  95.0 12.2 %collective-permute-start.13 = (bf16[2,18432]{1,0:T(2,128)(2,1)S(1)}, bf16[2,18432]{1,0:T(2,128)(2,1)S(1)}, u32[]{:S(2)}, u32[]{:S(2)}) collective-permute-start(bf16[2,18432]{1,0:T(2,128)(2,1)S(1)} %get-tuple-element.26), channel_id=1, source_target_pairs={{0,10},{1,11},{2,8},{3,9},{4,14},{5,15},{6,12},{7,13},{8,2},{9,3},... | collective-permute-start | bytes 221192 | tf_op jit(solution)/shard_map/ppermute | solution.py:379
  96.5 10.7 %collective-permute-start.14 = (bf16[2,18432]{1,0:T(2,128)(2,1)S(1)}, bf16[2,18432]{1,0:T(2,128)(2,1)S(1)}, u32[]{:S(2)}, u32[]{:S(2)}) collective-permute-start(bf16[2,18432]{1,0:T(2,128)(2,1)S(1)} %get-tuple-element.27), channel_id=1, source_target_pairs={{0,12},{1,13},{2,14},{3,15},{4,8},{5,9},{6,10},{7,11},{8,4},{9,5},... | collective-permute-start | bytes 221192 | tf_op jit(solution)/shard_map/ppermute | solution.py:379
  99.8 7.5 %collective-permute-start.15 = (bf16[2,18432]{1,0:T(2,128)(2,1)S(1)}, bf16[2,18432]{1,0:T(2,128)(2,1)S(1)}, u32[]{:S(2)}, u32[]{:S(2)}) collective-permute-start(bf16[2,18432]{1,0:T(2,128)(2,1)S(1)} %get-tuple-element.28), channel_id=1, source_target_pairs={{0,14},{1,15},{2,12},{3,13},{4,10},{5,11},{6,8},{7,9},{8,6},{9,7},... | collective-permute-start | bytes 221192 | tf_op jit(solution)/shard_map/ppermute | solution.py:379

commit v3 on v2

--- a/solution.py
+++ b/solution.py
@@ -50,99 +50,99 @@
 
 
 def attention_in_kernel(
-    chunks, me_ref, mine_ref, other_ref, wq_ref, wk_ref, out_ref, rows_ref,
-    pieces, spread, rows, wq, wk, acc_q, acc_k, piece_sem, q_sem, k_sem, rows_sem,
+    chunks, groups, me_ref, even_ref, odd_ref, wq_ref, wk_ref, out_ref, rows_ref,
+    spread, rows, acc, q_sem, k_sem, rows_sem, *weights,
 ):
-    half, steps, width = mine_ref.shape
-    step = width // chunks
+    half, steps, width = even_ref.shape
+    step = width // chunks
+    split = wq_ref.shape[0]
 
     def cols(c):
         return pl.ds(c * step, step)
 
-    piece_copies = [
-        pltpu.make_async_copy(mine_ref, pieces.at[pl.ds(0, half)], piece_sem.at[0]),
-        pltpu.make_async_copy(other_ref, pieces.at[pl.ds(half, half)], piece_sem.at[1]),
-    ]
-    q_copies = [
-        pltpu.make_async_copy(wq_ref.at[:, cols(c)], wq.at[c], q_sem.at[c]) for c in range(chunks)
-    ]
-    k_copies = [
-        pltpu.make_async_copy(wk_ref.at[:, cols(c)], wk.at[c], k_sem.at[c]) for c in range(chunks)
+    def place(c, which):
+        if groups == 2:
+            return weights[which].at[c]
+        return weights[0].at[c, pl.ds(which * split, (wq_ref, wk_ref)[which].shape[0])]
+
+    copies = [
+        (
+            pltpu.make_async_copy(wq_ref.at[:, cols(c)], place(c, 0), q_sem.at[c]),
+            pltpu.make_async_copy(wk_ref.at[:, cols(c)], place(c, 1), k_sem.at[c]),
+        )
+        for c in range(chunks)
     ]
     row_copies = [
         pltpu.make_async_copy(rows.at[:, cols(c)], rows_ref.at[:, cols(c)], rows_sem.at[c])
         for c in range(chunks)
     ]
-    for copy in piece_copies:
-        copy.start()
-    for c in range(chunks):
-        q_copies[c].start()
-        k_copies[c].start()
-    acc_q[...] = jnp.zeros_like(acc_q)
-    acc_k[...] = jnp.zeros_like(acc_k)
-    for copy in piece_copies:
-        copy.wait()
+    for pair in copies:
+        for copy in pair:
+            copy.start()
+    acc[...] = jnp.zeros_like(acc)
     for c in range(chunks):
         part = slice(c * step, (c + 1) * step)
-        for p in range(2 * half):
-            spread[p * steps : (p + 1) * steps, :] = pieces[p, :, part].astype(F32)
+        for p in range(half):
+            spread[p * steps : (p + 1) * steps, :] = even_ref[p, :, part].astype(F32)
+            q = half + p
+            spread[q * steps : (q + 1) * steps, :] = odd_ref[p, :, part].astype(F32)
         block = spread[...].astype(BF16)
         rows[:, part] = block
         row_copies[c].start()
-        q_copies[c].wait()
-        acc_q[...] += lax.dot_general(block, wq[c], NT, preferred_element_type=F32)
-        k_copies[c].wait()
-        acc_k[...] += lax.dot_general(block, wk[c], NT, preferred_element_type=F32)
-    split = acc_q.shape[1]
+        for copy in copies[c]:
+            copy.wait()
+        first = 0
+        for weight in weights:
+            last = first + weight.shape[1]
+            acc[:, first:last] += lax.dot_general(
+                block, weight[c], NT, preferred_element_type=F32
+            )
+            first = last
     for p in range(2 * half):
         owner = lax.bitwise_xor(me_ref[0], slot_at(p, half))
-        out_ref[owner, :, :split] = acc_q[p * steps : (p + 1) * steps, :]
-        out_ref[owner, :, split:] = acc_k[p * steps : (p + 1) * steps, :]
+        out_ref[owner] = acc[p * steps : (p + 1) * steps, :]
     for copy in row_copies:
         copy.wait()
 
 
-def attention_in(me, mine, other, w_query, w_keyval):
-    half, steps, width = mine.shape
+def attention_in(me, even, odd, w_query, w_keyval):
+    half, steps, width = even.shape
     n = 2 * half * steps
     chunks = cuts(width)
     step = width // chunks
     q_cols, k_cols = w_query.shape[0], w_keyval.shape[0]
-    return pl.pallas_call(
-        functools.partial(attention_in_kernel, chunks),
-        in_specs=[SMEM, ANY, ANY, ANY, ANY],
+    groups = 1 if q_cols % 16 == 0 and k_cols % 16 == 0 else 2
+    sizes = [q_cols + k_cols] if groups == 1 else [q_cols, k_cols]
+    return pl.pallas_call(
+        functools.partial(attention_in_kernel, chunks, groups),
+        in_specs=[SMEM, VMEM, VMEM, ANY, ANY],
         out_specs=[VMEM, ANY],
         out_shape=[
             jax.ShapeDtypeStruct((2 * half, steps, q_cols + k_cols), F32),
             jax.ShapeDtypeStruct((n, width), BF16),
         ],
         scratch_shapes=[
-            pltpu.VMEM((2 * half, steps, width), BF16),
             pltpu.VMEM((n, step), F32),
             pltpu.VMEM((n, width), BF16),
-            pltpu.VMEM((chunks, q_cols, step), BF16),
-            pltpu.VMEM((chunks, k_cols, step), BF16),
-            pltpu.VMEM((n, q_cols), F32),
-            pltpu.VMEM((n, k_cols), F32),
-            pltpu.SemaphoreType.DMA((2,)),
-            pltpu.SemaphoreType.DMA((chunks,)),
-            pltpu.SemaphoreType.DMA((chunks,)),
-            pltpu.SemaphoreType.DMA((chunks,)),
-        ],
+            pltpu.VMEM((n, q_cols + k_cols), F32),
+            pltpu.SemaphoreType.DMA((chunks,)),
+            pltpu.SemaphoreType.DMA((chunks,)),
+            pltpu.SemaphoreType.DMA((chunks,)),
+        ]
+        + [pltpu.VMEM((chunks, size, step), BF16) for size in sizes],
         compiler_params=params(52),
         cost_estimate=cost(n, w_query, w_keyval),
-    )(me, mine, other, w_query, w_keyval)
+    )(me, even, odd, w_query, w_keyval)
 
 
 def hidden_kernel(
-    chunks, rows_ref, wg_ref, wu_ref, out_ref, rows, wg, wu, acc_g, acc_u, row_sem, g_sem, u_sem
+    chunks, rows_ref, wg_ref, wu_ref, out_ref, wg, wu, acc_g, acc_u, g_sem, u_sem
 ):
     step = rows_ref.shape[1] // chunks
 
     def cols(c):
         return pl.ds(c * step, step)
 
-    row_copy = pltpu.make_async_copy(rows_ref, rows, row_sem)
     copies = [
         (
             pltpu.make_async_copy(wg_ref.at[:, cols(c)], wg.at[c], g_sem.at[c]),
@@ -150,15 +150,13 @@
         )
         for c in range(chunks)
     ]
-    row_copy.start()
     for gate_copy, up_copy in copies:
         gate_copy.start()
         up_copy.start()
     acc_g[...] = jnp.zeros_like(acc_g)
     acc_u[...] = jnp.zeros_like(acc_u)
-    row_copy.wait()
     for c in range(chunks):
-        block = rows[:, c * step : (c + 1) * step]
+        block = rows_ref[:, c * step : (c + 1) * step]
         copies[c][0].wait()
         acc_g[...] += lax.dot_general(block, wg[c], NT, preferred_element_type=F32)
         copies[c][1].wait()
@@ -174,16 +172,14 @@
     step = width // chunks
     return pl.pallas_call(
         functools.partial(hidden_kernel, chunks),
-        in_specs=[ANY, ANY, ANY],
+        in_specs=[VMEM, ANY, ANY],
         out_specs=VMEM,
         out_shape=jax.ShapeDtypeStruct((n, units), BF16),
         scratch_shapes=[
-            pltpu.VMEM((n, width), BF16),
             pltpu.VMEM((chunks, units, step), BF16),
             pltpu.VMEM((chunks, units, step), BF16),
             pltpu.VMEM((n, units), F32),
             pltpu.VMEM((n, units), F32),
-            pltpu.SemaphoreType.DMA,
             pltpu.SemaphoreType.DMA((chunks,)),
             pltpu.SemaphoreType.DMA((chunks,)),
         ],

time: 109 us -> 98.3 us (0.902)
  Pallas kernels: 53.5 us -> 43.1 us
    pallas_call x2, Pallas kernels: 36.8 us -> 26.5 us  [the longest x1 18.1 us: hidden_units(): pl.pallas_call(functools.partial(hidden_kernel, chunks), in_specs=[VMEM,...]
  transfers between devices with their start and end apart: 18 -> 18, of which waited for: 5 -> 5; matrix products, arithmetic and copies ran while one was open for 1% -> 2% of each run, Pallas kernels for 32% -> 27%
where the time goes in v3:
time: 98.3 us; the launch traced here: 97.8 us
  Pallas kernels  43.1 us (44%)
  starting transfers between devices  32.9 us (33%)
  waiting for transfers between devices  14.8 us (15%)
  local copies, waits for them, and re-layouts  3.01 us (3%)
  between operations  1.56 us (2%)
  other arithmetic  1.45 us (1%)
    ppermute x16, starting transfers between devices, swap(): return lax.ppermute(value, 'gx', [(i, i ^ bits) for i in range(devices)])  22.7 us
    pallas_call x1, Pallas kernels, hidden_units(): pl.pallas_call(functools.partial(hidden_kernel, chunks), in_specs=[VMEM,...  18.1 us
    ppermute x16, waiting for transfers between devices, swap(): return lax.ppermute(value, 'gx', [(i, i ^ bits) for i in range(devices)])  14.8 us
    pallas_call x1, Pallas kernels, attention_in(): pl.pallas_call(functools.partial(attention_in_kernel, chunks, groups), in...  8.37 us
    pallas_call x1, Pallas kernels, down_part(): pl.pallas_call(functools.partial(down_kernel, chunks), in_specs=[VMEM, AN...  7.87 us
    pallas_call x1, Pallas kernels, branch_parts(): pl.pallas_call(functools.partial(branch_kernel, chunks), in_specs=[SMEM,...  6.19 us
    all_to_all x1, starting transfers between devices, local(): lax.all_to_all(attended, 'gx', split_axis=0, concat_axis=0, tiled=True)  6.01 us
    all_to_all x1, starting transfers between devices, local(): lax.all_to_all(projected, 'gx', split_axis=0, concat_axis=0, tiled=True)  4.26 us
  transfers between devices with their start and end apart: 18, of which 5 were waited for; matrix products, arithmetic and copies ran while one was open for 2% of the time, Pallas kernels for 27%

profile of v3, /device:TPU:0, one launch (start us, length us, event | category | flops | bytes accessed | tf_op | source)
XLA Modules:
  0.0 97.8 jit_solution(3071714481751022083)
XLA Ops:
  0.0 2.2 %shard_map.118 = bf16[2,18432]{1,0:T(2,128)(2,1)} custom-call(bf16[2,18432]{1,0:T(2,128)(2,1)} %bitcast.65, f32[1,18432]{1,0:T(1,128)} %bitcast.68), custom_call_target="tpu_custom_call" | custom-call | tf_op jit(solution)/shard_map/pallas_call | solution.py:47
  2.2 5.0 %collective-permute-start.5 = (bf16[2,18432]{1,0:T(2,128)(2,1)}, bf16[2,18432]{1,0:T(2,128)(2,1)S(1)}, u32[]{:S(2)}, u32[]{:S(2)}) collective-permute-start(bf16[2,18432]{1,0:T(2,128)(2,1)} %shard_map.118), channel_id=1, source_target_pairs={{0,12},{1,13},{2,14},{3,15},{4,8},{5,9},{6,10},{7,11},{8,4},{9,5},... | collective-permute-start | bytes 221192 | tf_op jit(solution)/shard_map/ppermute | solution.py:375
  7.2 0.0 collective-permute-start.3
  7.2 0.6 collective-permute-start.1
  7.8 1.7 %collective-permute-start = (bf16[2,18432]{1,0:T(2,128)(2,1)}, bf16[2,18432]{1,0:T(2,128)(2,1)S(1)}, u32[]{:S(2)}, u32[]{:S(2)}) collective-permute-start(bf16[2,18432]{1,0:T(2,128)(2,1)} %shard_map.118), channel_id=1, source_target_pairs={{0,2},{1,3},{2,0},{3,1},{4,6},{5,7},{6,4},{7,5},{8,10},{9,11},{10,... | collective-permute-start | bytes 221192 | tf_op jit(solution)/shard_map/ppermute | solution.py:375
  9.5 1.0 bitcast_dynamic-update-slice_fusion.7
  10.5 0.0 collective-permute-done.5
  10.5 1.6 %collective-permute-start.6 = (bf16[2,18432]{1,0:T(2,128)(2,1)S(1)}, bf16[2,18432]{1,0:T(2,128)(2,1)S(1)}, u32[]{:S(2)}, u32[]{:S(2)}) collective-permute-start(bf16[2,18432]{1,0:T(2,128)(2,1)S(1)} %collective-permute-done.5), channel_id=1, source_target_pairs={{0,2},{1,3},{2,0},{3,1},{4,6},{5,7},{6,4},{7,5},{8,10},{9,11},{10,... | collective-permute-start | bytes 221192 | tf_op jit(solution)/shard_map/ppermute | solution.py:375
  12.0 1.6 %collective-permute-done.3 = bf16[2,18432]{1,0:T(2,128)(2,1)S(1)} collective-permute-done((bf16[2,18432]{1,0:T(2,128)(2,1)}, bf16[2,18432]{1,0:T(2,128)(2,1)S(1)}, u32[]{:S(2)}, u32[]{:S(2)}) %collective-permute-start.3) | collective-permute-done | bytes 73760 | tf_op jit(solution)/shard_map/ppermute | solution.py:375
  13.6 1.5 %collective-permute-start.4 = (bf16[2,18432]{1,0:T(2,128)(2,1)S(1)}, bf16[2,18432]{1,0:T(2,128)(2,1)S(1)}, u32[]{:S(2)}, u32[]{:S(2)}) collective-permute-start(bf16[2,18432]{1,0:T(2,128)(2,1)S(1)} %collective-permute-done.3), channel_id=1, source_target_pairs={{0,2},{1,3},{2,0},{3,1},{4,6},{5,7},{6,4},{7,5},{8,10},{9,11},{10,... | collective-permute-start | bytes 221192 | tf_op jit(solution)/shard_map/ppermute | solution.py:375
  15.1 0.0 collective-permute-done.1
  15.1 0.5 collective-permute-start.2
  15.7 0.0 collective-permute-done
  15.7 0.1 bitcast_dynamic-update-slice_fusion.6
  15.7 0.1 bitcast_dynamic-update-slice_fusion.5
  15.8 3.7 %collective-permute-done.2 = bf16[2,18432]{1,0:T(2,128)(2,1)S(1)} collective-permute-done((bf16[2,18432]{1,0:T(2,128)(2,1)S(1)}, bf16[2,18432]{1,0:T(2,128)(2,1)S(1)}, u32[]{:S(2)}, u32[]{:S(2)}) %collective-permute-start.2) | collective-permute-done | bytes 73760 | tf_op jit(solution)/shard_map/ppermute | solution.py:375
  19.5 0.1 bitcast_dynamic-update-slice_fusion.4
  19.6 0.1 bitcast_dynamic-update-slice_fusion.3
  19.6 0.0 collective-permute-done.4
  19.6 0.1 bitcast_dynamic-update-slice_fusion.2
  19.7 0.1 bitcast_dynamic-update-slice_fusion.1
  19.8 0.0 collective-permute-done.6
  19.8 0.1 bitcast_dynamic-update-slice_fusion.even_ref
  19.9 0.1 collective-permute-start.7
  21.3 0.1 multiply_cosine_fusion.1
  21.4 0.5 collective-permute-done.7.odd_ref
  21.9 8.4 %shard_map.119 = (f32[16,2,416]{2,1,0:T(2,128)}, bf16[32,18432]{1,0:T(8,128)(2,1)}) custom-call(s32[1]{0:T(128)} %bitcast.1.me_ref, bf16[8,2,18432]{2,1,0:T(2,128)(2,1)S(1)} %bitcast_dynamic-update-slice_fusion.even_ref, bf16[8,2,18432]{2,1,0:T(2,128)(2,1)S(1)} %collective-permute-done.7.odd_ref, bf16[384,18432]{1,0:T(8,128)(2,1)} %wq_ref.1, ...), custom_call_target="tpu_custom_call" | custom-call | flops 490733568 | bytes 15335424 | tf_op jit(solution)/shard_map/pallas_call | solution.py:116
  30.3 4.3 %all-to-all-start = ((f32[16,2,416]{2,1,0:T(2,128)}), f32[16,2,416]{2,1,0:T(2,128)S(1)}, u32[]{:S(2)}, u32[]{:S(2)}) async-start(f32[16,2,416]{2,1,0:T(2,128)} %get-tuple-element.17), calls=%async_computation | async-start | bytes 131072 | tf_op jit(solution)/shard_map/all_to_all | solution.py:412
  34.6 0.0 copy-start.3
  34.6 18.1 %shard_map.120.hidden_ref = bf16[32,576]{1,0:T(8,128)(2,1)} custom-call(bf16[32,18432]{1,0:T(8,128)(2,1)} %get-tuple-element.18.rows_ref, bf16[576,18432]{1,0:T(8,128)(2,1)} %wg_ref.1, bf16[576,18432]{1,0:T(8,128)(2,1)} %wu_ref.1), custom_call_target="tpu_custom_call" | custom-call | flops 1358954496 | bytes 42467328 | tf_op jit(solution)/shard_map/pallas_call | solution.py:173
  52.7 0.0 all-to-all-done
  52.8 0.1 reshape.342
  52.9 0.1 fusion.27
  53.0 0.4 fusion.31
  53.4 0.2 fusion.32
  53.6 0.2 fusion.6
  53.8 0.3 fusion.3
  54.0 0.2 fusion.1
  54.3 0.6 copy.17
  54.9 6.0 %all-to-all-start.1 = ((bf16[16,2,384]{2,1,0:T(2,128)(2,1)}), bf16[16,2,384]{2,1,0:T(2,128)(2,1)S(1)}, u32[]{:S(2)}, u32[]{:S(2)}) async-start(bf16[16,2,384]{2,1,0:T(2,128)(2,1)} %bitcast.62), calls=%async_computation.1 | async-start | bytes 49152 | tf_op jit(solution)/shard_map/all_to_all | solution.py:425
  60.9 0.8 copy-done.1
  61.7 7.9 %shard_map.121.part_ref = f32[32,18432]{1,0:T(8,128)S(1)} custom-call(bf16[32,576]{1,0:T(8,128)(2,1)S(1)} %copy-done.1, bf16[576,18432]{1,0:T(8,128)(2,1)} %w_ref.2), custom_call_target="tpu_custom_call" | custom-call | flops 679477248 | bytes 21233664 | tf_op jit(solution)/shard_map/pallas_call | solution.py:219
  69.6 0.0 copy-start.2
  69.6 0.0 all-to-all-done.1.attended_ref
  69.6 6.2 %shard_map.122 = (f32[16,18432]{1,0:T(8,128)S(1)}, bf16[16,18432]{1,0:T(8,128)(2,1)S(1)}) custom-call(s32[1]{0:T(128)} %bitcast.1.me_ref, bf16[16,2,384]{2,1,0:T(2,128)(2,1)S(1)} %all-to-all-done.1.attended_ref, f32[32,18432]{1,0:T(8,128)S(1)} %shard_map.121.part_ref, bf16[384,18432]{1,0:T(8,128)(2,1)} %w_ref.3), custom_call_target="tpu_custom_call" | custom-call | flops 452984832 | bytes 14155776 | tf_op jit(solution)/shard_map/pallas_call | solution.py:286
  75.8 0.5 collective-permute-start.8
  76.3 1.6 %collective-permute-done.8.came_ref = bf16[16,18432]{1,0:T(8,128)(2,1)S(1)} collective-permute-done((bf16[16,18432]{1,0:T(8,128)(2,1)S(1)}, bf16[16,18432]{1,0:T(8,128)(2,1)S(1)}, u32[]{:S(2)}, u32[]{:S(2)}) %collective-permute-start.8) | collective-permute-done | bytes 589856 | tf_op jit(solution)/shard_map/ppermute | solution.py:375
  77.9 0.4 shard_map.123
  78.3 2.0 %collective-permute-start.9 = (bf16[2,18432]{1,0:T(2,128)(2,1)S(1)}, bf16[2,18432]{1,0:T(2,128)(2,1)S(1)}, u32[]{:S(2)}, u32[]{:S(2)}) collective-permute-start(bf16[2,18432]{1,0:T(2,128)(2,1)S(1)} %get-tuple-element.22), channel_id=1, source_target_pairs={{0,2},{1,3},{2,0},{3,1},{4,6},{5,7},{6,4},{7,5},{8,10},{9,11},{10,... | collective-permute-start | bytes 221192 | tf_op jit(solution)/shard_map/ppermute | solution.py:375
  80.3 1.5 %collective-permute-start.10 = (bf16[2,18432]{1,0:T(2,128)(2,1)S(1)}, bf16[2,18432]{1,0:T(2,128)(2,1)S(1)}, u32[]{:S(2)}, u32[]{:S(2)}) collective-permute-start(bf16[2,18432]{1,0:T(2,128)(2,1)S(1)} %get-tuple-element.23), channel_id=1, source_target_pairs={{0,4},{1,5},{2,6},{3,7},{4,0},{5,1},{6,2},{7,3},{8,12},{9,13},{10,... | collective-permute-start | bytes 221192 | tf_op jit(solution)/shard_map/ppermute | solution.py:375
  81.7 0.1 collective-permute-start.11
  81.9 2.8 %collective-permute-start.12 = (bf16[2,18432]{1,0:T(2,128)(2,1)S(1)}, bf16[2,18432]{1,0:T(2,128)(2,1)S(1)}, u32[]{:S(2)}, u32[]{:S(2)}) collective-permute-start(bf16[2,18432]{1,0:T(2,128)(2,1)S(1)} %get-tuple-element.25), channel_id=1, source_target_pairs={{0,8},{1,9},{2,10},{3,11},{4,12},{5,13},{6,14},{7,15},{8,0},{9,1},... | collective-permute-start | bytes 221192 | tf_op jit(solution)/shard_map/ppermute | solution.py:375
  84.6 1.5 %collective-permute-start.13 = (bf16[2,18432]{1,0:T(2,128)(2,1)S(1)}, bf16[2,18432]{1,0:T(2,128)(2,1)S(1)}, u32[]{:S(2)}, u32[]{:S(2)}) collective-permute-start(bf16[2,18432]{1,0:T(2,128)(2,1)S(1)} %get-tuple-element.26), channel_id=1, source_target_pairs={{0,10},{1,11},{2,8},{3,9},{4,14},{5,15},{6,12},{7,13},{8,2},{9,3},... | collective-permute-start | bytes 221192 | tf_op jit(solution)/shard_map/ppermute | solution.py:375
  86.1 0.0 collective-permute-done.9
  86.1 3.3 %collective-permute-start.14 = (bf16[2,18432]{1,0:T(2,128)(2,1)S(1)}, bf16[2,18432]{1,0:T(2,128)(2,1)S(1)}, u32[]{:S(2)}, u32[]{:S(2)}) collective-permute-start(bf16[2,18432]{1,0:T(2,128)(2,1)S(1)} %get-tuple-element.27), channel_id=1, source_target_pairs={{0,12},{1,13},{2,14},{3,15},{4,8},{5,9},{6,10},{7,11},{8,4},{9,5},... | collective-permute-start | bytes 221192 | tf_op jit(solution)/shard_map/ppermute | solution.py:375
  89.4 0.0 collective-permute-done.10
  89.4 0.1 collective-permute-start.15
  89.5 0.0 collective-permute-done.11
  89.5 0.0 collective-permute-done.12
  89.5 7.3 %collective-permute-done.13 = bf16[2,18432]{1,0:T(2,128)(2,1)S(1)} collective-permute-done((bf16[2,18432]{1,0:T(2,128)(2,1)S(1)}, bf16[2,18432]{1,0:T(2,128)(2,1)S(1)}, u32[]{:S(2)}, u32[]{:S(2)}) %collective-permute-start.13) | collective-permute-done | bytes 73760 | tf_op jit(solution)/shard_map/ppermute | solution.py:375
  96.8 0.0 collective-permute-done.14
  96.8 0.0 collective-permute-done.15
  96.8 0.0 copy-done.2
  96.9 1.0 fusion.9
  (18 shorter events, 0.2 us)
Async XLA Ops:
  0.0 53.0 %copy-start = (bf16[1,1024,256]{2,1,0:T(8,128)(2,1)S(1)}, bf16[1,1024,256]{2,1,0:T(8,128)(2,1)}, u32[]{:S(2)}) copy-start(bf16[1,1024,256]{2,1,0:T(8,128)(2,1)} %param.20) | copy-start | bytes 1572868
  2.2 8.3 %collective-permute-start.5 = (bf16[2,18432]{1,0:T(2,128)(2,1)}, bf16[2,18432]{1,0:T(2,128)(2,1)S(1)}, u32[]{:S(2)}, u32[]{:S(2)}) collective-permute-start(bf16[2,18432]{1,0:T(2,128)(2,1)} %shard_map.118), channel_id=1, source_target_pairs={{0,12},{1,13},{2,14},{3,15},{4,8},{5,9},{6,10},{7,11},{8,4},{9,5},... | collective-permute-start | bytes 221192 | tf_op jit(solution)/shard_map/ppermute | solution.py:375
  7.2 6.4 %collective-permute-start.3 = (bf16[2,18432]{1,0:T(2,128)(2,1)}, bf16[2,18432]{1,0:T(2,128)(2,1)S(1)}, u32[]{:S(2)}, u32[]{:S(2)}) collective-permute-start(bf16[2,18432]{1,0:T(2,128)(2,1)} %shard_map.118), channel_id=1, source_target_pairs={{0,8},{1,9},{2,10},{3,11},{4,12},{5,13},{6,14},{7,15},{8,0},{9,1},... | collective-permute-start | bytes 221192 | tf_op jit(solution)/shard_map/ppermute | solution.py:375
  7.2 7.9 %collective-permute-start.1 = (bf16[2,18432]{1,0:T(2,128)(2,1)}, bf16[2,18432]{1,0:T(2,128)(2,1)S(1)}, u32[]{:S(2)}, u32[]{:S(2)}) collective-permute-start(bf16[2,18432]{1,0:T(2,128)(2,1)} %shard_map.118), channel_id=1, source_target_pairs={{0,4},{1,5},{2,6},{3,7},{4,0},{5,1},{6,2},{7,3},{8,12},{9,13},{10,... | collective-permute-start | bytes 221192 | tf_op jit(solution)/shard_map/ppermute | solution.py:375
  7.8 7.9 %collective-permute-start = (bf16[2,18432]{1,0:T(2,128)(2,1)}, bf16[2,18432]{1,0:T(2,128)(2,1)S(1)}, u32[]{:S(2)}, u32[]{:S(2)}) collective-permute-start(bf16[2,18432]{1,0:T(2,128)(2,1)} %shard_map.118), channel_id=1, source_target_pairs={{0,2},{1,3},{2,0},{3,1},{4,6},{5,7},{6,4},{7,5},{8,10},{9,11},{10,... | collective-permute-start | bytes 221192 | tf_op jit(solution)/shard_map/ppermute | solution.py:375
  10.5 9.3 %collective-permute-start.6 = (bf16[2,18432]{1,0:T(2,128)(2,1)S(1)}, bf16[2,18432]{1,0:T(2,128)(2,1)S(1)}, u32[]{:S(2)}, u32[]{:S(2)}) collective-permute-start(bf16[2,18432]{1,0:T(2,128)(2,1)S(1)} %collective-permute-done.5), channel_id=1, source_target_pairs={{0,2},{1,3},{2,0},{3,1},{4,6},{5,7},{6,4},{7,5},{8,10},{9,11},{10,... | collective-permute-start | bytes 221192 | tf_op jit(solution)/shard_map/ppermute | solution.py:375
  13.6 6.0 %collective-permute-start.4 = (bf16[2,18432]{1,0:T(2,128)(2,1)S(1)}, bf16[2,18432]{1,0:T(2,128)(2,1)S(1)}, u32[]{:S(2)}, u32[]{:S(2)}) collective-permute-start(bf16[2,18432]{1,0:T(2,128)(2,1)S(1)} %collective-permute-done.3), channel_id=1, source_target_pairs={{0,2},{1,3},{2,0},{3,1},{4,6},{5,7},{6,4},{7,5},{8,10},{9,11},{10,... | collective-permute-start | bytes 221192 | tf_op jit(solution)/shard_map/ppermute | solution.py:375
  15.1 4.4 %collective-permute-start.2 = (bf16[2,18432]{1,0:T(2,128)(2,1)S(1)}, bf16[2,18432]{1,0:T(2,128)(2,1)S(1)}, u32[]{:S(2)}, u32[]{:S(2)}) collective-permute-start(bf16[2,18432]{1,0:T(2,128)(2,1)S(1)} %collective-permute-done.1), channel_id=1, source_target_pairs={{0,2},{1,3},{2,0},{3,1},{4,6},{5,7},{6,4},{7,5},{8,10},{9,11},{10,... | collective-permute-start | bytes 221192 | tf_op jit(solution)/shard_map/ppermute | solution.py:375
  19.9 2.1 %collective-permute-start.7 = (bf16[8,2,18432]{2,1,0:T(2,128)(2,1)S(1)}, bf16[8,2,18432]{2,1,0:T(2,128)(2,1)S(1)}, u32[]{:S(2)}, u32[]{:S(2)}) collective-permute-start(bf16[8,2,18432]{2,1,0:T(2,128)(2,1)S(1)} %bitcast_dynamic-update-slice_fusion.even_ref), channel_id=1, source_target_pairs={{0,1},{1,0},{2,3},{3,2},{4,5},{5,4},{6,7},{7,6},{8,9},{9,8},{10,11... | collective-permute-start | bytes 1769480 | tf_op jit(solution)/shard_map/ppermute | solution.py:375
  30.3 22.4 %all-to-all-start = ((f32[16,2,416]{2,1,0:T(2,128)}), f32[16,2,416]{2,1,0:T(2,128)S(1)}, u32[]{:S(2)}, u32[]{:S(2)}) async-start(f32[16,2,416]{2,1,0:T(2,128)} %get-tuple-element.17), calls=%async_computation | async-start | bytes 131072 | tf_op jit(solution)/shard_map/all_to_all | solution.py:412
  34.6 19.2 %copy-start.3 = (bf16[1,1024,256]{2,1,0:T(8,128)(2,1)S(1)}, bf16[1,1024,256]{2,1,0:T(8,128)(2,1)}, u32[]{:S(2)}) copy-start(bf16[1,1024,256]{2,1,0:T(8,128)(2,1)} %param.21) | copy-start | bytes 1572868
  54.9 14.7 %all-to-all-start.1 = ((bf16[16,2,384]{2,1,0:T(2,128)(2,1)}), bf16[16,2,384]{2,1,0:T(2,128)(2,1)S(1)}, u32[]{:S(2)}, u32[]{:S(2)}) async-start(bf16[16,2,384]{2,1,0:T(2,128)(2,1)} %bitcast.62), calls=%async_computation.1 | async-start | bytes 49152 | tf_op jit(solution)/shard_map/all_to_all | solution.py:425
  60.9 0.8 copy-start.1
  69.6 27.3 %copy-start.2 = (bf16[2,1,18432]{2,0,1:T(2,128)(2,1)S(1)}, bf16[2,1,18432]{2,0,1:T(2,128)(2,1)}, u32[]{:S(2)}) copy-start(bf16[2,1,18432]{2,0,1:T(2,128)(2,1)} %param.12) | copy-start | bytes 221188
  75.8 2.1 %collective-permute-start.8 = (bf16[16,18432]{1,0:T(8,128)(2,1)S(1)}, bf16[16,18432]{1,0:T(8,128)(2,1)S(1)}, u32[]{:S(2)}, u32[]{:S(2)}) collective-permute-start(bf16[16,18432]{1,0:T(8,128)(2,1)S(1)} %get-tuple-element.20), channel_id=1, source_target_pairs={{0,1},{1,0},{2,3},{3,2},{4,5},{5,4},{6,7},{7,6},{8,9},{9,8},{10,11... | collective-permute-start | bytes 1769480 | tf_op jit(solution)/shard_map/ppermute | solution.py:375
  78.3 7.8 %collective-permute-start.9 = (bf16[2,18432]{1,0:T(2,128)(2,1)S(1)}, bf16[2,18432]{1,0:T(2,128)(2,1)S(1)}, u32[]{:S(2)}, u32[]{:S(2)}) collective-permute-start(bf16[2,18432]{1,0:T(2,128)(2,1)S(1)} %get-tuple-element.22), channel_id=1, source_target_pairs={{0,2},{1,3},{2,0},{3,1},{4,6},{5,7},{6,4},{7,5},{8,10},{9,11},{10,... | collective-permute-start | bytes 221192 | tf_op jit(solution)/shard_map/ppermute | solution.py:375
  80.3 9.1 %collective-permute-start.10 = (bf16[2,18432]{1,0:T(2,128)(2,1)S(1)}, bf16[2,18432]{1,0:T(2,128)(2,1)S(1)}, u32[]{:S(2)}, u32[]{:S(2)}) collective-permute-start(bf16[2,18432]{1,0:T(2,128)(2,1)S(1)} %get-tuple-element.23), channel_id=1, source_target_pairs={{0,4},{1,5},{2,6},{3,7},{4,0},{5,1},{6,2},{7,3},{8,12},{9,13},{10,... | collective-permute-start | bytes 221192 | tf_op jit(solution)/shard_map/ppermute | solution.py:375
  81.7 7.8 %collective-permute-start.11 = (bf16[2,18432]{1,0:T(2,128)(2,1)S(1)}, bf16[2,18432]{1,0:T(2,128)(2,1)S(1)}, u32[]{:S(2)}, u32[]{:S(2)}) collective-permute-start(bf16[2,18432]{1,0:T(2,128)(2,1)S(1)} %get-tuple-element.24), channel_id=1, source_target_pairs={{0,6},{1,7},{2,4},{3,5},{4,2},{5,3},{6,0},{7,1},{8,14},{9,15},{10,... | collective-permute-start | bytes 221192 | tf_op jit(solution)/shard_map/ppermute | solution.py:375
  81.9 7.7 %collective-permute-start.12 = (bf16[2,18432]{1,0:T(2,128)(2,1)S(1)}, bf16[2,18432]{1,0:T(2,128)(2,1)S(1)}, u32[]{:S(2)}, u32[]{:S(2)}) collective-permute-start(bf16[2,18432]{1,0:T(2,128)(2,1)S(1)} %get-tuple-element.25), channel_id=1, source_target_pairs={{0,8},{1,9},{2,10},{3,11},{4,12},{5,13},{6,14},{7,15},{8,0},{9,1},... | collective-permute-start | bytes 221192 | tf_op jit(solution)/shard_map/ppermute | solution.py:375
  84.6 12.2 %collective-permute-start.13 = (bf16[2,18432]{1,0:T(2,128)(2,1)S(1)}, bf16[2,18432]{1,0:T(2,128)(2,1)S(1)}, u32[]{:S(2)}, u32[]{:S(2)}) collective-permute-start(bf16[2,18432]{1,0:T(2,128)(2,1)S(1)} %get-tuple-element.26), channel_id=1, source_target_pairs={{0,10},{1,11},{2,8},{3,9},{4,14},{5,15},{6,12},{7,13},{8,2},{9,3},... | collective-permute-start | bytes 221192 | tf_op jit(solution)/shard_map/ppermute | solution.py:375
  86.1 10.7 %collective-permute-start.14 = (bf16[2,18432]{1,0:T(2,128)(2,1)S(1)}, bf16[2,18432]{1,0:T(2,128)(2,1)S(1)}, u32[]{:S(2)}, u32[]{:S(2)}) collective-permute-start(bf16[2,18432]{1,0:T(2,128)(2,1)S(1)} %get-tuple-element.27), channel_id=1, source_target_pairs={{0,12},{1,13},{2,14},{3,15},{4,8},{5,9},{6,10},{7,11},{8,4},{9,5},... | collective-permute-start | bytes 221192 | tf_op jit(solution)/shard_map/ppermute | solution.py:375
  89.4 7.5 %collective-permute-start.15 = (bf16[2,18432]{1,0:T(2,128)(2,1)S(1)}, bf16[2,18432]{1,0:T(2,128)(2,1)S(1)}, u32[]{:S(2)}, u32[]{:S(2)}) collective-permute-start(bf16[2,18432]{1,0:T(2,128)(2,1)S(1)} %get-tuple-element.28), channel_id=1, source_target_pairs={{0,14},{1,15},{2,12},{3,13},{4,10},{5,11},{6,8},{7,9},{8,6},{9,7},... | collective-permute-start | bytes 221192 | tf_op jit(solution)/shard_map/ppermute | solution.py:375

commit v4 on v3

--- a/solution.py
+++ b/solution.py
@@ -13,7 +13,6 @@
 NT = (((1,), (1,)), ((), ()))
 ANY = pl.BlockSpec(memory_space=pl.ANY)
 VMEM = pl.BlockSpec(memory_space=pltpu.VMEM)
-SMEM = pl.BlockSpec(memory_space=pltpu.SMEM)
 
 
 def params(mib):
@@ -45,41 +44,52 @@
 
 def layer_norm(tokens, norm_gain):
     return pl.pallas_call(
-        norm_kernel, out_shape=jax.ShapeDtypeStruct(tokens.shape, BF16)
+        norm_kernel,
+        out_shape=jax.ShapeDtypeStruct(tokens.shape, BF16),
+        compiler_params=params(4),
+        cost_estimate=pl.CostEstimate(
+            flops=25 * 10**9, bytes_accessed=75 * 10**6, transcendentals=0
+        ),
     )(tokens, norm_gain.reshape(1, -1))
 
 
-def attention_in_kernel(
-    chunks, groups, me_ref, even_ref, odd_ref, wq_ref, wk_ref, out_ref, rows_ref,
-    spread, rows, acc, q_sem, k_sem, rows_sem, *weights,
+def project_kernel(
+    chunks, even_ref, odd_ref, wq_ref, wg_ref, wu_ref, wk_ref, out_ref, hidden_ref,
+    spread, rows, acc, sem_u, sem_k, *streams,
 ):
     half, steps, width = even_ref.shape
     step = width // chunks
-    split = wq_ref.shape[0]
+    units = wu_ref.shape[0]
+    q_cols = wq_ref.shape[0]
 
     def cols(c):
         return pl.ds(c * step, step)
 
-    def place(c, which):
-        if groups == 2:
-            return weights[which].at[c]
-        return weights[0].at[c, pl.ds(which * split, (wq_ref, wk_ref)[which].shape[0])]
+    slots = streams[0].shape[0]
+
+    def keyval_place(c):
+        if len(streams) == 2:
+            return streams[1].at[c % slots]
+        return streams[0].at[c % slots, pl.ds(units, wk_ref.shape[0])]
+
+    def up_place(c):
+        if len(streams) == 2:
+            return streams[0].at[c % slots]
+        return streams[0].at[c % slots, pl.ds(0, units)]
 
     copies = [
         (
-            pltpu.make_async_copy(wq_ref.at[:, cols(c)], place(c, 0), q_sem.at[c]),
-            pltpu.make_async_copy(wk_ref.at[:, cols(c)], place(c, 1), k_sem.at[c]),
+            pltpu.make_async_copy(wu_ref.at[:, cols(c)], up_place(c), sem_u.at[c]),
+            pltpu.make_async_copy(wk_ref.at[:, cols(c)], keyval_place(c), sem_k.at[c]),
         )
         for c in range(chunks)
     ]
-    row_copies = [
-        pltpu.make_async_copy(rows.at[:, cols(c)], rows_ref.at[:, cols(c)], rows_sem.at[c])
-        for c in range(chunks)
-    ]
-    for pair in copies:
+    for pair in copies[:slots]:
         for copy in pair:
             copy.start()
     acc[...] = jnp.zeros_like(acc)
+    query = jnp.zeros((rows.shape[0], q_cols), F32)
+    gate = jnp.zeros((rows.shape[0], units), F32)
     for c in range(chunks):
         part = slice(c * step, (c + 1) * step)
         for p in range(half):
@@ -88,114 +98,73 @@
             spread[q * steps : (q + 1) * steps, :] = odd_ref[p, :, part].astype(F32)
         block = spread[...].astype(BF16)
         rows[:, part] = block
-        row_copies[c].start()
+        query += lax.dot_general(block, wq_ref[:, part], NT, preferred_element_type=F32)
+        gate += lax.dot_general(block, wg_ref[:, part], NT, preferred_element_type=F32)
+    for c in range(chunks):
         for copy in copies[c]:
             copy.wait()
         first = 0
-        for weight in weights:
-            last = first + weight.shape[1]
+        for stream in streams:
+            last = first + stream.shape[1]
             acc[:, first:last] += lax.dot_general(
-                block, weight[c], NT, preferred_element_type=F32
+                rows[:, c * step : (c + 1) * step], stream[c % slots], NT, preferred_element_type=F32
             )
             first = last
+        if c + slots < chunks:
+            for copy in copies[c + slots]:
+                copy.start()
+    me = lax.axis_index("gx")
     for p in range(2 * half):
-        owner = lax.bitwise_xor(me_ref[0], slot_at(p, half))
-        out_ref[owner] = acc[p * steps : (p + 1) * steps, :]
-    for copy in row_copies:
-        copy.wait()
-
-
-def attention_in(me, even, odd, w_query, w_keyval):
+        owner = lax.bitwise_xor(me, slot_at(p, half))
+        out_ref[owner, :, :q_cols] = query[p * steps : (p + 1) * steps]
+        out_ref[owner, :, q_cols:] = acc[p * steps : (p + 1) * steps, units:]
+    hidden_ref[...] = (jax.nn.silu(gate) * acc[:, :units]).astype(BF16)
+
+
+def project(even, odd, w_query, w_keyval, w_gate, w_up):
     half, steps, width = even.shape
     n = 2 * half * steps
     chunks = cuts(width)
     step = width // chunks
-    q_cols, k_cols = w_query.shape[0], w_keyval.shape[0]
-    groups = 1 if q_cols % 16 == 0 and k_cols % 16 == 0 else 2
-    sizes = [q_cols + k_cols] if groups == 1 else [q_cols, k_cols]
+    q_cols, k_cols, units = w_query.shape[0], w_keyval.shape[0], w_up.shape[0]
+    together = k_cols % 16 == 0 and units % 16 == 0
+    sizes = [units + k_cols] if together else [units, k_cols]
+    slots = min(chunks, 4)
+    taken = 2 * slots * step * (units + k_cols) + 6 * n * width + 4 * n * (step + 4 * units)
+    near = 2 * width * (q_cols + units)
+    taken += near if near < 8 << 20 else 0
     return pl.pallas_call(
-        functools.partial(attention_in_kernel, chunks, groups),
-        in_specs=[SMEM, VMEM, VMEM, ANY, ANY],
-        out_specs=[VMEM, ANY],
+        functools.partial(project_kernel, chunks),
+        in_specs=[VMEM, VMEM, VMEM, VMEM, ANY, ANY],
+        out_specs=[VMEM, VMEM],
         out_shape=[
             jax.ShapeDtypeStruct((2 * half, steps, q_cols + k_cols), F32),
-            jax.ShapeDtypeStruct((n, width), BF16),
+            jax.ShapeDtypeStruct((n, units), BF16),
         ],
         scratch_shapes=[
             pltpu.VMEM((n, step), F32),
             pltpu.VMEM((n, width), BF16),
-            pltpu.VMEM((n, q_cols + k_cols), F32),
-            pltpu.SemaphoreType.DMA((chunks,)),
+            pltpu.VMEM((n, units + k_cols), F32),
             pltpu.SemaphoreType.DMA((chunks,)),
             pltpu.SemaphoreType.DMA((chunks,)),
         ]
-        + [pltpu.VMEM((chunks, size, step), BF16) for size in sizes],
-        compiler_params=params(52),
-        cost_estimate=cost(n, w_query, w_keyval),
-    )(me, even, odd, w_query, w_keyval)
-
-
-def hidden_kernel(
-    chunks, rows_ref, wg_ref, wu_ref, out_ref, wg, wu, acc_g, acc_u, g_sem, u_sem
-):
-    step = rows_ref.shape[1] // chunks
+        + [pltpu.VMEM((slots, size, step), BF16) for size in sizes],
+        compiler_params=params((taken >> 20) + 3),
+        cost_estimate=cost(n, w_query, w_keyval, w_gate, w_up),
+    )(even, odd, w_query, w_gate, w_up, w_keyval)
+
+
+def down_kernel(chunks, offset, hidden_ref, w_ref, out_ref, w, out, w_sem, out_sem):
+    step = out_ref.shape[1] // chunks
 
     def cols(c):
         return pl.ds(c * step, step)
 
     copies = [
-        (
-            pltpu.make_async_copy(wg_ref.at[:, cols(c)], wg.at[c], g_sem.at[c]),
-            pltpu.make_async_copy(wu_ref.at[:, cols(c)], wu.at[c], u_sem.at[c]),
+        pltpu.make_async_copy(
+            w_ref.at[:, pl.ds(offset + c * step, step)], w.at[c], w_sem.at[c]
         )
         for c in range(chunks)
-    ]
-    for gate_copy, up_copy in copies:
-        gate_copy.start()
-        up_copy.start()
-    acc_g[...] = jnp.zeros_like(acc_g)
-    acc_u[...] = jnp.zeros_like(acc_u)
-    for c in range(chunks):
-        block = rows_ref[:, c * step : (c + 1) * step]
-        copies[c][0].wait()
-        acc_g[...] += lax.dot_general(block, wg[c], NT, preferred_element_type=F32)
-        copies[c][1].wait()
-        acc_u[...] += lax.dot_general(block, wu[c], NT, preferred_element_type=F32)
-    gate = acc_g[...]
-    out_ref[...] = (jax.nn.silu(gate) * acc_u[...]).astype(BF16)
-
-
-def hidden_units(rows, w_gate, w_up):
-    n, width = rows.shape
-    units = w_gate.shape[0]
-    chunks = cuts(width)
-    step = width // chunks
-    return pl.pallas_call(
-        functools.partial(hidden_kernel, chunks),
-        in_specs=[VMEM, ANY, ANY],
-        out_specs=VMEM,
-        out_shape=jax.ShapeDtypeStruct((n, units), BF16),
-        scratch_shapes=[
-            pltpu.VMEM((chunks, units, step), BF16),
-            pltpu.VMEM((chunks, units, step), BF16),
-            pltpu.VMEM((n, units), F32),
-            pltpu.VMEM((n, units), F32),
-            pltpu.SemaphoreType.DMA((chunks,)),
-            pltpu.SemaphoreType.DMA((chunks,)),
-        ],
-        compiler_params=params(56),
-        cost_estimate=cost(n, w_gate, w_up),
-    )(rows, w_gate, w_up)
-
-
-def down_kernel(chunks, hidden_ref, w_ref, out_ref, w, out, w_sem, out_sem):
-    step = w_ref.shape[1] // chunks
-
-    def cols(c):
-        return pl.ds(c * step, step)
-
-    copies = [
-        pltpu.make_async_copy(w_ref.at[:, cols(c)], w.at[c], w_sem.at[c]) for c in range(chunks)
     ]
     out_copies = [
         pltpu.make_async_copy(out.at[c], out_ref.at[:, cols(c)], out_sem.at[c])
@@ -211,13 +180,13 @@
         copy.wait()
 
 
-def down_part(hidden, w_down):
+def down_part(hidden, w_down, first, last):
     n, units = hidden.shape
-    width = w_down.shape[1]
-    chunks = cuts(width)
-    step = width // chunks
+    step = w_down.shape[1] // cuts(w_down.shape[1])
+    chunks = last - first
+    width = chunks * step
     return pl.pallas_call(
-        functools.partial(down_kernel, chunks),
+        functools.partial(down_kernel, chunks, first * step),
         in_specs=[VMEM, ANY],
         out_specs=ANY,
         out_shape=jax.ShapeDtypeStruct((n, width), F32),
@@ -228,25 +197,32 @@
             pltpu.SemaphoreType.DMA((chunks,)),
         ],
         compiler_params=params(40),
-        cost_estimate=cost(n, w_down),
+        cost_estimate=pl.CostEstimate(
+            flops=2 * n * units * width, bytes_accessed=2 * units * width, transcendentals=0
+        ),
     )(hidden, w_down)
 
 
 def branch_kernel(
-    chunks, me_ref, attended_ref, part_ref, w_ref, keep_ref, send_ref,
+    chunks, attended_ref, first_ref, second_ref, w_ref, keep_ref, send_ref,
     spread, w, part, keep, send, w_sem, part_sem, keep_sem, send_sem,
 ):
     slots, steps, _ = attended_ref.shape
     half = keep_ref.shape[0]
     step = w_ref.shape[1] // chunks
+    middle = first_ref.shape[1] // step
+    me = lax.axis_index("gx")
 
     def cols(c):
         return pl.ds(c * step, step)
+
+    def part_at(c):
+        return first_ref.at[:, cols(c)] if c < middle else second_ref.at[:, cols(c - middle)]
 
     copies = [
         (
             pltpu.make_async_copy(w_ref.at[:, cols(c)], w.at[c], w_sem.at[c]),
-            pltpu.make_async_copy(part_ref.at[:, cols(c)], part.at[c], part_sem.at[c]),
+            pltpu.make_async_copy(part_at(c), part.at[c], part_sem.at[c]),
         )
         for c in range(chunks)
     ]
@@ -261,7 +237,7 @@
         w_copy.start()
         part_copy.start()
     for p in range(slots):
-        owner = lax.bitwise_xor(me_ref[0], slot_at(p, slots // 2))
+        owner = lax.bitwise_xor(me, slot_at(p, slots // 2))
         spread[p * steps : (p + 1) * steps, :] = attended_ref[owner].astype(F32)
     attended = spread[...].astype(BF16)
     for c in range(chunks):
@@ -277,15 +253,15 @@
             copy.wait()
 
 
-def branch_parts(me, attended, part, w_out):
+def branch_parts(attended, first, second, w_out):
     slots, steps, features = attended.shape
-    n, width = part.shape
+    n, width = first.shape[0], w_out.shape[1]
     half = n // 2
     chunks = cuts(width)
     step = width // chunks
     return pl.pallas_call(
         functools.partial(branch_kernel, chunks),
-        in_specs=[SMEM, VMEM, ANY, ANY],
+        in_specs=[VMEM, ANY, ANY, ANY],
         out_specs=[ANY, ANY],
         out_shape=[
             jax.ShapeDtypeStruct((half, width), F32),
@@ -304,7 +280,7 @@
         ],
         compiler_params=params(40),
         cost_estimate=cost(n, w_out),
-    )(me, attended, part, w_out)
+    )(attended, first, second, w_out)
 
 
 def cut_kernel(keep_ref, came_ref, own_ref, *send_refs):
@@ -403,18 +379,17 @@
     query_cols = w_query.shape[0]
     devices = lax.axis_size("gx")
     batch = steps * rows
-    me = lax.axis_index("gx").astype(jnp.int32).reshape(1)
-
     own_tokens = tokens.reshape(batch, width)
     even, odd = gather_rows(layer_norm(own_tokens, norm_gain), devices)
-    projected, everyone = attention_in(me, even, odd, w_query, w_keyval)
-
+    projected, hidden = project(even, odd, w_query, w_keyval, w_gate, w_up)
+
+    chunks = cuts(width)
+    first = down_part(hidden, w_down, 0, chunks // 2)
     arrived = lax.all_to_all(projected, "gx", split_axis=0, concat_axis=0, tiled=True)
+    arrived, first = lax.optimization_barrier((arrived, first))
     arrived = arrived.reshape(devices, steps, rows, -1).transpose(2, 1, 0, 3)
     query = arrived[..., :query_cols].reshape(rows, steps, -1, head)
     keyval = arrived[..., query_cols:].reshape(rows, steps, 2 * head)
-    hidden = hidden_units(everyone, w_gate, w_up)
-
     angle_pos = (positions[:, None] + jnp.arange(steps)[None, :]).astype(F32)
     rotated = rotate(query, angle_pos[:, :, None]).astype(BF16)
     new_keys = rotate(keyval[..., :head], angle_pos).astype(BF16)
@@ -422,10 +397,11 @@
     attended = attend(rotated, new_keys, new_values, cache_keys, cache_values, lengths)
     attended = attended.reshape(rows, steps, devices, -1).transpose(2, 1, 0, 3)
     attended = attended.reshape(devices, batch, -1)
+    attended, hidden = lax.optimization_barrier((attended, hidden))
     attended = lax.all_to_all(attended, "gx", split_axis=0, concat_axis=0, tiled=True)
 
-    part = down_part(hidden, w_down)
-    keep, send = branch_parts(me, attended, part, w_out)
+    second = down_part(hidden, w_down, chunks // 2, chunks)
+    keep, send = branch_parts(attended, first, second, w_out)
     pieces = cut_parts(keep, swap(send, 1, devices), batch)
     branch = pieces[0]
     for place in range(1, devices // 2):

time: 98.3 us -> 93.6 us (0.952)
  Pallas kernels: 43.1 us -> 36.7 us
  waiting for transfers between devices: 14.8 us -> 17.8 us
  starting transfers between devices: 32.9 us -> 31 us
    pallas_call x4, Pallas kernels: 40.5 us -> 35.7 us  [the longest x1 20 us: project(): pl.pallas_call(functools.partial(project_kernel, chunks), in_specs=[VMEM,...]
    all_to_all x1, waiting for transfers between devices: 0.01 us -> 2.09 us  [local(): lax.all_to_all(projected, 'gx', split_axis=0, concat_axis=0, tiled=True)]
    all_to_all x1, starting transfers between devices: 6.01 us -> 3.93 us  [local(): lax.all_to_all(attended, 'gx', split_axis=0, concat_axis=0, tiled=True)]
    all_to_all x1, waiting for transfers between devices: 0.01 us -> 1.77 us  [local(): lax.all_to_all(attended, 'gx', split_axis=0, concat_axis=0, tiled=True)]
    pallas_call x1, Pallas kernels: 2.16 us -> 0.56 us  [layer_norm(): pl.pallas_call(norm_kernel, out_shape=jax.ShapeDtypeStruct(tokens.shape,...]
    unnamed x15 -> x33, local copies, waits for them, and re-layouts: 2.16 us -> 2.83 us
  transfers between devices with their start and end apart: 18 -> 18, of which waited for: 5 -> 9; matrix products, arithmetic and copies ran while one was open for 2% -> 1% of each run, Pallas kernels for 27% -> 10%
where the time goes in v4:
time: 93.6 us; the launch traced here: 93.2 us
  Pallas kernels  36.7 us (39%)
  starting transfers between devices  31 us (33%)
  waiting for transfers between devices  17.8 us (19%)
  local copies, waits for them, and re-layouts  3.68 us (4%)
  between operations  1.61 us (2%)
  other arithmetic  1.45 us (2%)
  matrix products  0.98 us (1%)
    ppermute x16, starting transfers between devices, swap(): return lax.ppermute(value, 'gx', [(i, i ^ bits) for i in range(devices)])  22.6 us
    pallas_call x1, Pallas kernels, project(): pl.pallas_call(functools.partial(project_kernel, chunks), in_specs=[VMEM,...  20 us
    ppermute x16, waiting for transfers between devices, swap(): return lax.ppermute(value, 'gx', [(i, i ^ bits) for i in range(devices)])  13.9 us
    pallas_call x2, Pallas kernels, down_part(): pl.pallas_call(functools.partial(down_kernel, chunks, first * step), in_s...  9.56 us
    pallas_call x1, Pallas kernels, branch_parts(): pl.pallas_call(functools.partial(branch_kernel, chunks), in_specs=[VMEM,...  6.15 us
    all_to_all x1, starting transfers between devices, local(): lax.all_to_all(projected, 'gx', split_axis=0, concat_axis=0, tiled=True)  4.47 us
    all_to_all x1, starting transfers between devices, local(): lax.all_to_all(attended, 'gx', split_axis=0, concat_axis=0, tiled=True)  3.93 us
    unnamed x33, local copies, waits for them, and re-layouts  2.83 us
  transfers between devices with their start and end apart: 18, of which 9 were waited for; matrix products, arithmetic and copies ran while one was open for 1% of the time, Pallas kernels for 10%

profile of v4, /device:TPU:0, one launch (start us, length us, event | category | flops | bytes accessed | tf_op | source)
XLA Modules:
  0.0 93.2 jit_solution(3389106645299795202)
XLA Ops:
  0.0 1.0 %copy-done.3 = bf16[2,1,18432]{2,0,1:T(2,128)(2,1)S(1)} copy-done((bf16[2,1,18432]{2,0,1:T(2,128)(2,1)S(1)}, bf16[2,1,18432]{2,0,1:T(2,128)(2,1)}, u32[]{:S(2)}) %copy-start.3) | copy-done | bytes 73752
  1.0 1.3 %copy-done.5 = f32[18432]{0:T(1024)S(1)} copy-done((f32[18432]{0:T(1024)S(1)}, f32[18432]{0:T(1024)}, u32[]{:S(2)}) %copy-start.5) | copy-done | bytes 73752
  2.4 0.0 slice-start.5
  2.4 0.6 shard_map.118
  2.9 5.1 %collective-permute-start.5 = (bf16[2,18432]{1,0:T(2,128)(2,1)S(1)}, bf16[2,18432]{1,0:T(2,128)(2,1)S(1)}, u32[]{:S(2)}, u32[]{:S(2)}) collective-permute-start(bf16[2,18432]{1,0:T(2,128)(2,1)S(1)} %shard_map.118), channel_id=1, source_target_pairs={{0,12},{1,13},{2,14},{3,15},{4,8},{5,9},{6,10},{7,11},{8,4},{9,5},... | collective-permute-start | bytes 221192 | tf_op jit(solution)/shard_map/ppermute | solution.py:351
  8.1 0.0 collective-permute-start.3
  8.1 0.6 collective-permute-start.1
  8.7 1.6 %collective-permute-start = (bf16[2,18432]{1,0:T(2,128)(2,1)S(1)}, bf16[2,18432]{1,0:T(2,128)(2,1)S(1)}, u32[]{:S(2)}, u32[]{:S(2)}) collective-permute-start(bf16[2,18432]{1,0:T(2,128)(2,1)S(1)} %shard_map.118), channel_id=1, source_target_pairs={{0,2},{1,3},{2,0},{3,1},{4,6},{5,7},{6,4},{7,5},{8,10},{9,11},{10,... | collective-permute-start | bytes 221192 | tf_op jit(solution)/shard_map/ppermute | solution.py:351
  10.3 0.1 bitcast_dynamic-update-slice_fusion.7
  10.4 0.4 collective-permute-done.5
  10.8 1.9 %collective-permute-start.6 = (bf16[2,18432]{1,0:T(2,128)(2,1)S(1)}, bf16[2,18432]{1,0:T(2,128)(2,1)S(1)}, u32[]{:S(2)}, u32[]{:S(2)}) collective-permute-start(bf16[2,18432]{1,0:T(2,128)(2,1)S(1)} %collective-permute-done.5), channel_id=1, source_target_pairs={{0,2},{1,3},{2,0},{3,1},{4,6},{5,7},{6,4},{7,5},{8,10},{9,11},{10,... | collective-permute-start | bytes 221192 | tf_op jit(solution)/shard_map/ppermute | solution.py:351
  12.7 1.6 %collective-permute-done.3 = bf16[2,18432]{1,0:T(2,128)(2,1)S(1)} collective-permute-done((bf16[2,18432]{1,0:T(2,128)(2,1)S(1)}, bf16[2,18432]{1,0:T(2,128)(2,1)S(1)}, u32[]{:S(2)}, u32[]{:S(2)}) %collective-permute-start.3) | collective-permute-done | bytes 73760 | tf_op jit(solution)/shard_map/ppermute | solution.py:351
  14.3 1.5 %collective-permute-start.4 = (bf16[2,18432]{1,0:T(2,128)(2,1)S(1)}, bf16[2,18432]{1,0:T(2,128)(2,1)S(1)}, u32[]{:S(2)}, u32[]{:S(2)}) collective-permute-start(bf16[2,18432]{1,0:T(2,128)(2,1)S(1)} %collective-permute-done.3), channel_id=1, source_target_pairs={{0,2},{1,3},{2,0},{3,1},{4,6},{5,7},{6,4},{7,5},{8,10},{9,11},{10,... | collective-permute-start | bytes 221192 | tf_op jit(solution)/shard_map/ppermute | solution.py:351
  15.8 0.0 collective-permute-done.1
  15.8 0.5 collective-permute-start.2
  16.3 0.0 collective-permute-done
  16.3 0.1 bitcast_dynamic-update-slice_fusion.6
  16.4 0.1 bitcast_dynamic-update-slice_fusion.5
  16.4 3.7 %collective-permute-done.2 = bf16[2,18432]{1,0:T(2,128)(2,1)S(1)} collective-permute-done((bf16[2,18432]{1,0:T(2,128)(2,1)S(1)}, bf16[2,18432]{1,0:T(2,128)(2,1)S(1)}, u32[]{:S(2)}, u32[]{:S(2)}) %collective-permute-start.2) | collective-permute-done | bytes 73760 | tf_op jit(solution)/shard_map/ppermute | solution.py:351
  20.1 0.1 bitcast_dynamic-update-slice_fusion.4
  20.2 0.1 bitcast_dynamic-update-slice_fusion.3
  20.3 0.0 collective-permute-done.4
  20.3 0.1 bitcast_dynamic-update-slice_fusion.2
  20.3 0.1 bitcast_dynamic-update-slice_fusion.1
  20.4 0.0 collective-permute-done.6
  20.4 0.1 bitcast_dynamic-update-slice_fusion.even_ref
  20.5 0.1 collective-permute-start.7
  21.9 0.1 multiply_cosine_fusion.1
  22.0 0.5 collective-permute-done.7.odd_ref
  22.6 20.0 %shard_map.119 = (f32[16,2,416]{2,1,0:T(2,128)}, bf16[32,576]{1,0:T(8,128)(2,1)S(1)}) custom-call(bf16[8,2,18432]{2,1,0:T(2,128)(2,1)S(1)} %bitcast_dynamic-update-slice_fusion.even_ref, bf16[8,2,18432]{2,1,0:T(2,128)(2,1)S(1)} %collective-permute-done.7.odd_ref, bf16[384,18432]{1,0:T(8,128)(2,1)S(1)} %copy-done.1, bf16[576,18432]{1,0:T(8,128)(2,1)S(1)} %bitcast.65, ...), custom_call_target="tpu_custom_call" | custom-call | flops 1849688064 | bytes 57802752 | tf_op jit(solution)/shard_map/pallas_call | solution.py:136
  42.7 0.0 copy-start.6
  42.7 4.5 %all-to-all-start = ((f32[16,2,416]{2,1,0:T(2,128)}), f32[16,2,416]{2,1,0:T(2,128)S(1)}, u32[]{:S(2)}, u32[]{:S(2)}) async-start(f32[16,2,416]{2,1,0:T(2,128)} %get-tuple-element.21), calls=%async_computation | async-start | bytes 131072 | tf_op jit(solution)/shard_map/all_to_all | solution.py:388
  47.2 4.8 %shard_map.120.first_ref = f32[32,9216]{1,0:T(8,128)S(1)} custom-call(bf16[32,576]{1,0:T(8,128)(2,1)S(1)} %get-tuple-element.26.hidden_ref, bf16[576,18432]{1,0:T(8,128)(2,1)} %w_ref.4), custom_call_target="tpu_custom_call" | custom-call | flops 339738624 | bytes 10616832 | tf_op jit(solution)/shard_map/pallas_call | solution.py:188
  51.9 2.1 %all-to-all-done = f32[16,2,416]{2,1,0:T(2,128)S(1)} async-done(((f32[16,2,416]{2,1,0:T(2,128)}), f32[16,2,416]{2,1,0:T(2,128)S(1)}, u32[]{:S(2)}, u32[]{:S(2)}) %all-to-all-start) | async-done | bytes 53280 | tf_op jit(solution)/shard_map/all_to_all | solution.py:388
  54.1 0.1 reshape.338
  54.2 0.1 fusion.27
  54.3 0.4 fusion.31
  54.7 0.2 fusion.32
  54.9 0.2 fusion.6
  55.1 0.3 fusion.3
  55.4 0.2 fusion.1
  55.6 0.6 copy.17
  56.2 3.9 %all-to-all-start.1 = ((bf16[16,2,384]{2,1,0:T(2,128)(2,1)}), bf16[16,2,384]{2,1,0:T(2,128)(2,1)S(1)}, u32[]{:S(2)}, u32[]{:S(2)}) async-start(bf16[16,2,384]{2,1,0:T(2,128)(2,1)} %bitcast.61), calls=%async_computation.1 | async-start | bytes 49152 | tf_op jit(solution)/shard_map/all_to_all | solution.py:401
  60.2 4.8 %shard_map.121.second_ref = f32[32,9216]{1,0:T(8,128)S(1)} custom-call(bf16[32,576]{1,0:T(8,128)(2,1)S(1)} %get-tuple-element.26.hidden_ref, bf16[576,18432]{1,0:T(8,128)(2,1)} %w_ref.4), custom_call_target="tpu_custom_call" | custom-call | flops 339738624 | bytes 10616832 | tf_op jit(solution)/shard_map/pallas_call | solution.py:188
  64.9 0.0 copy-start.4
  65.0 1.8 %all-to-all-done.1.attended_ref = bf16[16,2,384]{2,1,0:T(2,128)(2,1)S(1)} async-done(((bf16[16,2,384]{2,1,0:T(2,128)(2,1)}), bf16[16,2,384]{2,1,0:T(2,128)(2,1)S(1)}, u32[]{:S(2)}, u32[]{:S(2)}) %all-to-all-start.1) | async-done | bytes 24608 | tf_op jit(solution)/shard_map/all_to_all | solution.py:401
  66.7 6.2 %shard_map.122 = (f32[16,18432]{1,0:T(8,128)S(1)}, bf16[16,18432]{1,0:T(8,128)(2,1)S(1)}) custom-call(bf16[16,2,384]{2,1,0:T(2,128)(2,1)S(1)} %all-to-all-done.1.attended_ref, f32[32,9216]{1,0:T(8,128)S(1)} %shard_map.120.first_ref, f32[32,9216]{1,0:T(8,128)S(1)} %shard_map.121.second_ref, bf16[384,18432]{1,0:T(8,128)(2,1)} %w_ref.5), custom_call_target="tpu_custom_call" | custom-call | flops 452984832 | bytes 14155776 | tf_op jit(solution)/shard_map/pallas_call | solution.py:262
  72.9 0.1 collective-permute-start.8
  73.0 2.0 %collective-permute-done.8.came_ref = bf16[16,18432]{1,0:T(8,128)(2,1)S(1)} collective-permute-done((bf16[16,18432]{1,0:T(8,128)(2,1)S(1)}, bf16[16,18432]{1,0:T(8,128)(2,1)S(1)}, u32[]{:S(2)}, u32[]{:S(2)}) %collective-permute-start.8) | collective-permute-done | bytes 589856 | tf_op jit(solution)/shard_map/ppermute | solution.py:351
  75.0 0.4 shard_map.123
  75.4 0.5 collective-permute-start.9
  75.8 1.3 %collective-permute-start.10 = (bf16[2,18432]{1,0:T(2,128)(2,1)S(1)}, bf16[2,18432]{1,0:T(2,128)(2,1)S(1)}, u32[]{:S(2)}, u32[]{:S(2)}) collective-permute-start(bf16[2,18432]{1,0:T(2,128)(2,1)S(1)} %get-tuple-element.31), channel_id=1, source_target_pairs={{0,4},{1,5},{2,6},{3,7},{4,0},{5,1},{6,2},{7,3},{8,12},{9,13},{10,... | collective-permute-start | bytes 221192 | tf_op jit(solution)/shard_map/ppermute | solution.py:351
  77.1 1.8 %collective-permute-start.11 = (bf16[2,18432]{1,0:T(2,128)(2,1)S(1)}, bf16[2,18432]{1,0:T(2,128)(2,1)S(1)}, u32[]{:S(2)}, u32[]{:S(2)}) collective-permute-start(bf16[2,18432]{1,0:T(2,128)(2,1)S(1)} %get-tuple-element.32), channel_id=1, source_target_pairs={{0,6},{1,7},{2,4},{3,5},{4,2},{5,3},{6,0},{7,1},{8,14},{9,15},{10,... | collective-permute-start | bytes 221192 | tf_op jit(solution)/shard_map/ppermute | solution.py:351
  78.9 1.1 %collective-permute-start.12 = (bf16[2,18432]{1,0:T(2,128)(2,1)S(1)}, bf16[2,18432]{1,0:T(2,128)(2,1)S(1)}, u32[]{:S(2)}, u32[]{:S(2)}) collective-permute-start(bf16[2,18432]{1,0:T(2,128)(2,1)S(1)} %get-tuple-element.33), channel_id=1, source_target_pairs={{0,8},{1,9},{2,10},{3,11},{4,12},{5,13},{6,14},{7,15},{8,0},{9,1},... | collective-permute-start | bytes 221192 | tf_op jit(solution)/shard_map/ppermute | solution.py:351
  80.0 1.7 %collective-permute-start.13 = (bf16[2,18432]{1,0:T(2,128)(2,1)S(1)}, bf16[2,18432]{1,0:T(2,128)(2,1)S(1)}, u32[]{:S(2)}, u32[]{:S(2)}) collective-permute-start(bf16[2,18432]{1,0:T(2,128)(2,1)S(1)} %get-tuple-element.34), channel_id=1, source_target_pairs={{0,10},{1,11},{2,8},{3,9},{4,14},{5,15},{6,12},{7,13},{8,2},{9,3},... | collective-permute-start | bytes 221192 | tf_op jit(solution)/shard_map/ppermute | solution.py:351
  81.7 0.0 collective-permute-done.9
  81.7 3.1 %collective-permute-start.14 = (bf16[2,18432]{1,0:T(2,128)(2,1)S(1)}, bf16[2,18432]{1,0:T(2,128)(2,1)S(1)}, u32[]{:S(2)}, u32[]{:S(2)}) collective-permute-start(bf16[2,18432]{1,0:T(2,128)(2,1)S(1)} %get-tuple-element.35), channel_id=1, source_target_pairs={{0,12},{1,13},{2,14},{3,15},{4,8},{5,9},{6,10},{7,11},{8,4},{9,5},... | collective-permute-start | bytes 221192 | tf_op jit(solution)/shard_map/ppermute | solution.py:351
  84.7 0.0 collective-permute-done.10
  84.8 1.8 %collective-permute-start.15 = (bf16[2,18432]{1,0:T(2,128)(2,1)S(1)}, bf16[2,18432]{1,0:T(2,128)(2,1)S(1)}, u32[]{:S(2)}, u32[]{:S(2)}) collective-permute-start(bf16[2,18432]{1,0:T(2,128)(2,1)S(1)} %get-tuple-element.36), channel_id=1, source_target_pairs={{0,14},{1,15},{2,12},{3,13},{4,10},{5,11},{6,8},{7,9},{8,6},{9,7},... | collective-permute-start | bytes 221192 | tf_op jit(solution)/shard_map/ppermute | solution.py:351
  86.6 0.0 collective-permute-done.11
  86.6 3.5 %collective-permute-done.12 = bf16[2,18432]{1,0:T(2,128)(2,1)S(1)} collective-permute-done((bf16[2,18432]{1,0:T(2,128)(2,1)S(1)}, bf16[2,18432]{1,0:T(2,128)(2,1)S(1)}, u32[]{:S(2)}, u32[]{:S(2)}) %collective-permute-start.12) | collective-permute-done | bytes 73760 | tf_op jit(solution)/shard_map/ppermute | solution.py:351
  90.1 2.1 %collective-permute-done.13 = bf16[2,18432]{1,0:T(2,128)(2,1)S(1)} collective-permute-done((bf16[2,18432]{1,0:T(2,128)(2,1)S(1)}, bf16[2,18432]{1,0:T(2,128)(2,1)S(1)}, u32[]{:S(2)}, u32[]{:S(2)}) %collective-permute-start.13) | collective-permute-done | bytes 73760 | tf_op jit(solution)/shard_map/ppermute | solution.py:351
  92.2 0.0 collective-permute-done.14
  92.2 1.0 %fusion.9 = bf16[2,1,18432]{2,0,1:T(2,128)(2,1)} fusion(bf16[2,18432]{1,0:T(2,128)(2,1)S(1)} %collective-permute-done.15, bf16[2,18432]{1,0:T(2,128)(2,1)S(1)} %collective-permute-done.14, bf16[2,18432]{1,0:T(2,128)(2,1)S(1)} %collective-permute-done.13, bf16[2,18432]{1,0:T(2,128)(2,1)S(1)} %collective-permute-done.12, ...), kind=kLoop, calls=%fused_computation.23 | loop fusion | flops 626688 | bytes 811008 | tf_op jit(solution)/shard_map/reshape | solution.py:410
  (37 shorter events, 0.2 us)
Async XLA Ops:
  0.0 54.3 %copy-start = (bf16[1,1024,256]{2,1,0:T(8,128)(2,1)S(1)}, bf16[1,1024,256]{2,1,0:T(8,128)(2,1)}, u32[]{:S(2)}) copy-start(bf16[1,1024,256]{2,1,0:T(8,128)(2,1)} %param.20) | copy-start | bytes 1572868
  0.0 22.5 %slice-start = ((s8[21233664]{0:T(1024)(128)(4,1)}), s8[4194304]{0:T(1024)(128)(4,1)S(1)}, s32[]{:S(2)}) async-start(s8[21233664]{0:T(1024)(128)(4,1)} %bitcast.64), calls=%async_computation.2 | async-start | bytes 8388608
  0.0 1.0 %copy-start.3 = (bf16[2,1,18432]{2,0,1:T(2,128)(2,1)S(1)}, bf16[2,1,18432]{2,0,1:T(2,128)(2,1)}, u32[]{:S(2)}) copy-start(bf16[2,1,18432]{2,0,1:T(2,128)(2,1)} %param.12) | copy-start | bytes 221188
  1.0 1.3 %copy-start.5 = (f32[18432]{0:T(1024)S(1)}, f32[18432]{0:T(1024)}, u32[]{:S(2)}) copy-start(f32[18432]{0:T(1024)} %param.13) | copy-start | bytes 221188
  2.3 20.2 %slice-start.1 = ((s8[21233664]{0:T(1024)(128)(4,1)}), s8[4194304]{0:T(1024)(128)(4,1)S(1)}, s32[]{:S(2)}) async-start(s8[21233664]{0:T(1024)(128)(4,1)} %bitcast.64), calls=%async_computation.3 | async-start | bytes 8388608
  2.3 20.2 %slice-start.2 = ((s8[21233664]{0:T(1024)(128)(4,1)}), s8[4194304]{0:T(1024)(128)(4,1)S(1)}, s32[]{:S(2)}) async-start(s8[21233664]{0:T(1024)(128)(4,1)} %bitcast.64), calls=%async_computation.4 | async-start | bytes 8388608
  2.3 20.2 %slice-start.3 = ((s8[21233664]{0:T(1024)(128)(4,1)}), s8[4194304]{0:T(1024)(128)(4,1)S(1)}, s32[]{:S(2)}) async-start(s8[21233664]{0:T(1024)(128)(4,1)} %bitcast.64), calls=%async_computation.5 | async-start | bytes 8388608
  2.3 20.2 %slice-start.4 = ((s8[21233664]{0:T(1024)(128)(4,1)}), s8[4194304]{0:T(1024)(128)(4,1)S(1)}, s32[]{:S(2)}) async-start(s8[21233664]{0:T(1024)(128)(4,1)} %bitcast.64), calls=%async_computation.6 | async-start | bytes 8388608
  2.4 20.2 %slice-start.5 = ((s8[21233664]{0:T(1024)(128)(4,1)}), s8[262144]{0:T(1024)(128)(4,1)S(1)}, s32[]{:S(2)}) async-start(s8[21233664]{0:T(1024)(128)(4,1)} %bitcast.64), calls=%async_computation.7 | async-start | bytes 524288
  2.4 20.2 %copy-start.1 = (bf16[384,18432]{1,0:T(8,128)(2,1)S(1)}, bf16[384,18432]{1,0:T(8,128)(2,1)}, u32[]{:S(2)}) copy-start(bf16[384,18432]{1,0:T(8,128)(2,1)} %wq_ref.1) | copy-start | bytes 42467332
  2.4 20.2 %copy-start.2 = (bf16[32,18432]{1,0:T(8,128)(2,1)S(1)}, bf16[32,18432]{1,0:T(8,128)(2,1)}, u32[]{:S(2)}) copy-start(bf16[32,18432]{1,0:T(8,128)(2,1)} %wk_ref.1) | copy-start | bytes 3538948
  2.9 7.9 %collective-permute-start.5 = (bf16[2,18432]{1,0:T(2,128)(2,1)S(1)}, bf16[2,18432]{1,0:T(2,128)(2,1)S(1)}, u32[]{:S(2)}, u32[]{:S(2)}) collective-permute-start(bf16[2,18432]{1,0:T(2,128)(2,1)S(1)} %shard_map.118), channel_id=1, source_target_pairs={{0,12},{1,13},{2,14},{3,15},{4,8},{5,9},{6,10},{7,11},{8,4},{9,5},... | collective-permute-start | bytes 221192 | tf_op jit(solution)/shard_map/ppermute | solution.py:351
  8.1 6.2 %collective-permute-start.3 = (bf16[2,18432]{1,0:T(2,128)(2,1)S(1)}, bf16[2,18432]{1,0:T(2,128)(2,1)S(1)}, u32[]{:S(2)}, u32[]{:S(2)}) collective-permute-start(bf16[2,18432]{1,0:T(2,128)(2,1)S(1)} %shard_map.118), channel_id=1, source_target_pairs={{0,8},{1,9},{2,10},{3,11},{4,12},{5,13},{6,14},{7,15},{8,0},{9,1},... | collective-permute-start | bytes 221192 | tf_op jit(solution)/shard_map/ppermute | solution.py:351
  8.1 7.7 %collective-permute-start.1 = (bf16[2,18432]{1,0:T(2,128)(2,1)S(1)}, bf16[2,18432]{1,0:T(2,128)(2,1)S(1)}, u32[]{:S(2)}, u32[]{:S(2)}) collective-permute-start(bf16[2,18432]{1,0:T(2,128)(2,1)S(1)} %shard_map.118), channel_id=1, source_target_pairs={{0,4},{1,5},{2,6},{3,7},{4,0},{5,1},{6,2},{7,3},{8,12},{9,13},{10,... | collective-permute-start | bytes 221192 | tf_op jit(solution)/shard_map/ppermute | solution.py:351
  8.7 7.6 %collective-permute-start = (bf16[2,18432]{1,0:T(2,128)(2,1)S(1)}, bf16[2,18432]{1,0:T(2,128)(2,1)S(1)}, u32[]{:S(2)}, u32[]{:S(2)}) collective-permute-start(bf16[2,18432]{1,0:T(2,128)(2,1)S(1)} %shard_map.118), channel_id=1, source_target_pairs={{0,2},{1,3},{2,0},{3,1},{4,6},{5,7},{6,4},{7,5},{8,10},{9,11},{10,... | collective-permute-start | bytes 221192 | tf_op jit(solution)/shard_map/ppermute | solution.py:351
  10.8 9.6 %collective-permute-start.6 = (bf16[2,18432]{1,0:T(2,128)(2,1)S(1)}, bf16[2,18432]{1,0:T(2,128)(2,1)S(1)}, u32[]{:S(2)}, u32[]{:S(2)}) collective-permute-start(bf16[2,18432]{1,0:T(2,128)(2,1)S(1)} %collective-permute-done.5), channel_id=1, source_target_pairs={{0,2},{1,3},{2,0},{3,1},{4,6},{5,7},{6,4},{7,5},{8,10},{9,11},{10,... | collective-permute-start | bytes 221192 | tf_op jit(solution)/shard_map/ppermute | solution.py:351
  14.3 6.0 %collective-permute-start.4 = (bf16[2,18432]{1,0:T(2,128)(2,1)S(1)}, bf16[2,18432]{1,0:T(2,128)(2,1)S(1)}, u32[]{:S(2)}, u32[]{:S(2)}) collective-permute-start(bf16[2,18432]{1,0:T(2,128)(2,1)S(1)} %collective-permute-done.3), channel_id=1, source_target_pairs={{0,2},{1,3},{2,0},{3,1},{4,6},{5,7},{6,4},{7,5},{8,10},{9,11},{10,... | collective-permute-start | bytes 221192 | tf_op jit(solution)/shard_map/ppermute | solution.py:351
  15.8 4.4 %collective-permute-start.2 = (bf16[2,18432]{1,0:T(2,128)(2,1)S(1)}, bf16[2,18432]{1,0:T(2,128)(2,1)S(1)}, u32[]{:S(2)}, u32[]{:S(2)}) collective-permute-start(bf16[2,18432]{1,0:T(2,128)(2,1)S(1)} %collective-permute-done.1), channel_id=1, source_target_pairs={{0,2},{1,3},{2,0},{3,1},{4,6},{5,7},{6,4},{7,5},{8,10},{9,11},{10,... | collective-permute-start | bytes 221192 | tf_op jit(solution)/shard_map/ppermute | solution.py:351
  20.5 2.1 %collective-permute-start.7 = (bf16[8,2,18432]{2,1,0:T(2,128)(2,1)S(1)}, bf16[8,2,18432]{2,1,0:T(2,128)(2,1)S(1)}, u32[]{:S(2)}, u32[]{:S(2)}) collective-permute-start(bf16[8,2,18432]{2,1,0:T(2,128)(2,1)S(1)} %bitcast_dynamic-update-slice_fusion.even_ref), channel_id=1, source_target_pairs={{0,1},{1,0},{2,3},{3,2},{4,5},{5,4},{6,7},{7,6},{8,9},{9,8},{10,11... | collective-permute-start | bytes 1769480 | tf_op jit(solution)/shard_map/ppermute | solution.py:351
  42.7 12.4 %copy-start.6 = (bf16[1,1024,256]{2,1,0:T(8,128)(2,1)S(1)}, bf16[1,1024,256]{2,1,0:T(8,128)(2,1)}, u32[]{:S(2)}) copy-start(bf16[1,1024,256]{2,1,0:T(8,128)(2,1)} %param.21) | copy-start | bytes 1572868
  42.7 11.4 %all-to-all-start = ((f32[16,2,416]{2,1,0:T(2,128)}), f32[16,2,416]{2,1,0:T(2,128)S(1)}, u32[]{:S(2)}, u32[]{:S(2)}) async-start(f32[16,2,416]{2,1,0:T(2,128)} %get-tuple-element.21), calls=%async_computation | async-start | bytes 131072 | tf_op jit(solution)/shard_map/all_to_all | solution.py:388
  56.2 10.5 %all-to-all-start.1 = ((bf16[16,2,384]{2,1,0:T(2,128)(2,1)}), bf16[16,2,384]{2,1,0:T(2,128)(2,1)S(1)}, u32[]{:S(2)}, u32[]{:S(2)}) async-start(bf16[16,2,384]{2,1,0:T(2,128)(2,1)} %bitcast.61), calls=%async_computation.1 | async-start | bytes 49152 | tf_op jit(solution)/shard_map/all_to_all | solution.py:401
  64.9 27.3 %copy-start.4 = (bf16[2,1,18432]{2,0,1:T(2,128)(2,1)S(1)}, bf16[2,1,18432]{2,0,1:T(2,128)(2,1)}, u32[]{:S(2)}) copy-start(bf16[2,1,18432]{2,0,1:T(2,128)(2,1)} %param.12) | copy-start | bytes 221188
  72.9 2.1 %collective-permute-start.8 = (bf16[16,18432]{1,0:T(8,128)(2,1)S(1)}, bf16[16,18432]{1,0:T(8,128)(2,1)S(1)}, u32[]{:S(2)}, u32[]{:S(2)}) collective-permute-start(bf16[16,18432]{1,0:T(8,128)(2,1)S(1)} %get-tuple-element.28), channel_id=1, source_target_pairs={{0,1},{1,0},{2,3},{3,2},{4,5},{5,4},{6,7},{7,6},{8,9},{9,8},{10,11... | collective-permute-start | bytes 1769480 | tf_op jit(solution)/shard_map/ppermute | solution.py:351
  75.4 6.3 %collective-permute-start.9 = (bf16[2,18432]{1,0:T(2,128)(2,1)S(1)}, bf16[2,18432]{1,0:T(2,128)(2,1)S(1)}, u32[]{:S(2)}, u32[]{:S(2)}) collective-permute-start(bf16[2,18432]{1,0:T(2,128)(2,1)S(1)} %get-tuple-element.30), channel_id=1, source_target_pairs={{0,2},{1,3},{2,0},{3,1},{4,6},{5,7},{6,4},{7,5},{8,10},{9,11},{10,... | collective-permute-start | bytes 221192 | tf_op jit(solution)/shard_map/ppermute | solution.py:351
  75.8 8.9 %collective-permute-start.10 = (bf16[2,18432]{1,0:T(2,128)(2,1)S(1)}, bf16[2,18432]{1,0:T(2,128)(2,1)S(1)}, u32[]{:S(2)}, u32[]{:S(2)}) collective-permute-start(bf16[2,18432]{1,0:T(2,128)(2,1)S(1)} %get-tuple-element.31), channel_id=1, source_target_pairs={{0,4},{1,5},{2,6},{3,7},{4,0},{5,1},{6,2},{7,3},{8,12},{9,13},{10,... | collective-permute-start | bytes 221192 | tf_op jit(solution)/shard_map/ppermute | solution.py:351
  77.1 9.5 %collective-permute-start.11 = (bf16[2,18432]{1,0:T(2,128)(2,1)S(1)}, bf16[2,18432]{1,0:T(2,128)(2,1)S(1)}, u32[]{:S(2)}, u32[]{:S(2)}) collective-permute-start(bf16[2,18432]{1,0:T(2,128)(2,1)S(1)} %get-tuple-element.32), channel_id=1, source_target_pairs={{0,6},{1,7},{2,4},{3,5},{4,2},{5,3},{6,0},{7,1},{8,14},{9,15},{10,... | collective-permute-start | bytes 221192 | tf_op jit(solution)/shard_map/ppermute | solution.py:351
  78.9 11.2 %collective-permute-start.12 = (bf16[2,18432]{1,0:T(2,128)(2,1)S(1)}, bf16[2,18432]{1,0:T(2,128)(2,1)S(1)}, u32[]{:S(2)}, u32[]{:S(2)}) collective-permute-start(bf16[2,18432]{1,0:T(2,128)(2,1)S(1)} %get-tuple-element.33), channel_id=1, source_target_pairs={{0,8},{1,9},{2,10},{3,11},{4,12},{5,13},{6,14},{7,15},{8,0},{9,1},... | collective-permute-start | bytes 221192 | tf_op jit(solution)/shard_map/ppermute | solution.py:351
  80.0 12.2 %collective-permute-start.13 = (bf16[2,18432]{1,0:T(2,128)(2,1)S(1)}, bf16[2,18432]{1,0:T(2,128)(2,1)S(1)}, u32[]{:S(2)}, u32[]{:S(2)}) collective-permute-start(bf16[2,18432]{1,0:T(2,128)(2,1)S(1)} %get-tuple-element.34), channel_id=1, source_target_pairs={{0,10},{1,11},{2,8},{3,9},{4,14},{5,15},{6,12},{7,13},{8,2},{9,3},... | collective-permute-start | bytes 221192 | tf_op jit(solution)/shard_map/ppermute | solution.py:351
  81.7 10.5 %collective-permute-start.14 = (bf16[2,18432]{1,0:T(2,128)(2,1)S(1)}, bf16[2,18432]{1,0:T(2,128)(2,1)S(1)}, u32[]{:S(2)}, u32[]{:S(2)}) collective-permute-start(bf16[2,18432]{1,0:T(2,128)(2,1)S(1)} %get-tuple-element.35), channel_id=1, source_target_pairs={{0,12},{1,13},{2,14},{3,15},{4,8},{5,9},{6,10},{7,11},{8,4},{9,5},... | collective-permute-start | bytes 221192 | tf_op jit(solution)/shard_map/ppermute | solution.py:351
  84.8 7.5 %collective-permute-start.15 = (bf16[2,18432]{1,0:T(2,128)(2,1)S(1)}, bf16[2,18432]{1,0:T(2,128)(2,1)S(1)}, u32[]{:S(2)}, u32[]{:S(2)}) collective-permute-start(bf16[2,18432]{1,0:T(2,128)(2,1)S(1)} %get-tuple-element.36), channel_id=1, source_target_pairs={{0,14},{1,15},{2,12},{3,13},{4,10},{5,11},{6,8},{7,9},{8,6},{9,7},... | collective-permute-start | bytes 221192 | tf_op jit(solution)/shard_map/ppermute | solution.py:351

commit v5 on v4

--- a/solution.py
+++ b/solution.py
@@ -35,27 +35,36 @@
     return 1
 
 
-def norm_kernel(tokens_ref, gain_ref, out_ref):
+def center_kernel(tokens_ref, out_ref):
     values = tokens_ref[...].astype(F32)
     centered = values - jnp.mean(values, axis=-1, keepdims=True)
     spread = jnp.mean(centered * centered, axis=-1, keepdims=True)
-    out_ref[...] = (centered / jnp.sqrt(spread + 1e-05) * gain_ref[...]).astype(BF16)
+    out_ref[...] = centered / jnp.sqrt(spread + 1e-05)
+
+
+def gain_kernel(values_ref, gain_ref, out_ref):
+    out_ref[...] = (values_ref[...] * gain_ref[...]).astype(BF16)
 
 
 def layer_norm(tokens, norm_gain):
-    return pl.pallas_call(
-        norm_kernel,
-        out_shape=jax.ShapeDtypeStruct(tokens.shape, BF16),
+    centered = pl.pallas_call(
+        center_kernel,
+        out_shape=jax.ShapeDtypeStruct(tokens.shape, F32),
         compiler_params=params(4),
         cost_estimate=pl.CostEstimate(
             flops=25 * 10**9, bytes_accessed=75 * 10**6, transcendentals=0
         ),
-    )(tokens, norm_gain.reshape(1, -1))
+    )(tokens)
+    return pl.pallas_call(
+        gain_kernel,
+        out_shape=jax.ShapeDtypeStruct(tokens.shape, BF16),
+        compiler_params=params(4),
+    )(centered, norm_gain.reshape(1, -1))
 
 
 def project_kernel(
     chunks, even_ref, odd_ref, wq_ref, wg_ref, wu_ref, wk_ref, out_ref, hidden_ref,
-    spread, rows, acc, sem_u, sem_k, *streams,
+    rows, acc, sem_u, sem_k, *streams,
 ):
     half, steps, width = even_ref.shape
     step = width // chunks
@@ -93,11 +102,10 @@
     for c in range(chunks):
         part = slice(c * step, (c + 1) * step)
         for p in range(half):
-            spread[p * steps : (p + 1) * steps, :] = even_ref[p, :, part].astype(F32)
+            rows[p * steps : (p + 1) * steps, part] = even_ref[p, :, part]
             q = half + p
-            spread[q * steps : (q + 1) * steps, :] = odd_ref[p, :, part].astype(F32)
-        block = spread[...].astype(BF16)
-        rows[:, part] = block
+            rows[q * steps : (q + 1) * steps, part] = odd_ref[p, :, part]
+        block = rows[:, part]
         query += lax.dot_general(block, wq_ref[:, part], NT, preferred_element_type=F32)
         gate += lax.dot_general(block, wg_ref[:, part], NT, preferred_element_type=F32)
     for c in range(chunks):
@@ -142,7 +150,6 @@
             jax.ShapeDtypeStruct((n, units), BF16),
         ],
         scratch_shapes=[
-            pltpu.VMEM((n, step), F32),
             pltpu.VMEM((n, width), BF16),
             pltpu.VMEM((n, units + k_cols), F32),
             pltpu.SemaphoreType.DMA((chunks,)),
@@ -404,7 +411,7 @@
     keep, send = branch_parts(attended, first, second, w_out)
     pieces = cut_parts(keep, swap(send, 1, devices), batch)
     branch = pieces[0]
-    for place in range(1, devices // 2):
+    for place in reversed(range(1, devices // 2)):
         branch = branch + swap(pieces[place], 2 * place, devices).astype(F32)
     result = (own_tokens.astype(F32) + branch).astype(BF16)
     return result.reshape(tokens.shape)

time: 93.6 us -> 92.6 us (0.989)
  transfers between devices with their start and end apart: 18 -> 18, of which waited for: 9 -> 10; matrix products, arithmetic and copies ran while one was open for 1% -> 1% of each run, Pallas kernels for 10% -> 10%
where the time goes in v5:
time: 92.6 us; the launch traced here: 92.3 us
  Pallas kernels  36.4 us (39%)
  starting transfers between devices  31.7 us (34%)
  waiting for transfers between devices  17 us (18%)
  local copies, waits for them, and re-layouts  3.13 us (3%)
  between operations  1.62 us (2%)
  other arithmetic  1.45 us (2%)
  matrix products  0.98 us (1%)
    ppermute x16, starting transfers between devices, swap(): return lax.ppermute(value, 'gx', [(i, i ^ bits) for i in range(devices)])  23.3 us
    pallas_call x1, Pallas kernels, project(): pl.pallas_call(functools.partial(project_kernel, chunks), in_specs=[VMEM,...  19.7 us
    ppermute x16, waiting for transfers between devices, swap(): return lax.ppermute(value, 'gx', [(i, i ^ bits) for i in range(devices)])  13.2 us
    pallas_call x2, Pallas kernels, down_part(): pl.pallas_call(functools.partial(down_kernel, chunks, first * step), in_s...  9.56 us
    pallas_call x1, Pallas kernels, branch_parts(): pl.pallas_call(functools.partial(branch_kernel, chunks), in_specs=[VMEM,...  6.15 us
    all_to_all x1, starting transfers between devices, local(): lax.all_to_all(projected, 'gx', split_axis=0, concat_axis=0, tiled=True)  4.47 us
    all_to_all x1, starting transfers between devices, local(): lax.all_to_all(attended, 'gx', split_axis=0, concat_axis=0, tiled=True)  3.93 us
    unnamed x33, local copies, waits for them, and re-layouts  2.28 us
  transfers between devices with their start and end apart: 18, of which 10 were waited for; matrix products, arithmetic and copies ran while one was open for 1% of the time, Pallas kernels for 10%

profile of v5, /device:TPU:0, one launch (start us, length us, event | category | flops | bytes accessed | tf_op | source)
XLA Modules:
  0.0 92.3 jit_solution(14636522799867578254)
XLA Ops:
  0.0 1.0 %copy-done.3 = bf16[2,1,18432]{2,0,1:T(2,128)(2,1)S(1)} copy-done((bf16[2,1,18432]{2,0,1:T(2,128)(2,1)S(1)}, bf16[2,1,18432]{2,0,1:T(2,128)(2,1)}, u32[]{:S(2)}) %copy-start.3) | copy-done | bytes 73752
  1.1 0.0 slice-start.4
  1.1 0.0 slice-start.5
  1.1 0.5 shard_map.118.values_ref
  1.6 0.8 copy-done.5
  2.3 0.1 shard_map.119
  2.4 5.1 %collective-permute-start.5 = (bf16[2,18432]{1,0:T(2,128)(2,1)S(1)}, bf16[2,18432]{1,0:T(2,128)(2,1)S(1)}, u32[]{:S(2)}, u32[]{:S(2)}) collective-permute-start(bf16[2,18432]{1,0:T(2,128)(2,1)S(1)} %shard_map.119), channel_id=1, source_target_pairs={{0,12},{1,13},{2,14},{3,15},{4,8},{5,9},{6,10},{7,11},{8,4},{9,5},... | collective-permute-start | bytes 221192 | tf_op jit(solution)/shard_map/ppermute | solution.py:358
  7.5 0.0 collective-permute-start.3
  7.6 0.6 collective-permute-start.1
  8.2 1.6 %collective-permute-start = (bf16[2,18432]{1,0:T(2,128)(2,1)S(1)}, bf16[2,18432]{1,0:T(2,128)(2,1)S(1)}, u32[]{:S(2)}, u32[]{:S(2)}) collective-permute-start(bf16[2,18432]{1,0:T(2,128)(2,1)S(1)} %shard_map.119), channel_id=1, source_target_pairs={{0,2},{1,3},{2,0},{3,1},{4,6},{5,7},{6,4},{7,5},{8,10},{9,11},{10,... | collective-permute-start | bytes 221192 | tf_op jit(solution)/shard_map/ppermute | solution.py:358
  9.8 0.1 bitcast_dynamic-update-slice_fusion.7
  9.9 0.4 collective-permute-done.5
  10.3 1.9 %collective-permute-start.6 = (bf16[2,18432]{1,0:T(2,128)(2,1)S(1)}, bf16[2,18432]{1,0:T(2,128)(2,1)S(1)}, u32[]{:S(2)}, u32[]{:S(2)}) collective-permute-start(bf16[2,18432]{1,0:T(2,128)(2,1)S(1)} %collective-permute-done.5), channel_id=1, source_target_pairs={{0,2},{1,3},{2,0},{3,1},{4,6},{5,7},{6,4},{7,5},{8,10},{9,11},{10,... | collective-permute-start | bytes 221192 | tf_op jit(solution)/shard_map/ppermute | solution.py:358
  12.2 1.6 %collective-permute-done.3 = bf16[2,18432]{1,0:T(2,128)(2,1)S(1)} collective-permute-done((bf16[2,18432]{1,0:T(2,128)(2,1)S(1)}, bf16[2,18432]{1,0:T(2,128)(2,1)S(1)}, u32[]{:S(2)}, u32[]{:S(2)}) %collective-permute-start.3) | collective-permute-done | bytes 73760 | tf_op jit(solution)/shard_map/ppermute | solution.py:358
  13.8 1.5 %collective-permute-start.4 = (bf16[2,18432]{1,0:T(2,128)(2,1)S(1)}, bf16[2,18432]{1,0:T(2,128)(2,1)S(1)}, u32[]{:S(2)}, u32[]{:S(2)}) collective-permute-start(bf16[2,18432]{1,0:T(2,128)(2,1)S(1)} %collective-permute-done.3), channel_id=1, source_target_pairs={{0,2},{1,3},{2,0},{3,1},{4,6},{5,7},{6,4},{7,5},{8,10},{9,11},{10,... | collective-permute-start | bytes 221192 | tf_op jit(solution)/shard_map/ppermute | solution.py:358
  15.3 0.0 collective-permute-done.1
  15.3 0.5 collective-permute-start.2
  15.8 0.0 collective-permute-done
  15.8 0.1 bitcast_dynamic-update-slice_fusion.6
  15.9 0.1 bitcast_dynamic-update-slice_fusion.5
  15.9 3.7 %collective-permute-done.2 = bf16[2,18432]{1,0:T(2,128)(2,1)S(1)} collective-permute-done((bf16[2,18432]{1,0:T(2,128)(2,1)S(1)}, bf16[2,18432]{1,0:T(2,128)(2,1)S(1)}, u32[]{:S(2)}, u32[]{:S(2)}) %collective-permute-start.2) | collective-permute-done | bytes 73760 | tf_op jit(solution)/shard_map/ppermute | solution.py:358
  19.6 0.1 bitcast_dynamic-update-slice_fusion.4
  19.7 0.1 bitcast_dynamic-update-slice_fusion.3
  19.7 0.0 collective-permute-done.4
  19.8 0.1 bitcast_dynamic-update-slice_fusion.2
  19.8 0.1 bitcast_dynamic-update-slice_fusion.1
  19.9 0.0 collective-permute-done.6
  19.9 0.1 bitcast_dynamic-update-slice_fusion.even_ref
  20.0 0.1 collective-permute-start.7
  21.4 0.1 multiply_cosine_fusion.1
  21.5 0.5 collective-permute-done.7.odd_ref
  22.1 19.7 %shard_map.120 = (f32[16,2,416]{2,1,0:T(2,128)}, bf16[32,576]{1,0:T(8,128)(2,1)S(1)}) custom-call(bf16[8,2,18432]{2,1,0:T(2,128)(2,1)S(1)} %bitcast_dynamic-update-slice_fusion.even_ref, bf16[8,2,18432]{2,1,0:T(2,128)(2,1)S(1)} %collective-permute-done.7.odd_ref, bf16[384,18432]{1,0:T(8,128)(2,1)S(1)} %copy-done.1, bf16[576,18432]{1,0:T(8,128)(2,1)S(1)} %bitcast.65, ...), custom_call_target="tpu_custom_call" | custom-call | flops 1849688064 | bytes 57802752 | tf_op jit(solution)/shard_map/pallas_call | solution.py:144
  41.8 0.0 copy-start.6
  41.9 4.5 %all-to-all-start = ((f32[16,2,416]{2,1,0:T(2,128)}), f32[16,2,416]{2,1,0:T(2,128)S(1)}, u32[]{:S(2)}, u32[]{:S(2)}) async-start(f32[16,2,416]{2,1,0:T(2,128)} %get-tuple-element.21), calls=%async_computation | async-start | bytes 131072 | tf_op jit(solution)/shard_map/all_to_all | solution.py:395
  46.3 4.8 %shard_map.121.first_ref = f32[32,9216]{1,0:T(8,128)S(1)} custom-call(bf16[32,576]{1,0:T(8,128)(2,1)S(1)} %get-tuple-element.26.hidden_ref, bf16[576,18432]{1,0:T(8,128)(2,1)} %w_ref.4), custom_call_target="tpu_custom_call" | custom-call | flops 339738624 | bytes 10616832 | tf_op jit(solution)/shard_map/pallas_call | solution.py:195
  51.1 2.1 %all-to-all-done = f32[16,2,416]{2,1,0:T(2,128)S(1)} async-done(((f32[16,2,416]{2,1,0:T(2,128)}), f32[16,2,416]{2,1,0:T(2,128)S(1)}, u32[]{:S(2)}, u32[]{:S(2)}) %all-to-all-start) | async-done | bytes 53280 | tf_op jit(solution)/shard_map/all_to_all | solution.py:395
  53.3 0.1 reshape.338
  53.4 0.1 fusion.27
  53.5 0.4 fusion.31
  53.9 0.2 fusion.32
  54.1 0.2 fusion.6
  54.3 0.3 fusion.3
  54.5 0.2 fusion.1
  54.8 0.6 copy.17
  55.4 3.9 %all-to-all-start.1 = ((bf16[16,2,384]{2,1,0:T(2,128)(2,1)}), bf16[16,2,384]{2,1,0:T(2,128)(2,1)S(1)}, u32[]{:S(2)}, u32[]{:S(2)}) async-start(bf16[16,2,384]{2,1,0:T(2,128)(2,1)} %bitcast.61), calls=%async_computation.1 | async-start | bytes 49152 | tf_op jit(solution)/shard_map/all_to_all | solution.py:408
  59.4 4.8 %shard_map.122.second_ref = f32[32,9216]{1,0:T(8,128)S(1)} custom-call(bf16[32,576]{1,0:T(8,128)(2,1)S(1)} %get-tuple-element.26.hidden_ref, bf16[576,18432]{1,0:T(8,128)(2,1)} %w_ref.4), custom_call_target="tpu_custom_call" | custom-call | flops 339738624 | bytes 10616832 | tf_op jit(solution)/shard_map/pallas_call | solution.py:195
  64.1 0.0 copy-start.4
  64.2 1.8 %all-to-all-done.1.attended_ref = bf16[16,2,384]{2,1,0:T(2,128)(2,1)S(1)} async-done(((bf16[16,2,384]{2,1,0:T(2,128)(2,1)}), bf16[16,2,384]{2,1,0:T(2,128)(2,1)S(1)}, u32[]{:S(2)}, u32[]{:S(2)}) %all-to-all-start.1) | async-done | bytes 24608 | tf_op jit(solution)/shard_map/all_to_all | solution.py:408
  65.9 6.2 %shard_map.123 = (f32[16,18432]{1,0:T(8,128)S(1)}, bf16[16,18432]{1,0:T(8,128)(2,1)S(1)}) custom-call(bf16[16,2,384]{2,1,0:T(2,128)(2,1)S(1)} %all-to-all-done.1.attended_ref, f32[32,9216]{1,0:T(8,128)S(1)} %shard_map.121.first_ref, f32[32,9216]{1,0:T(8,128)S(1)} %shard_map.122.second_ref, bf16[384,18432]{1,0:T(8,128)(2,1)} %w_ref.5), custom_call_target="tpu_custom_call" | custom-call | flops 452984832 | bytes 14155776 | tf_op jit(solution)/shard_map/pallas_call | solution.py:269
  72.1 0.1 collective-permute-start.8
  72.2 2.0 %collective-permute-done.8.came_ref = bf16[16,18432]{1,0:T(8,128)(2,1)S(1)} collective-permute-done((bf16[16,18432]{1,0:T(8,128)(2,1)S(1)}, bf16[16,18432]{1,0:T(8,128)(2,1)S(1)}, u32[]{:S(2)}, u32[]{:S(2)}) %collective-permute-start.8) | collective-permute-done | bytes 589856 | tf_op jit(solution)/shard_map/ppermute | solution.py:358
  74.1 0.4 shard_map.124
  74.6 3.0 %collective-permute-start.9 = (bf16[2,18432]{1,0:T(2,128)(2,1)S(1)}, bf16[2,18432]{1,0:T(2,128)(2,1)S(1)}, u32[]{:S(2)}, u32[]{:S(2)}) collective-permute-start(bf16[2,18432]{1,0:T(2,128)(2,1)S(1)} %get-tuple-element.30), channel_id=1, source_target_pairs={{0,14},{1,15},{2,12},{3,13},{4,10},{5,11},{6,8},{7,9},{8,6},{9,7},... | collective-permute-start | bytes 221192 | tf_op jit(solution)/shard_map/ppermute | solution.py:358
  77.5 0.8 collective-permute-start.10
  78.3 0.4 collective-permute-start.11
  78.6 3.6 %collective-permute-start.12 = (bf16[2,18432]{1,0:T(2,128)(2,1)S(1)}, bf16[2,18432]{1,0:T(2,128)(2,1)S(1)}, u32[]{:S(2)}, u32[]{:S(2)}) collective-permute-start(bf16[2,18432]{1,0:T(2,128)(2,1)S(1)} %get-tuple-element.33), channel_id=1, source_target_pairs={{0,8},{1,9},{2,10},{3,11},{4,12},{5,13},{6,14},{7,15},{8,0},{9,1},... | collective-permute-start | bytes 221192 | tf_op jit(solution)/shard_map/ppermute | solution.py:358
  82.3 0.5 collective-permute-start.13
  82.8 0.0 collective-permute-done.9
  82.8 3.6 %collective-permute-start.14 = (bf16[2,18432]{1,0:T(2,128)(2,1)S(1)}, bf16[2,18432]{1,0:T(2,128)(2,1)S(1)}, u32[]{:S(2)}, u32[]{:S(2)}) collective-permute-start(bf16[2,18432]{1,0:T(2,128)(2,1)S(1)} %get-tuple-element.35), channel_id=1, source_target_pairs={{0,4},{1,5},{2,6},{3,7},{4,0},{5,1},{6,2},{7,3},{8,12},{9,13},{10,... | collective-permute-start | bytes 221192 | tf_op jit(solution)/shard_map/ppermute | solution.py:358
  86.4 3.4 %collective-permute-done.11 = bf16[2,18432]{1,0:T(2,128)(2,1)S(1)} collective-permute-done((bf16[2,18432]{1,0:T(2,128)(2,1)S(1)}, bf16[2,18432]{1,0:T(2,128)(2,1)S(1)}, u32[]{:S(2)}, u32[]{:S(2)}) %collective-permute-start.11) | collective-permute-done | bytes 73760 | tf_op jit(solution)/shard_map/ppermute | solution.py:358
  89.9 0.8 collective-permute-done.12
  90.7 0.7 collective-permute-done.14
  91.4 0.0 collective-permute-done.15
  91.4 1.0 %fusion.9 = bf16[2,1,18432]{2,0,1:T(2,128)(2,1)} fusion(bf16[2,18432]{1,0:T(2,128)(2,1)S(1)} %collective-permute-done.15, bf16[2,18432]{1,0:T(2,128)(2,1)S(1)} %collective-permute-done.14, bf16[2,18432]{1,0:T(2,128)(2,1)S(1)} %collective-permute-done.13, bf16[2,18432]{1,0:T(2,128)(2,1)S(1)} %collective-permute-done.12, ...), kind=kLoop, calls=%fused_computation.23 | loop fusion | flops 626688 | bytes 811008 | tf_op jit(solution)/shard_map/reshape | solution.py:417
  (38 shorter events, 0.2 us)
Async XLA Ops:
  0.0 53.5 %copy-start = (bf16[1,1024,256]{2,1,0:T(8,128)(2,1)S(1)}, bf16[1,1024,256]{2,1,0:T(8,128)(2,1)}, u32[]{:S(2)}) copy-start(bf16[1,1024,256]{2,1,0:T(8,128)(2,1)} %param.20) | copy-start | bytes 1572868
  0.0 22.0 %slice-start = ((s8[21233664]{0:T(1024)(128)(4,1)}), s8[4194304]{0:T(1024)(128)(4,1)S(1)}, s32[]{:S(2)}) async-start(s8[21233664]{0:T(1024)(128)(4,1)} %bitcast.64), calls=%async_computation.2 | async-start | bytes 8388608
  0.0 1.0 %copy-start.3 = (bf16[2,1,18432]{2,0,1:T(2,128)(2,1)S(1)}, bf16[2,1,18432]{2,0,1:T(2,128)(2,1)}, u32[]{:S(2)}) copy-start(bf16[2,1,18432]{2,0,1:T(2,128)(2,1)} %param.12) | copy-start | bytes 221188
  1.0 1.3 %copy-start.5 = (f32[18432]{0:T(1024)S(1)}, f32[18432]{0:T(1024)}, u32[]{:S(2)}) copy-start(f32[18432]{0:T(1024)} %param.13) | copy-start | bytes 221188
  1.0 21.0 %slice-start.1 = ((s8[21233664]{0:T(1024)(128)(4,1)}), s8[4194304]{0:T(1024)(128)(4,1)S(1)}, s32[]{:S(2)}) async-start(s8[21233664]{0:T(1024)(128)(4,1)} %bitcast.64), calls=%async_computation.3 | async-start | bytes 8388608
  1.0 21.0 %slice-start.2 = ((s8[21233664]{0:T(1024)(128)(4,1)}), s8[4194304]{0:T(1024)(128)(4,1)S(1)}, s32[]{:S(2)}) async-start(s8[21233664]{0:T(1024)(128)(4,1)} %bitcast.64), calls=%async_computation.4 | async-start | bytes 8388608
  1.0 21.0 %slice-start.3 = ((s8[21233664]{0:T(1024)(128)(4,1)}), s8[4194304]{0:T(1024)(128)(4,1)S(1)}, s32[]{:S(2)}) async-start(s8[21233664]{0:T(1024)(128)(4,1)} %bitcast.64), calls=%async_computation.5 | async-start | bytes 8388608
  1.1 21.0 %slice-start.4 = ((s8[21233664]{0:T(1024)(128)(4,1)}), s8[4194304]{0:T(1024)(128)(4,1)S(1)}, s32[]{:S(2)}) async-start(s8[21233664]{0:T(1024)(128)(4,1)} %bitcast.64), calls=%async_computation.6 | async-start | bytes 8388608
  1.1 21.0 %slice-start.5 = ((s8[21233664]{0:T(1024)(128)(4,1)}), s8[262144]{0:T(1024)(128)(4,1)S(1)}, s32[]{:S(2)}) async-start(s8[21233664]{0:T(1024)(128)(4,1)} %bitcast.64), calls=%async_computation.7 | async-start | bytes 524288
  1.1 21.0 %copy-start.1 = (bf16[384,18432]{1,0:T(8,128)(2,1)S(1)}, bf16[384,18432]{1,0:T(8,128)(2,1)}, u32[]{:S(2)}) copy-start(bf16[384,18432]{1,0:T(8,128)(2,1)} %wq_ref.1) | copy-start | bytes 42467332
  1.1 21.0 %copy-start.2 = (bf16[32,18432]{1,0:T(8,128)(2,1)S(1)}, bf16[32,18432]{1,0:T(8,128)(2,1)}, u32[]{:S(2)}) copy-start(bf16[32,18432]{1,0:T(8,128)(2,1)} %wk_ref.1) | copy-start | bytes 3538948
  2.4 7.9 %collective-permute-start.5 = (bf16[2,18432]{1,0:T(2,128)(2,1)S(1)}, bf16[2,18432]{1,0:T(2,128)(2,1)S(1)}, u32[]{:S(2)}, u32[]{:S(2)}) collective-permute-start(bf16[2,18432]{1,0:T(2,128)(2,1)S(1)} %shard_map.119), channel_id=1, source_target_pairs={{0,12},{1,13},{2,14},{3,15},{4,8},{5,9},{6,10},{7,11},{8,4},{9,5},... | collective-permute-start | bytes 221192 | tf_op jit(solution)/shard_map/ppermute | solution.py:358
  7.5 6.2 %collective-permute-start.3 = (bf16[2,18432]{1,0:T(2,128)(2,1)S(1)}, bf16[2,18432]{1,0:T(2,128)(2,1)S(1)}, u32[]{:S(2)}, u32[]{:S(2)}) collective-permute-start(bf16[2,18432]{1,0:T(2,128)(2,1)S(1)} %shard_map.119), channel_id=1, source_target_pairs={{0,8},{1,9},{2,10},{3,11},{4,12},{5,13},{6,14},{7,15},{8,0},{9,1},... | collective-permute-start | bytes 221192 | tf_op jit(solution)/shard_map/ppermute | solution.py:358
  7.6 7.7 %collective-permute-start.1 = (bf16[2,18432]{1,0:T(2,128)(2,1)S(1)}, bf16[2,18432]{1,0:T(2,128)(2,1)S(1)}, u32[]{:S(2)}, u32[]{:S(2)}) collective-permute-start(bf16[2,18432]{1,0:T(2,128)(2,1)S(1)} %shard_map.119), channel_id=1, source_target_pairs={{0,4},{1,5},{2,6},{3,7},{4,0},{5,1},{6,2},{7,3},{8,12},{9,13},{10,... | collective-permute-start | bytes 221192 | tf_op jit(solution)/shard_map/ppermute | solution.py:358
  8.2 7.6 %collective-permute-start = (bf16[2,18432]{1,0:T(2,128)(2,1)S(1)}, bf16[2,18432]{1,0:T(2,128)(2,1)S(1)}, u32[]{:S(2)}, u32[]{:S(2)}) collective-permute-start(bf16[2,18432]{1,0:T(2,128)(2,1)S(1)} %shard_map.119), channel_id=1, source_target_pairs={{0,2},{1,3},{2,0},{3,1},{4,6},{5,7},{6,4},{7,5},{8,10},{9,11},{10,... | collective-permute-start | bytes 221192 | tf_op jit(solution)/shard_map/ppermute | solution.py:358
  10.3 9.6 %collective-permute-start.6 = (bf16[2,18432]{1,0:T(2,128)(2,1)S(1)}, bf16[2,18432]{1,0:T(2,128)(2,1)S(1)}, u32[]{:S(2)}, u32[]{:S(2)}) collective-permute-start(bf16[2,18432]{1,0:T(2,128)(2,1)S(1)} %collective-permute-done.5), channel_id=1, source_target_pairs={{0,2},{1,3},{2,0},{3,1},{4,6},{5,7},{6,4},{7,5},{8,10},{9,11},{10,... | collective-permute-start | bytes 221192 | tf_op jit(solution)/shard_map/ppermute | solution.py:358
  13.8 6.0 %collective-permute-start.4 = (bf16[2,18432]{1,0:T(2,128)(2,1)S(1)}, bf16[2,18432]{1,0:T(2,128)(2,1)S(1)}, u32[]{:S(2)}, u32[]{:S(2)}) collective-permute-start(bf16[2,18432]{1,0:T(2,128)(2,1)S(1)} %collective-permute-done.3), channel_id=1, source_target_pairs={{0,2},{1,3},{2,0},{3,1},{4,6},{5,7},{6,4},{7,5},{8,10},{9,11},{10,... | collective-permute-start | bytes 221192 | tf_op jit(solution)/shard_map/ppermute | solution.py:358
  15.3 4.4 %collective-permute-start.2 = (bf16[2,18432]{1,0:T(2,128)(2,1)S(1)}, bf16[2,18432]{1,0:T(2,128)(2,1)S(1)}, u32[]{:S(2)}, u32[]{:S(2)}) collective-permute-start(bf16[2,18432]{1,0:T(2,128)(2,1)S(1)} %collective-permute-done.1), channel_id=1, source_target_pairs={{0,2},{1,3},{2,0},{3,1},{4,6},{5,7},{6,4},{7,5},{8,10},{9,11},{10,... | collective-permute-start | bytes 221192 | tf_op jit(solution)/shard_map/ppermute | solution.py:358
  20.0 2.1 %collective-permute-start.7 = (bf16[8,2,18432]{2,1,0:T(2,128)(2,1)S(1)}, bf16[8,2,18432]{2,1,0:T(2,128)(2,1)S(1)}, u32[]{:S(2)}, u32[]{:S(2)}) collective-permute-start(bf16[8,2,18432]{2,1,0:T(2,128)(2,1)S(1)} %bitcast_dynamic-update-slice_fusion.even_ref), channel_id=1, source_target_pairs={{0,1},{1,0},{2,3},{3,2},{4,5},{5,4},{6,7},{7,6},{8,9},{9,8},{10,11... | collective-permute-start | bytes 1769480 | tf_op jit(solution)/shard_map/ppermute | solution.py:358
  41.8 12.4 %copy-start.6 = (bf16[1,1024,256]{2,1,0:T(8,128)(2,1)S(1)}, bf16[1,1024,256]{2,1,0:T(8,128)(2,1)}, u32[]{:S(2)}) copy-start(bf16[1,1024,256]{2,1,0:T(8,128)(2,1)} %param.21) | copy-start | bytes 1572868
  41.9 11.4 %all-to-all-start = ((f32[16,2,416]{2,1,0:T(2,128)}), f32[16,2,416]{2,1,0:T(2,128)S(1)}, u32[]{:S(2)}, u32[]{:S(2)}) async-start(f32[16,2,416]{2,1,0:T(2,128)} %get-tuple-element.21), calls=%async_computation | async-start | bytes 131072 | tf_op jit(solution)/shard_map/all_to_all | solution.py:395
  55.4 10.5 %all-to-all-start.1 = ((bf16[16,2,384]{2,1,0:T(2,128)(2,1)}), bf16[16,2,384]{2,1,0:T(2,128)(2,1)S(1)}, u32[]{:S(2)}, u32[]{:S(2)}) async-start(bf16[16,2,384]{2,1,0:T(2,128)(2,1)} %bitcast.61), calls=%async_computation.1 | async-start | bytes 49152 | tf_op jit(solution)/shard_map/all_to_all | solution.py:408
  64.1 27.2 %copy-start.4 = (bf16[2,1,18432]{2,0,1:T(2,128)(2,1)S(1)}, bf16[2,1,18432]{2,0,1:T(2,128)(2,1)}, u32[]{:S(2)}) copy-start(bf16[2,1,18432]{2,0,1:T(2,128)(2,1)} %param.12) | copy-start | bytes 221188
  72.1 2.1 %collective-permute-start.8 = (bf16[16,18432]{1,0:T(8,128)(2,1)S(1)}, bf16[16,18432]{1,0:T(8,128)(2,1)S(1)}, u32[]{:S(2)}, u32[]{:S(2)}) collective-permute-start(bf16[16,18432]{1,0:T(8,128)(2,1)S(1)} %get-tuple-element.28), channel_id=1, source_target_pairs={{0,1},{1,0},{2,3},{3,2},{4,5},{5,4},{6,7},{7,6},{8,9},{9,8},{10,11... | collective-permute-start | bytes 1769480 | tf_op jit(solution)/shard_map/ppermute | solution.py:358
  74.6 8.3 %collective-permute-start.9 = (bf16[2,18432]{1,0:T(2,128)(2,1)S(1)}, bf16[2,18432]{1,0:T(2,128)(2,1)S(1)}, u32[]{:S(2)}, u32[]{:S(2)}) collective-permute-start(bf16[2,18432]{1,0:T(2,128)(2,1)S(1)} %get-tuple-element.30), channel_id=1, source_target_pairs={{0,14},{1,15},{2,12},{3,13},{4,10},{5,11},{6,8},{7,9},{8,6},{9,7},... | collective-permute-start | bytes 221192 | tf_op jit(solution)/shard_map/ppermute | solution.py:358
  77.5 8.9 %collective-permute-start.10 = (bf16[2,18432]{1,0:T(2,128)(2,1)S(1)}, bf16[2,18432]{1,0:T(2,128)(2,1)S(1)}, u32[]{:S(2)}, u32[]{:S(2)}) collective-permute-start(bf16[2,18432]{1,0:T(2,128)(2,1)S(1)} %get-tuple-element.31), channel_id=1, source_target_pairs={{0,12},{1,13},{2,14},{3,15},{4,8},{5,9},{6,10},{7,11},{8,4},{9,5},... | collective-permute-start | bytes 221192 | tf_op jit(solution)/shard_map/ppermute | solution.py:358
  78.3 11.6 %collective-permute-start.11 = (bf16[2,18432]{1,0:T(2,128)(2,1)S(1)}, bf16[2,18432]{1,0:T(2,128)(2,1)S(1)}, u32[]{:S(2)}, u32[]{:S(2)}) collective-permute-start(bf16[2,18432]{1,0:T(2,128)(2,1)S(1)} %get-tuple-element.32), channel_id=1, source_target_pairs={{0,10},{1,11},{2,8},{3,9},{4,14},{5,15},{6,12},{7,13},{8,2},{9,3},... | collective-permute-start | bytes 221192 | tf_op jit(solution)/shard_map/ppermute | solution.py:358
  78.6 12.0 %collective-permute-start.12 = (bf16[2,18432]{1,0:T(2,128)(2,1)S(1)}, bf16[2,18432]{1,0:T(2,128)(2,1)S(1)}, u32[]{:S(2)}, u32[]{:S(2)}) collective-permute-start(bf16[2,18432]{1,0:T(2,128)(2,1)S(1)} %get-tuple-element.33), channel_id=1, source_target_pairs={{0,8},{1,9},{2,10},{3,11},{4,12},{5,13},{6,14},{7,15},{8,0},{9,1},... | collective-permute-start | bytes 221192 | tf_op jit(solution)/shard_map/ppermute | solution.py:358
  82.3 8.4 %collective-permute-start.13 = (bf16[2,18432]{1,0:T(2,128)(2,1)S(1)}, bf16[2,18432]{1,0:T(2,128)(2,1)S(1)}, u32[]{:S(2)}, u32[]{:S(2)}) collective-permute-start(bf16[2,18432]{1,0:T(2,128)(2,1)S(1)} %get-tuple-element.34), channel_id=1, source_target_pairs={{0,6},{1,7},{2,4},{3,5},{4,2},{5,3},{6,0},{7,1},{8,14},{9,15},{10,... | collective-permute-start | bytes 221192 | tf_op jit(solution)/shard_map/ppermute | solution.py:358
  82.8 8.5 %collective-permute-start.14 = (bf16[2,18432]{1,0:T(2,128)(2,1)S(1)}, bf16[2,18432]{1,0:T(2,128)(2,1)S(1)}, u32[]{:S(2)}, u32[]{:S(2)}) collective-permute-start(bf16[2,18432]{1,0:T(2,128)(2,1)S(1)} %get-tuple-element.35), channel_id=1, source_target_pairs={{0,4},{1,5},{2,6},{3,7},{4,0},{5,1},{6,2},{7,3},{8,12},{9,13},{10,... | collective-permute-start | bytes 221192 | tf_op jit(solution)/shard_map/ppermute | solution.py:358
  86.4 4.9 %collective-permute-start.15 = (bf16[2,18432]{1,0:T(2,128)(2,1)S(1)}, bf16[2,18432]{1,0:T(2,128)(2,1)S(1)}, u32[]{:S(2)}, u32[]{:S(2)}) collective-permute-start(bf16[2,18432]{1,0:T(2,128)(2,1)S(1)} %get-tuple-element.36), channel_id=1, source_target_pairs={{0,2},{1,3},{2,0},{3,1},{4,6},{5,7},{6,4},{7,5},{8,10},{9,11},{10,... | collective-permute-start | bytes 221192 | tf_op jit(solution)/shard_map/ppermute | solution.py:358

commit v6 on v5

--- a/solution.py
+++ b/solution.py
@@ -290,33 +290,77 @@
     )(attended, first, second, w_out)
 
 
-def cut_kernel(keep_ref, came_ref, own_ref, *send_refs):
+def cut_kernel(plan, keep_ref, came_ref, own_ref, far_ref, *send_refs):
+    near, kept, sent = plan
     steps = own_ref.shape[0]
     total = keep_ref[...] + came_ref[...].astype(F32)
-    own_ref[...] = total[:steps]
-    for p, send_ref in enumerate(send_refs):
-        send_ref[...] = total[(p + 1) * steps : (p + 2) * steps].astype(BF16)
-
-
-def cut_parts(keep, came, steps):
+
+    def piece(place):
+        return total[place * steps : (place + 1) * steps]
+
+    own_ref[...] = piece(0)
+    for k, place in enumerate(kept):
+        far_ref[k] = piece(place)
+    for place, send_ref in zip(near, send_refs):
+        send_ref[...] = piece(place).astype(BF16)
+    for group, send_ref in zip(sent, send_refs[len(near) :]):
+        for k, place in enumerate(group):
+            send_ref[k] = piece(place).astype(BF16)
+
+
+def cut_parts(keep, came, steps, plan):
     half, width = keep.shape
-    slots = half // steps
+    near, kept, sent = plan
     chunks = 3 if width % 384 == 0 else 1
     step = width // chunks
     whole = pl.BlockSpec((half, step), lambda c: (0, c))
     piece = pl.BlockSpec((steps, step), lambda c: (0, c))
-    return pl.pallas_call(
-        cut_kernel,
+    pair = pl.BlockSpec((len(kept), steps, step), lambda c: (0, 0, c))
+    pair_shape = (len(kept), steps, width)
+    return pl.pallas_call(
+        functools.partial(cut_kernel, plan),
         grid=(chunks,),
         in_specs=[whole, whole],
-        out_specs=[piece] * slots,
-        out_shape=[jax.ShapeDtypeStruct((steps, width), F32)]
-        + [jax.ShapeDtypeStruct((steps, width), BF16)] * (slots - 1),
+        out_specs=[piece, pair] + [piece] * len(near) + [pair] * len(sent),
+        out_shape=[
+            jax.ShapeDtypeStruct((steps, width), F32),
+            jax.ShapeDtypeStruct(pair_shape, F32),
+        ]
+        + [jax.ShapeDtypeStruct((steps, width), BF16)] * len(near)
+        + [jax.ShapeDtypeStruct(pair_shape, BF16)] * len(sent),
         compiler_params=params(32),
         cost_estimate=pl.CostEstimate(
             flops=2 * half * width, bytes_accessed=8 * half * width, transcendentals=0
         ),
     )(keep, came)
+
+
+def far_kernel(far_ref, *refs):
+    count = far_ref.shape[0]
+    for k in range(count):
+        total = far_ref[k]
+        for came_ref in refs[:-count]:
+            total = total + came_ref[k].astype(F32)
+        refs[len(refs) - count + k][...] = total.astype(BF16)
+
+
+def far_parts(far, arrived):
+    count, steps, width = far.shape
+    chunks = 3 if width % 384 == 0 else 1
+    step = width // chunks
+    pair = pl.BlockSpec((count, steps, step), lambda c: (0, 0, c))
+    piece = pl.BlockSpec((steps, step), lambda c: (0, c))
+    return pl.pallas_call(
+        far_kernel,
+        grid=(chunks,),
+        in_specs=[pair] * (1 + len(arrived)),
+        out_specs=[piece] * count,
+        out_shape=[jax.ShapeDtypeStruct((steps, width), BF16)] * count,
+        compiler_params=params(32),
+        cost_estimate=pl.CostEstimate(
+            flops=far.size, bytes_accessed=8 * far.size, transcendentals=0
+        ),
+    )(far, *arrived)
 
 
 def rotate(vector, angle_pos):
@@ -365,6 +409,24 @@
     far = [near] + [[swap(p, 2 * b, devices) for p in near] for b in range(1, inner)]
     even = jnp.stack([far[b][a] for a in range(outer) for b in range(inner)])
     return even, swap(even, 1, devices)
+
+
+def scatter_sums(keep, came, batch, devices):
+    outer = min(4, devices // 2)
+    inner = devices // (2 * outer)
+    middle = outer // 2
+    near = [p for p in range(1, middle * inner)]
+    kept = [a * inner for a in range(middle, outer)]
+    sent = [[p + b for p in kept] for b in range(1, inner)]
+    own, far, *sends = cut_parts(keep, came, batch, (near, kept, sent))
+    arrived = [
+        swap(group, 2 * b, devices) for b, group in zip(range(1, inner), sends[len(near) :])
+    ]
+    parts = [swap(piece, 2 * p, devices) for p, piece in zip(near, sends)]
+    late = [swap(piece, 2 * p, devices) for p, piece in zip(kept, far_parts(far, arrived))]
+    for part in parts + late:
+        own = own + part.astype(F32)
+    return own
 
 
 def local(
@@ -409,10 +471,7 @@
 
     second = down_part(hidden, w_down, chunks // 2, chunks)
     keep, send = branch_parts(attended, first, second, w_out)
-    pieces = cut_parts(keep, swap(send, 1, devices), batch)
-    branch = pieces[0]
-    for place in reversed(range(1, devices // 2)):
-        branch = branch + swap(pieces[place], 2 * place, devices).astype(F32)
+    branch = scatter_sums(keep, swap(send, 1, devices), batch, devices)
     result = (own_tokens.astype(F32) + branch).astype(BF16)
     return result.reshape(tokens.shape)
 

time: 92.6 us -> 90.8 us (0.981)
  starting transfers between devices: 31.7 us -> 25.4 us
  waiting for transfers between devices: 17 us -> 21.2 us
    ppermute x16 -> x15, starting transfers between devices: 23.3 us -> 17 us  [swap(): return lax.ppermute(value, 'gx', [(i, i ^ bits) for i in range(devices)])]
    ppermute x16 -> x15, waiting for transfers between devices: 13.2 us -> 17.4 us  [swap(): return lax.ppermute(value, 'gx', [(i, i ^ bits) for i in range(devices)])]
  transfers between devices with their start and end apart: 18 -> 17, of which waited for: 10 -> 10; matrix products, arithmetic and copies ran while one was open for 1% -> 1% of each run, Pallas kernels for 10% -> 11%
where the time goes in v6:
time: 90.8 us; the launch traced here: 90.5 us
  Pallas kernels  36.7 us (40%)
  starting transfers between devices  25.4 us (28%)
  waiting for transfers between devices  21.2 us (23%)
  local copies, waits for them, and re-layouts  3.13 us (3%)
  between operations  1.63 us (2%)
  other arithmetic  1.37 us (2%)
  matrix products  0.98 us (1%)
    pallas_call x1, Pallas kernels, project(): pl.pallas_call(functools.partial(project_kernel, chunks), in_specs=[VMEM,...  19.7 us
    ppermute x15, waiting for transfers between devices, swap(): return lax.ppermute(value, 'gx', [(i, i ^ bits) for i in range(devices)])  17.4 us
    ppermute x15, starting transfers between devices, swap(): return lax.ppermute(value, 'gx', [(i, i ^ bits) for i in range(devices)])  17 us
    pallas_call x2, Pallas kernels, down_part(): pl.pallas_call(functools.partial(down_kernel, chunks, first * step), in_s...  9.56 us
    pallas_call x1, Pallas kernels, branch_parts(): pl.pallas_call(functools.partial(branch_kernel, chunks), in_specs=[VMEM,...  6.15 us
    all_to_all x1, starting transfers between devices, local(): lax.all_to_all(projected, 'gx', split_axis=0, concat_axis=0, tiled=True)  4.47 us
    all_to_all x1, starting transfers between devices, local(): lax.all_to_all(attended, 'gx', split_axis=0, concat_axis=0, tiled=True)  3.93 us
    unnamed x33, local copies, waits for them, and re-layouts  2.28 us
  transfers between devices with their start and end apart: 17, of which 10 were waited for; matrix products, arithmetic and copies ran while one was open for 1% of the time, Pallas kernels for 11%

profile of v6, /device:TPU:0, one launch (start us, length us, event | category | flops | bytes accessed | tf_op | source)
XLA Modules:
  0.0 90.5 jit_solution(12029484817268576816)
XLA Ops:
  0.0 1.0 %copy-done.4 = bf16[2,1,18432]{2,0,1:T(2,128)(2,1)S(1)} copy-done((bf16[2,1,18432]{2,0,1:T(2,128)(2,1)S(1)}, bf16[2,1,18432]{2,0,1:T(2,128)(2,1)}, u32[]{:S(2)}) %copy-start.4) | copy-done | bytes 73752
  1.1 0.0 slice-start.4
  1.1 0.0 slice-start.5
  1.1 0.5 shard_map.118.values_ref
  1.6 0.8 copy-done.3
  2.3 0.1 shard_map.119
  2.4 5.1 %collective-permute-start.5 = (bf16[2,18432]{1,0:T(2,128)(2,1)S(1)}, bf16[2,18432]{1,0:T(2,128)(2,1)S(1)}, u32[]{:S(2)}, u32[]{:S(2)}) collective-permute-start(bf16[2,18432]{1,0:T(2,128)(2,1)S(1)} %shard_map.119), channel_id=1, source_target_pairs={{0,12},{1,13},{2,14},{3,15},{4,8},{5,9},{6,10},{7,11},{8,4},{9,5},... | collective-permute-start | bytes 221192 | tf_op jit(solution)/shard_map/ppermute | solution.py:402
  7.5 0.0 collective-permute-start.3
  7.6 0.6 collective-permute-start.1
  8.2 1.6 %collective-permute-start = (bf16[2,18432]{1,0:T(2,128)(2,1)S(1)}, bf16[2,18432]{1,0:T(2,128)(2,1)S(1)}, u32[]{:S(2)}, u32[]{:S(2)}) collective-permute-start(bf16[2,18432]{1,0:T(2,128)(2,1)S(1)} %shard_map.119), channel_id=1, source_target_pairs={{0,2},{1,3},{2,0},{3,1},{4,6},{5,7},{6,4},{7,5},{8,10},{9,11},{10,... | collective-permute-start | bytes 221192 | tf_op jit(solution)/shard_map/ppermute | solution.py:402
  9.8 0.1 bitcast_dynamic-update-slice_fusion.7
  9.9 0.4 collective-permute-done.5
  10.3 1.9 %collective-permute-start.6 = (bf16[2,18432]{1,0:T(2,128)(2,1)S(1)}, bf16[2,18432]{1,0:T(2,128)(2,1)S(1)}, u32[]{:S(2)}, u32[]{:S(2)}) collective-permute-start(bf16[2,18432]{1,0:T(2,128)(2,1)S(1)} %collective-permute-done.5), channel_id=1, source_target_pairs={{0,2},{1,3},{2,0},{3,1},{4,6},{5,7},{6,4},{7,5},{8,10},{9,11},{10,... | collective-permute-start | bytes 221192 | tf_op jit(solution)/shard_map/ppermute | solution.py:402
  12.2 1.6 %collective-permute-done.3 = bf16[2,18432]{1,0:T(2,128)(2,1)S(1)} collective-permute-done((bf16[2,18432]{1,0:T(2,128)(2,1)S(1)}, bf16[2,18432]{1,0:T(2,128)(2,1)S(1)}, u32[]{:S(2)}, u32[]{:S(2)}) %collective-permute-start.3) | collective-permute-done | bytes 73760 | tf_op jit(solution)/shard_map/ppermute | solution.py:402
  13.8 1.5 %collective-permute-start.4 = (bf16[2,18432]{1,0:T(2,128)(2,1)S(1)}, bf16[2,18432]{1,0:T(2,128)(2,1)S(1)}, u32[]{:S(2)}, u32[]{:S(2)}) collective-permute-start(bf16[2,18432]{1,0:T(2,128)(2,1)S(1)} %collective-permute-done.3), channel_id=1, source_target_pairs={{0,2},{1,3},{2,0},{3,1},{4,6},{5,7},{6,4},{7,5},{8,10},{9,11},{10,... | collective-permute-start | bytes 221192 | tf_op jit(solution)/shard_map/ppermute | solution.py:402
  15.3 0.5 collective-permute-start.2
  15.8 0.0 collective-permute-done
  15.8 0.1 bitcast_dynamic-update-slice_fusion.6
  15.9 0.1 bitcast_dynamic-update-slice_fusion.5
  15.9 3.7 %collective-permute-done.2 = bf16[2,18432]{1,0:T(2,128)(2,1)S(1)} collective-permute-done((bf16[2,18432]{1,0:T(2,128)(2,1)S(1)}, bf16[2,18432]{1,0:T(2,128)(2,1)S(1)}, u32[]{:S(2)}, u32[]{:S(2)}) %collective-permute-start.2) | collective-permute-done | bytes 73760 | tf_op jit(solution)/shard_map/ppermute | solution.py:402
  19.6 0.1 bitcast_dynamic-update-slice_fusion.4
  19.7 0.1 bitcast_dynamic-update-slice_fusion.3
  19.8 0.1 bitcast_dynamic-update-slice_fusion.2
  19.8 0.1 bitcast_dynamic-update-slice_fusion.1
  19.9 0.0 collective-permute-done.6
  19.9 0.1 bitcast_dynamic-update-slice_fusion.even_ref
  20.0 0.1 collective-permute-start.7
  21.4 0.1 multiply_cosine_fusion.1
  21.5 0.5 collective-permute-done.7.odd_ref
  22.1 19.7 %shard_map.120 = (f32[16,2,416]{2,1,0:T(2,128)}, bf16[32,576]{1,0:T(8,128)(2,1)S(1)}) custom-call(bf16[8,2,18432]{2,1,0:T(2,128)(2,1)S(1)} %bitcast_dynamic-update-slice_fusion.even_ref, bf16[8,2,18432]{2,1,0:T(2,128)(2,1)S(1)} %collective-permute-done.7.odd_ref, bf16[384,18432]{1,0:T(8,128)(2,1)S(1)} %copy-done.1, bf16[576,18432]{1,0:T(8,128)(2,1)S(1)} %bitcast.65, ...), custom_call_target="tpu_custom_call" | custom-call | flops 1849688064 | bytes 57802752 | tf_op jit(solution)/shard_map/pallas_call | solution.py:144
  41.8 0.0 copy-start.6
  41.9 4.5 %all-to-all-start = ((f32[16,2,416]{2,1,0:T(2,128)}), f32[16,2,416]{2,1,0:T(2,128)S(1)}, u32[]{:S(2)}, u32[]{:S(2)}) async-start(f32[16,2,416]{2,1,0:T(2,128)} %get-tuple-element.21), calls=%async_computation | async-start | bytes 131072 | tf_op jit(solution)/shard_map/all_to_all | solution.py:457
  46.3 4.8 %shard_map.121.first_ref = f32[32,9216]{1,0:T(8,128)S(1)} custom-call(bf16[32,576]{1,0:T(8,128)(2,1)S(1)} %get-tuple-element.26.hidden_ref, bf16[576,18432]{1,0:T(8,128)(2,1)} %w_ref.4), custom_call_target="tpu_custom_call" | custom-call | flops 339738624 | bytes 10616832 | tf_op jit(solution)/shard_map/pallas_call | solution.py:195
  51.1 2.1 %all-to-all-done = f32[16,2,416]{2,1,0:T(2,128)S(1)} async-done(((f32[16,2,416]{2,1,0:T(2,128)}), f32[16,2,416]{2,1,0:T(2,128)S(1)}, u32[]{:S(2)}, u32[]{:S(2)}) %all-to-all-start) | async-done | bytes 53280 | tf_op jit(solution)/shard_map/all_to_all | solution.py:457
  53.3 0.1 reshape.338
  53.4 0.1 fusion.27
  53.5 0.4 fusion.31
  53.9 0.2 fusion.32
  54.1 0.2 fusion.6
  54.3 0.3 fusion.3
  54.5 0.2 fusion.1
  54.8 0.6 copy.17
  55.4 3.9 %all-to-all-start.1 = ((bf16[16,2,384]{2,1,0:T(2,128)(2,1)}), bf16[16,2,384]{2,1,0:T(2,128)(2,1)S(1)}, u32[]{:S(2)}, u32[]{:S(2)}) async-start(bf16[16,2,384]{2,1,0:T(2,128)(2,1)} %bitcast.61), calls=%async_computation.1 | async-start | bytes 49152 | tf_op jit(solution)/shard_map/all_to_all | solution.py:470
  59.4 4.8 %shard_map.122.second_ref = f32[32,9216]{1,0:T(8,128)S(1)} custom-call(bf16[32,576]{1,0:T(8,128)(2,1)S(1)} %get-tuple-element.26.hidden_ref, bf16[576,18432]{1,0:T(8,128)(2,1)} %w_ref.4), custom_call_target="tpu_custom_call" | custom-call | flops 339738624 | bytes 10616832 | tf_op jit(solution)/shard_map/pallas_call | solution.py:195
  64.1 0.0 copy-start.5
  64.2 1.8 %all-to-all-done.1.attended_ref = bf16[16,2,384]{2,1,0:T(2,128)(2,1)S(1)} async-done(((bf16[16,2,384]{2,1,0:T(2,128)(2,1)}), bf16[16,2,384]{2,1,0:T(2,128)(2,1)S(1)}, u32[]{:S(2)}, u32[]{:S(2)}) %all-to-all-start.1) | async-done | bytes 24608 | tf_op jit(solution)/shard_map/all_to_all | solution.py:470
  65.9 6.2 %shard_map.123 = (f32[16,18432]{1,0:T(8,128)S(1)}, bf16[16,18432]{1,0:T(8,128)(2,1)S(1)}) custom-call(bf16[16,2,384]{2,1,0:T(2,128)(2,1)S(1)} %all-to-all-done.1.attended_ref, f32[32,9216]{1,0:T(8,128)S(1)} %shard_map.121.first_ref, f32[32,9216]{1,0:T(8,128)S(1)} %shard_map.122.second_ref, bf16[384,18432]{1,0:T(8,128)(2,1)} %w_ref.5), custom_call_target="tpu_custom_call" | custom-call | flops 452984832 | bytes 14155776 | tf_op jit(solution)/shard_map/pallas_call | solution.py:269
  72.1 0.1 collective-permute-start.8
  72.2 2.0 %collective-permute-done.8.came_ref = bf16[16,18432]{1,0:T(8,128)(2,1)S(1)} collective-permute-done((bf16[16,18432]{1,0:T(8,128)(2,1)S(1)}, bf16[16,18432]{1,0:T(8,128)(2,1)S(1)}, u32[]{:S(2)}, u32[]{:S(2)}) %collective-permute-start.8) | collective-permute-done | bytes 589856 | tf_op jit(solution)/shard_map/ppermute | solution.py:402
  74.1 0.5 shard_map.124
  74.6 0.5 collective-permute-start.12
  75.1 1.6 %collective-permute-start.9 = (bf16[2,18432]{1,0:T(2,128)(2,1)S(1)}, bf16[2,18432]{1,0:T(2,128)(2,1)S(1)}, u32[]{:S(2)}, u32[]{:S(2)}) collective-permute-start(bf16[2,18432]{1,0:T(2,128)(2,1)S(1)} %get-tuple-element.30), channel_id=1, source_target_pairs={{0,2},{1,3},{2,0},{3,1},{4,6},{5,7},{6,4},{7,5},{8,10},{9,11},{10,... | collective-permute-start | bytes 221192 | tf_op jit(solution)/shard_map/ppermute | solution.py:402
  76.7 0.4 collective-permute-start.10
  77.1 1.5 %collective-permute-start.11 = (bf16[2,18432]{1,0:T(2,128)(2,1)S(1)}, bf16[2,18432]{1,0:T(2,128)(2,1)S(1)}, u32[]{:S(2)}, u32[]{:S(2)}) collective-permute-start(bf16[2,18432]{1,0:T(2,128)(2,1)S(1)} %get-tuple-element.32), channel_id=1, source_target_pairs={{0,6},{1,7},{2,4},{3,5},{4,2},{5,3},{6,0},{7,1},{8,14},{9,15},{10,... | collective-permute-start | bytes 221192 | tf_op jit(solution)/shard_map/ppermute | solution.py:402
  78.6 4.4 %collective-permute-done.12.refs_0_ = bf16[2,2,18432]{2,1,0:T(2,128)(2,1)S(1)} collective-permute-done((bf16[2,2,18432]{2,1,0:T(2,128)(2,1)S(1)}, bf16[2,2,18432]{2,1,0:T(2,128)(2,1)S(1)}, u32[]{:S(2)}, u32[]{:S(2)}) %collective-permute-start.12) | collective-permute-done | bytes 147488 | tf_op jit(solution)/shard_map/ppermute | solution.py:402
  82.9 0.2 shard_map.125
  83.2 0.2 collective-permute-start.13
  83.4 1.5 %collective-permute-start.14 = (bf16[2,18432]{1,0:T(2,128)(2,1)S(1)}, bf16[2,18432]{1,0:T(2,128)(2,1)S(1)}, u32[]{:S(2)}, u32[]{:S(2)}) collective-permute-start(bf16[2,18432]{1,0:T(2,128)(2,1)S(1)} %get-tuple-element.36), channel_id=1, source_target_pairs={{0,12},{1,13},{2,14},{3,15},{4,8},{5,9},{6,10},{7,11},{8,4},{9,5},... | collective-permute-start | bytes 221192 | tf_op jit(solution)/shard_map/ppermute | solution.py:402
  84.8 0.0 collective-permute-done.9
  84.9 0.0 collective-permute-done.10
  84.9 0.0 collective-permute-done.11
  84.9 3.7 %collective-permute-done.13 = bf16[2,18432]{1,0:T(2,128)(2,1)S(1)} collective-permute-done((bf16[2,18432]{1,0:T(2,128)(2,1)S(1)}, bf16[2,18432]{1,0:T(2,128)(2,1)S(1)}, u32[]{:S(2)}, u32[]{:S(2)}) %collective-permute-start.13) | collective-permute-done | bytes 73760 | tf_op jit(solution)/shard_map/ppermute | solution.py:402
  88.5 1.1 %collective-permute-done.14 = bf16[2,18432]{1,0:T(2,128)(2,1)S(1)} collective-permute-done((bf16[2,18432]{1,0:T(2,128)(2,1)S(1)}, bf16[2,18432]{1,0:T(2,128)(2,1)S(1)}, u32[]{:S(2)}, u32[]{:S(2)}) %collective-permute-start.14) | collective-permute-done | bytes 73760 | tf_op jit(solution)/shard_map/ppermute | solution.py:402
  89.6 0.9 fusion.9
  (37 shorter events, 0.2 us)
Async XLA Ops:
  0.0 53.5 %copy-start = (bf16[1,1024,256]{2,1,0:T(8,128)(2,1)S(1)}, bf16[1,1024,256]{2,1,0:T(8,128)(2,1)}, u32[]{:S(2)}) copy-start(bf16[1,1024,256]{2,1,0:T(8,128)(2,1)} %param.20) | copy-start | bytes 1572868
  0.0 22.0 %slice-start = ((s8[21233664]{0:T(1024)(128)(4,1)}), s8[4194304]{0:T(1024)(128)(4,1)S(1)}, s32[]{:S(2)}) async-start(s8[21233664]{0:T(1024)(128)(4,1)} %bitcast.64), calls=%async_computation.2 | async-start | bytes 8388608
  0.0 1.0 %copy-start.4 = (bf16[2,1,18432]{2,0,1:T(2,128)(2,1)S(1)}, bf16[2,1,18432]{2,0,1:T(2,128)(2,1)}, u32[]{:S(2)}) copy-start(bf16[2,1,18432]{2,0,1:T(2,128)(2,1)} %param.12) | copy-start | bytes 221188
  1.0 1.3 %copy-start.3 = (f32[18432]{0:T(1024)S(1)}, f32[18432]{0:T(1024)}, u32[]{:S(2)}) copy-start(f32[18432]{0:T(1024)} %param.13) | copy-start | bytes 221188
  1.0 21.0 %slice-start.1 = ((s8[21233664]{0:T(1024)(128)(4,1)}), s8[4194304]{0:T(1024)(128)(4,1)S(1)}, s32[]{:S(2)}) async-start(s8[21233664]{0:T(1024)(128)(4,1)} %bitcast.64), calls=%async_computation.3 | async-start | bytes 8388608
  1.0 21.0 %slice-start.2 = ((s8[21233664]{0:T(1024)(128)(4,1)}), s8[4194304]{0:T(1024)(128)(4,1)S(1)}, s32[]{:S(2)}) async-start(s8[21233664]{0:T(1024)(128)(4,1)} %bitcast.64), calls=%async_computation.4 | async-start | bytes 8388608
  1.0 21.0 %slice-start.3 = ((s8[21233664]{0:T(1024)(128)(4,1)}), s8[4194304]{0:T(1024)(128)(4,1)S(1)}, s32[]{:S(2)}) async-start(s8[21233664]{0:T(1024)(128)(4,1)} %bitcast.64), calls=%async_computation.5 | async-start | bytes 8388608
  1.1 21.0 %slice-start.4 = ((s8[21233664]{0:T(1024)(128)(4,1)}), s8[4194304]{0:T(1024)(128)(4,1)S(1)}, s32[]{:S(2)}) async-start(s8[21233664]{0:T(1024)(128)(4,1)} %bitcast.64), calls=%async_computation.6 | async-start | bytes 8388608
  1.1 21.0 %slice-start.5 = ((s8[21233664]{0:T(1024)(128)(4,1)}), s8[262144]{0:T(1024)(128)(4,1)S(1)}, s32[]{:S(2)}) async-start(s8[21233664]{0:T(1024)(128)(4,1)} %bitcast.64), calls=%async_computation.7 | async-start | bytes 524288
  1.1 21.0 %copy-start.1 = (bf16[384,18432]{1,0:T(8,128)(2,1)S(1)}, bf16[384,18432]{1,0:T(8,128)(2,1)}, u32[]{:S(2)}) copy-start(bf16[384,18432]{1,0:T(8,128)(2,1)} %wq_ref.1) | copy-start | bytes 42467332
  1.1 21.0 %copy-start.2 = (bf16[32,18432]{1,0:T(8,128)(2,1)S(1)}, bf16[32,18432]{1,0:T(8,128)(2,1)}, u32[]{:S(2)}) copy-start(bf16[32,18432]{1,0:T(8,128)(2,1)} %wk_ref.1) | copy-start | bytes 3538948
  2.4 7.9 %collective-permute-start.5 = (bf16[2,18432]{1,0:T(2,128)(2,1)S(1)}, bf16[2,18432]{1,0:T(2,128)(2,1)S(1)}, u32[]{:S(2)}, u32[]{:S(2)}) collective-permute-start(bf16[2,18432]{1,0:T(2,128)(2,1)S(1)} %shard_map.119), channel_id=1, source_target_pairs={{0,12},{1,13},{2,14},{3,15},{4,8},{5,9},{6,10},{7,11},{8,4},{9,5},... | collective-permute-start | bytes 221192 | tf_op jit(solution)/shard_map/ppermute | solution.py:402
  7.5 6.2 %collective-permute-start.3 = (bf16[2,18432]{1,0:T(2,128)(2,1)S(1)}, bf16[2,18432]{1,0:T(2,128)(2,1)S(1)}, u32[]{:S(2)}, u32[]{:S(2)}) collective-permute-start(bf16[2,18432]{1,0:T(2,128)(2,1)S(1)} %shard_map.119), channel_id=1, source_target_pairs={{0,8},{1,9},{2,10},{3,11},{4,12},{5,13},{6,14},{7,15},{8,0},{9,1},... | collective-permute-start | bytes 221192 | tf_op jit(solution)/shard_map/ppermute | solution.py:402
  7.6 7.7 %collective-permute-start.1 = (bf16[2,18432]{1,0:T(2,128)(2,1)S(1)}, bf16[2,18432]{1,0:T(2,128)(2,1)S(1)}, u32[]{:S(2)}, u32[]{:S(2)}) collective-permute-start(bf16[2,18432]{1,0:T(2,128)(2,1)S(1)} %shard_map.119), channel_id=1, source_target_pairs={{0,4},{1,5},{2,6},{3,7},{4,0},{5,1},{6,2},{7,3},{8,12},{9,13},{10,... | collective-permute-start | bytes 221192 | tf_op jit(solution)/shard_map/ppermute | solution.py:402
  8.2 7.6 %collective-permute-start = (bf16[2,18432]{1,0:T(2,128)(2,1)S(1)}, bf16[2,18432]{1,0:T(2,128)(2,1)S(1)}, u32[]{:S(2)}, u32[]{:S(2)}) collective-permute-start(bf16[2,18432]{1,0:T(2,128)(2,1)S(1)} %shard_map.119), channel_id=1, source_target_pairs={{0,2},{1,3},{2,0},{3,1},{4,6},{5,7},{6,4},{7,5},{8,10},{9,11},{10,... | collective-permute-start | bytes 221192 | tf_op jit(solution)/shard_map/ppermute | solution.py:402
  10.3 9.6 %collective-permute-start.6 = (bf16[2,18432]{1,0:T(2,128)(2,1)S(1)}, bf16[2,18432]{1,0:T(2,128)(2,1)S(1)}, u32[]{:S(2)}, u32[]{:S(2)}) collective-permute-start(bf16[2,18432]{1,0:T(2,128)(2,1)S(1)} %collective-permute-done.5), channel_id=1, source_target_pairs={{0,2},{1,3},{2,0},{3,1},{4,6},{5,7},{6,4},{7,5},{8,10},{9,11},{10,... | collective-permute-start | bytes 221192 | tf_op jit(solution)/shard_map/ppermute | solution.py:402
  13.8 6.0 %collective-permute-start.4 = (bf16[2,18432]{1,0:T(2,128)(2,1)S(1)}, bf16[2,18432]{1,0:T(2,128)(2,1)S(1)}, u32[]{:S(2)}, u32[]{:S(2)}) collective-permute-start(bf16[2,18432]{1,0:T(2,128)(2,1)S(1)} %collective-permute-done.3), channel_id=1, source_target_pairs={{0,2},{1,3},{2,0},{3,1},{4,6},{5,7},{6,4},{7,5},{8,10},{9,11},{10,... | collective-permute-start | bytes 221192 | tf_op jit(solution)/shard_map/ppermute | solution.py:402
  15.3 4.4 %collective-permute-start.2 = (bf16[2,18432]{1,0:T(2,128)(2,1)S(1)}, bf16[2,18432]{1,0:T(2,128)(2,1)S(1)}, u32[]{:S(2)}, u32[]{:S(2)}) collective-permute-start(bf16[2,18432]{1,0:T(2,128)(2,1)S(1)} %collective-permute-done.1), channel_id=1, source_target_pairs={{0,2},{1,3},{2,0},{3,1},{4,6},{5,7},{6,4},{7,5},{8,10},{9,11},{10,... | collective-permute-start | bytes 221192 | tf_op jit(solution)/shard_map/ppermute | solution.py:402
  20.0 2.1 %collective-permute-start.7 = (bf16[8,2,18432]{2,1,0:T(2,128)(2,1)S(1)}, bf16[8,2,18432]{2,1,0:T(2,128)(2,1)S(1)}, u32[]{:S(2)}, u32[]{:S(2)}) collective-permute-start(bf16[8,2,18432]{2,1,0:T(2,128)(2,1)S(1)} %bitcast_dynamic-update-slice_fusion.even_ref), channel_id=1, source_target_pairs={{0,1},{1,0},{2,3},{3,2},{4,5},{5,4},{6,7},{7,6},{8,9},{9,8},{10,11... | collective-permute-start | bytes 1769480 | tf_op jit(solution)/shard_map/ppermute | solution.py:402
  41.8 12.4 %copy-start.6 = (bf16[1,1024,256]{2,1,0:T(8,128)(2,1)S(1)}, bf16[1,1024,256]{2,1,0:T(8,128)(2,1)}, u32[]{:S(2)}) copy-start(bf16[1,1024,256]{2,1,0:T(8,128)(2,1)} %param.21) | copy-start | bytes 1572868
  41.9 11.4 %all-to-all-start = ((f32[16,2,416]{2,1,0:T(2,128)}), f32[16,2,416]{2,1,0:T(2,128)S(1)}, u32[]{:S(2)}, u32[]{:S(2)}) async-start(f32[16,2,416]{2,1,0:T(2,128)} %get-tuple-element.21), calls=%async_computation | async-start | bytes 131072 | tf_op jit(solution)/shard_map/all_to_all | solution.py:457
  55.4 10.5 %all-to-all-start.1 = ((bf16[16,2,384]{2,1,0:T(2,128)(2,1)}), bf16[16,2,384]{2,1,0:T(2,128)(2,1)S(1)}, u32[]{:S(2)}, u32[]{:S(2)}) async-start(bf16[16,2,384]{2,1,0:T(2,128)(2,1)} %bitcast.61), calls=%async_computation.1 | async-start | bytes 49152 | tf_op jit(solution)/shard_map/all_to_all | solution.py:470
  64.1 25.5 %copy-start.5 = (bf16[2,1,18432]{2,0,1:T(2,128)(2,1)S(1)}, bf16[2,1,18432]{2,0,1:T(2,128)(2,1)}, u32[]{:S(2)}) copy-start(bf16[2,1,18432]{2,0,1:T(2,128)(2,1)} %param.12) | copy-start | bytes 221188
  72.1 2.1 %collective-permute-start.8 = (bf16[16,18432]{1,0:T(8,128)(2,1)S(1)}, bf16[16,18432]{1,0:T(8,128)(2,1)S(1)}, u32[]{:S(2)}, u32[]{:S(2)}) collective-permute-start(bf16[16,18432]{1,0:T(8,128)(2,1)S(1)} %get-tuple-element.28), channel_id=1, source_target_pairs={{0,1},{1,0},{2,3},{3,2},{4,5},{5,4},{6,7},{7,6},{8,9},{9,8},{10,11... | collective-permute-start | bytes 1769480 | tf_op jit(solution)/shard_map/ppermute | solution.py:402
  74.6 8.3 %collective-permute-start.12 = (bf16[2,2,18432]{2,1,0:T(2,128)(2,1)S(1)}, bf16[2,2,18432]{2,1,0:T(2,128)(2,1)S(1)}, u32[]{:S(2)}, u32[]{:S(2)}) collective-permute-start(bf16[2,2,18432]{2,1,0:T(2,128)(2,1)S(1)} %get-tuple-element.34), channel_id=1, source_target_pairs={{0,2},{1,3},{2,0},{3,1},{4,6},{5,7},{6,4},{7,5},{8,10},{9,11},{10,... | collective-permute-start | bytes 442376 | tf_op jit(solution)/shard_map/ppermute | solution.py:402
  75.1 9.8 %collective-permute-start.9 = (bf16[2,18432]{1,0:T(2,128)(2,1)S(1)}, bf16[2,18432]{1,0:T(2,128)(2,1)S(1)}, u32[]{:S(2)}, u32[]{:S(2)}) collective-permute-start(bf16[2,18432]{1,0:T(2,128)(2,1)S(1)} %get-tuple-element.30), channel_id=1, source_target_pairs={{0,2},{1,3},{2,0},{3,1},{4,6},{5,7},{6,4},{7,5},{8,10},{9,11},{10,... | collective-permute-start | bytes 221192 | tf_op jit(solution)/shard_map/ppermute | solution.py:402
  76.7 8.1 %collective-permute-start.10 = (bf16[2,18432]{1,0:T(2,128)(2,1)S(1)}, bf16[2,18432]{1,0:T(2,128)(2,1)S(1)}, u32[]{:S(2)}, u32[]{:S(2)}) collective-permute-start(bf16[2,18432]{1,0:T(2,128)(2,1)S(1)} %get-tuple-element.31), channel_id=1, source_target_pairs={{0,4},{1,5},{2,6},{3,7},{4,0},{5,1},{6,2},{7,3},{8,12},{9,13},{10,... | collective-permute-start | bytes 221192 | tf_op jit(solution)/shard_map/ppermute | solution.py:402
  77.1 7.7 %collective-permute-start.11 = (bf16[2,18432]{1,0:T(2,128)(2,1)S(1)}, bf16[2,18432]{1,0:T(2,128)(2,1)S(1)}, u32[]{:S(2)}, u32[]{:S(2)}) collective-permute-start(bf16[2,18432]{1,0:T(2,128)(2,1)S(1)} %get-tuple-element.32), channel_id=1, source_target_pairs={{0,6},{1,7},{2,4},{3,5},{4,2},{5,3},{6,0},{7,1},{8,14},{9,15},{10,... | collective-permute-start | bytes 221192 | tf_op jit(solution)/shard_map/ppermute | solution.py:402
  83.2 5.3 %collective-permute-start.13 = (bf16[2,18432]{1,0:T(2,128)(2,1)S(1)}, bf16[2,18432]{1,0:T(2,128)(2,1)S(1)}, u32[]{:S(2)}, u32[]{:S(2)}) collective-permute-start(bf16[2,18432]{1,0:T(2,128)(2,1)S(1)} %get-tuple-element.35), channel_id=1, source_target_pairs={{0,8},{1,9},{2,10},{3,11},{4,12},{5,13},{6,14},{7,15},{8,0},{9,1},... | collective-permute-start | bytes 221192 | tf_op jit(solution)/shard_map/ppermute | solution.py:402
  83.4 6.3 %collective-permute-start.14 = (bf16[2,18432]{1,0:T(2,128)(2,1)S(1)}, bf16[2,18432]{1,0:T(2,128)(2,1)S(1)}, u32[]{:S(2)}, u32[]{:S(2)}) collective-permute-start(bf16[2,18432]{1,0:T(2,128)(2,1)S(1)} %get-tuple-element.36), channel_id=1, source_target_pairs={{0,12},{1,13},{2,14},{3,15},{4,8},{5,9},{6,10},{7,11},{8,4},{9,5},... | collective-permute-start | bytes 221192 | tf_op jit(solution)/shard_map/ppermute | solution.py:402

commit v7 on v6

--- a/solution.py
+++ b/solution.py
@@ -64,7 +64,7 @@
 
 def project_kernel(
     chunks, even_ref, odd_ref, wq_ref, wg_ref, wu_ref, wk_ref, out_ref, hidden_ref,
-    rows, acc, sem_u, sem_k, *streams,
+    rows, acc, query, gate, sem_u, sem_k, *streams,
 ):
     half, steps, width = even_ref.shape
     step = width // chunks
@@ -97,8 +97,6 @@
         for copy in pair:
             copy.start()
     acc[...] = jnp.zeros_like(acc)
-    query = jnp.zeros((rows.shape[0], q_cols), F32)
-    gate = jnp.zeros((rows.shape[0], units), F32)
     for c in range(chunks):
         part = slice(c * step, (c + 1) * step)
         for p in range(half):
@@ -106,8 +104,9 @@
             q = half + p
             rows[q * steps : (q + 1) * steps, part] = odd_ref[p, :, part]
         block = rows[:, part]
-        query += lax.dot_general(block, wq_ref[:, part], NT, preferred_element_type=F32)
-        gate += lax.dot_general(block, wg_ref[:, part], NT, preferred_element_type=F32)
+        for total, weight in ((query, wq_ref), (gate, wg_ref)):
+            product = lax.dot_general(block, weight[:, part], NT, preferred_element_type=F32)
+            total[...] = product if c == 0 else total[...] + product
     for c in range(chunks):
         for copy in copies[c]:
             copy.wait()
@@ -124,9 +123,9 @@
     me = lax.axis_index("gx")
     for p in range(2 * half):
         owner = lax.bitwise_xor(me, slot_at(p, half))
-        out_ref[owner, :, :q_cols] = query[p * steps : (p + 1) * steps]
+        out_ref[owner, :, :q_cols] = query[p * steps : (p + 1) * steps, :]
         out_ref[owner, :, q_cols:] = acc[p * steps : (p + 1) * steps, units:]
-    hidden_ref[...] = (jax.nn.silu(gate) * acc[:, :units]).astype(BF16)
+    hidden_ref[...] = (jax.nn.silu(gate[...]) * acc[:, :units]).astype(BF16)
 
 
 def project(even, odd, w_query, w_keyval, w_gate, w_up):
@@ -152,6 +151,8 @@
         scratch_shapes=[
             pltpu.VMEM((n, width), BF16),
             pltpu.VMEM((n, units + k_cols), F32),
+            pltpu.VMEM((n, q_cols), F32),
+            pltpu.VMEM((n, units), F32),
             pltpu.SemaphoreType.DMA((chunks,)),
             pltpu.SemaphoreType.DMA((chunks,)),
         ]

time: 90.8 us -> 90 us (level)
  no operation moved by 1% of the time
where the time goes in v7:
time: 90 us; the launch traced here: 89.8 us
  Pallas kernels  36 us (40%)
  starting transfers between devices  25.4 us (28%)
  waiting for transfers between devices  21.2 us (24%)
  local copies, waits for them, and re-layouts  3.13 us (3%)
  between operations  1.63 us (2%)
  other arithmetic  1.37 us (2%)
  matrix products  0.98 us (1%)
    pallas_call x1, Pallas kernels, project(): pl.pallas_call(functools.partial(project_kernel, chunks), in_specs=[VMEM,...  19 us
    ppermute x15, waiting for transfers between devices, swap(): return lax.ppermute(value, 'gx', [(i, i ^ bits) for i in range(devices)])  17.4 us
    ppermute x15, starting transfers between devices, swap(): return lax.ppermute(value, 'gx', [(i, i ^ bits) for i in range(devices)])  17 us
    pallas_call x2, Pallas kernels, down_part(): pl.pallas_call(functools.partial(down_kernel, chunks, first * step), in_s...  9.56 us
    pallas_call x1, Pallas kernels, branch_parts(): pl.pallas_call(functools.partial(branch_kernel, chunks), in_specs=[VMEM,...  6.15 us
    all_to_all x1, starting transfers between devices, local(): lax.all_to_all(projected, 'gx', split_axis=0, concat_axis=0, tiled=True)  4.47 us
    all_to_all x1, starting transfers between devices, local(): lax.all_to_all(attended, 'gx', split_axis=0, concat_axis=0, tiled=True)  3.93 us
    unnamed x33, local copies, waits for them, and re-layouts  2.28 us
  transfers between devices with their start and end apart: 17, of which 10 were waited for; matrix products, arithmetic and copies ran while one was open for 1% of the time, Pallas kernels for 11%

profile of v7, /device:TPU:0, one launch (start us, length us, event | category | flops | bytes accessed | tf_op | source)
XLA Modules:
  0.0 89.8 jit_solution(2435584665076741363)
XLA Ops:
  0.0 1.0 %copy-done.4 = bf16[2,1,18432]{2,0,1:T(2,128)(2,1)S(1)} copy-done((bf16[2,1,18432]{2,0,1:T(2,128)(2,1)S(1)}, bf16[2,1,18432]{2,0,1:T(2,128)(2,1)}, u32[]{:S(2)}) %copy-start.4) | copy-done | bytes 73752
  1.1 0.0 slice-start.4
  1.1 0.0 slice-start.5
  1.1 0.5 shard_map.118.values_ref
  1.6 0.8 copy-done.3
  2.3 0.1 shard_map.119
  2.4 5.1 %collective-permute-start.5 = (bf16[2,18432]{1,0:T(2,128)(2,1)S(1)}, bf16[2,18432]{1,0:T(2,128)(2,1)S(1)}, u32[]{:S(2)}, u32[]{:S(2)}) collective-permute-start(bf16[2,18432]{1,0:T(2,128)(2,1)S(1)} %shard_map.119), channel_id=1, source_target_pairs={{0,12},{1,13},{2,14},{3,15},{4,8},{5,9},{6,10},{7,11},{8,4},{9,5},... | collective-permute-start | bytes 221192 | tf_op jit(solution)/shard_map/ppermute | solution.py:403
  7.5 0.0 collective-permute-start.3
  7.6 0.6 collective-permute-start.1
  8.2 1.6 %collective-permute-start = (bf16[2,18432]{1,0:T(2,128)(2,1)S(1)}, bf16[2,18432]{1,0:T(2,128)(2,1)S(1)}, u32[]{:S(2)}, u32[]{:S(2)}) collective-permute-start(bf16[2,18432]{1,0:T(2,128)(2,1)S(1)} %shard_map.119), channel_id=1, source_target_pairs={{0,2},{1,3},{2,0},{3,1},{4,6},{5,7},{6,4},{7,5},{8,10},{9,11},{10,... | collective-permute-start | bytes 221192 | tf_op jit(solution)/shard_map/ppermute | solution.py:403
  9.8 0.1 bitcast_dynamic-update-slice_fusion.7
  9.9 0.4 collective-permute-done.5
  10.3 1.9 %collective-permute-start.6 = (bf16[2,18432]{1,0:T(2,128)(2,1)S(1)}, bf16[2,18432]{1,0:T(2,128)(2,1)S(1)}, u32[]{:S(2)}, u32[]{:S(2)}) collective-permute-start(bf16[2,18432]{1,0:T(2,128)(2,1)S(1)} %collective-permute-done.5), channel_id=1, source_target_pairs={{0,2},{1,3},{2,0},{3,1},{4,6},{5,7},{6,4},{7,5},{8,10},{9,11},{10,... | collective-permute-start | bytes 221192 | tf_op jit(solution)/shard_map/ppermute | solution.py:403
  12.2 1.6 %collective-permute-done.3 = bf16[2,18432]{1,0:T(2,128)(2,1)S(1)} collective-permute-done((bf16[2,18432]{1,0:T(2,128)(2,1)S(1)}, bf16[2,18432]{1,0:T(2,128)(2,1)S(1)}, u32[]{:S(2)}, u32[]{:S(2)}) %collective-permute-start.3) | collective-permute-done | bytes 73760 | tf_op jit(solution)/shard_map/ppermute | solution.py:403
  13.8 1.5 %collective-permute-start.4 = (bf16[2,18432]{1,0:T(2,128)(2,1)S(1)}, bf16[2,18432]{1,0:T(2,128)(2,1)S(1)}, u32[]{:S(2)}, u32[]{:S(2)}) collective-permute-start(bf16[2,18432]{1,0:T(2,128)(2,1)S(1)} %collective-permute-done.3), channel_id=1, source_target_pairs={{0,2},{1,3},{2,0},{3,1},{4,6},{5,7},{6,4},{7,5},{8,10},{9,11},{10,... | collective-permute-start | bytes 221192 | tf_op jit(solution)/shard_map/ppermute | solution.py:403
  15.3 0.0 collective-permute-done.1
  15.3 0.5 collective-permute-start.2
  15.8 0.0 collective-permute-done
  15.8 0.1 bitcast_dynamic-update-slice_fusion.6
  15.9 0.1 bitcast_dynamic-update-slice_fusion.5
  15.9 3.7 %collective-permute-done.2 = bf16[2,18432]{1,0:T(2,128)(2,1)S(1)} collective-permute-done((bf16[2,18432]{1,0:T(2,128)(2,1)S(1)}, bf16[2,18432]{1,0:T(2,128)(2,1)S(1)}, u32[]{:S(2)}, u32[]{:S(2)}) %collective-permute-start.2) | collective-permute-done | bytes 73760 | tf_op jit(solution)/shard_map/ppermute | solution.py:403
  19.6 0.1 bitcast_dynamic-update-slice_fusion.4
  19.7 0.1 bitcast_dynamic-update-slice_fusion.3
  19.7 0.0 collective-permute-done.4
  19.8 0.1 bitcast_dynamic-update-slice_fusion.2
  19.8 0.1 bitcast_dynamic-update-slice_fusion.1
  19.9 0.0 collective-permute-done.6
  19.9 0.1 bitcast_dynamic-update-slice_fusion.even_ref
  20.0 0.1 collective-permute-start.7
  21.4 0.1 multiply_cosine_fusion.1
  21.5 0.5 collective-permute-done.7.odd_ref
  22.1 19.0 %shard_map.120 = (f32[16,2,416]{2,1,0:T(2,128)}, bf16[32,576]{1,0:T(8,128)(2,1)S(1)}) custom-call(bf16[8,2,18432]{2,1,0:T(2,128)(2,1)S(1)} %bitcast_dynamic-update-slice_fusion.even_ref, bf16[8,2,18432]{2,1,0:T(2,128)(2,1)S(1)} %collective-permute-done.7.odd_ref, bf16[384,18432]{1,0:T(8,128)(2,1)S(1)} %copy-done.1, bf16[576,18432]{1,0:T(8,128)(2,1)S(1)} %bitcast.65, ...), custom_call_target="tpu_custom_call" | custom-call | flops 1849688064 | bytes 57802752 | tf_op jit(solution)/shard_map/pallas_call | solution.py:143
  41.1 0.0 copy-start.6
  41.1 4.5 %all-to-all-start = ((f32[16,2,416]{2,1,0:T(2,128)}), f32[16,2,416]{2,1,0:T(2,128)S(1)}, u32[]{:S(2)}, u32[]{:S(2)}) async-start(f32[16,2,416]{2,1,0:T(2,128)} %get-tuple-element.21), calls=%async_computation | async-start | bytes 131072 | tf_op jit(solution)/shard_map/all_to_all | solution.py:458
  45.6 4.8 %shard_map.121.first_ref = f32[32,9216]{1,0:T(8,128)S(1)} custom-call(bf16[32,576]{1,0:T(8,128)(2,1)S(1)} %get-tuple-element.26.hidden_ref, bf16[576,18432]{1,0:T(8,128)(2,1)} %w_ref.4), custom_call_target="tpu_custom_call" | custom-call | flops 339738624 | bytes 10616832 | tf_op jit(solution)/shard_map/pallas_call | solution.py:196
  50.4 2.1 %all-to-all-done = f32[16,2,416]{2,1,0:T(2,128)S(1)} async-done(((f32[16,2,416]{2,1,0:T(2,128)}), f32[16,2,416]{2,1,0:T(2,128)S(1)}, u32[]{:S(2)}, u32[]{:S(2)}) %all-to-all-start) | async-done | bytes 53280 | tf_op jit(solution)/shard_map/all_to_all | solution.py:458
  52.6 0.1 reshape.338
  52.7 0.1 fusion.27
  52.8 0.4 fusion.31
  53.1 0.2 fusion.32
  53.4 0.2 fusion.6
  53.6 0.3 fusion.3
  53.8 0.2 fusion.1
  54.1 0.6 copy.17
  54.7 3.9 %all-to-all-start.1 = ((bf16[16,2,384]{2,1,0:T(2,128)(2,1)}), bf16[16,2,384]{2,1,0:T(2,128)(2,1)S(1)}, u32[]{:S(2)}, u32[]{:S(2)}) async-start(bf16[16,2,384]{2,1,0:T(2,128)(2,1)} %bitcast.61), calls=%async_computation.1 | async-start | bytes 49152 | tf_op jit(solution)/shard_map/all_to_all | solution.py:471
  58.6 4.8 %shard_map.122.second_ref = f32[32,9216]{1,0:T(8,128)S(1)} custom-call(bf16[32,576]{1,0:T(8,128)(2,1)S(1)} %get-tuple-element.26.hidden_ref, bf16[576,18432]{1,0:T(8,128)(2,1)} %w_ref.4), custom_call_target="tpu_custom_call" | custom-call | flops 339738624 | bytes 10616832 | tf_op jit(solution)/shard_map/pallas_call | solution.py:196
  63.4 0.0 copy-start.5
  63.4 1.8 %all-to-all-done.1.attended_ref = bf16[16,2,384]{2,1,0:T(2,128)(2,1)S(1)} async-done(((bf16[16,2,384]{2,1,0:T(2,128)(2,1)}), bf16[16,2,384]{2,1,0:T(2,128)(2,1)S(1)}, u32[]{:S(2)}, u32[]{:S(2)}) %all-to-all-start.1) | async-done | bytes 24608 | tf_op jit(solution)/shard_map/all_to_all | solution.py:471
  65.2 6.2 %shard_map.123 = (f32[16,18432]{1,0:T(8,128)S(1)}, bf16[16,18432]{1,0:T(8,128)(2,1)S(1)}) custom-call(bf16[16,2,384]{2,1,0:T(2,128)(2,1)S(1)} %all-to-all-done.1.attended_ref, f32[32,9216]{1,0:T(8,128)S(1)} %shard_map.121.first_ref, f32[32,9216]{1,0:T(8,128)S(1)} %shard_map.122.second_ref, bf16[384,18432]{1,0:T(8,128)(2,1)} %w_ref.5), custom_call_target="tpu_custom_call" | custom-call | flops 452984832 | bytes 14155776 | tf_op jit(solution)/shard_map/pallas_call | solution.py:270
  71.4 0.1 collective-permute-start.8
  71.4 2.0 %collective-permute-done.8.came_ref = bf16[16,18432]{1,0:T(8,128)(2,1)S(1)} collective-permute-done((bf16[16,18432]{1,0:T(8,128)(2,1)S(1)}, bf16[16,18432]{1,0:T(8,128)(2,1)S(1)}, u32[]{:S(2)}, u32[]{:S(2)}) %collective-permute-start.8) | collective-permute-done | bytes 589856 | tf_op jit(solution)/shard_map/ppermute | solution.py:403
  73.4 0.5 shard_map.124
  73.9 0.5 collective-permute-start.12
  74.4 1.6 %collective-permute-start.9 = (bf16[2,18432]{1,0:T(2,128)(2,1)S(1)}, bf16[2,18432]{1,0:T(2,128)(2,1)S(1)}, u32[]{:S(2)}, u32[]{:S(2)}) collective-permute-start(bf16[2,18432]{1,0:T(2,128)(2,1)S(1)} %get-tuple-element.30), channel_id=1, source_target_pairs={{0,2},{1,3},{2,0},{3,1},{4,6},{5,7},{6,4},{7,5},{8,10},{9,11},{10,... | collective-permute-start | bytes 221192 | tf_op jit(solution)/shard_map/ppermute | solution.py:403
  76.0 0.4 collective-permute-start.10
  76.4 1.5 %collective-permute-start.11 = (bf16[2,18432]{1,0:T(2,128)(2,1)S(1)}, bf16[2,18432]{1,0:T(2,128)(2,1)S(1)}, u32[]{:S(2)}, u32[]{:S(2)}) collective-permute-start(bf16[2,18432]{1,0:T(2,128)(2,1)S(1)} %get-tuple-element.32), channel_id=1, source_target_pairs={{0,6},{1,7},{2,4},{3,5},{4,2},{5,3},{6,0},{7,1},{8,14},{9,15},{10,... | collective-permute-start | bytes 221192 | tf_op jit(solution)/shard_map/ppermute | solution.py:403
  77.8 4.4 %collective-permute-done.12.refs_0_ = bf16[2,2,18432]{2,1,0:T(2,128)(2,1)S(1)} collective-permute-done((bf16[2,2,18432]{2,1,0:T(2,128)(2,1)S(1)}, bf16[2,2,18432]{2,1,0:T(2,128)(2,1)S(1)}, u32[]{:S(2)}, u32[]{:S(2)}) %collective-permute-start.12) | collective-permute-done | bytes 147488 | tf_op jit(solution)/shard_map/ppermute | solution.py:403
  82.2 0.2 shard_map.125
  82.5 0.2 collective-permute-start.13
  82.6 1.5 %collective-permute-start.14 = (bf16[2,18432]{1,0:T(2,128)(2,1)S(1)}, bf16[2,18432]{1,0:T(2,128)(2,1)S(1)}, u32[]{:S(2)}, u32[]{:S(2)}) collective-permute-start(bf16[2,18432]{1,0:T(2,128)(2,1)S(1)} %get-tuple-element.36), channel_id=1, source_target_pairs={{0,12},{1,13},{2,14},{3,15},{4,8},{5,9},{6,10},{7,11},{8,4},{9,5},... | collective-permute-start | bytes 221192 | tf_op jit(solution)/shard_map/ppermute | solution.py:403
  84.1 0.0 collective-permute-done.9
  84.1 3.7 %collective-permute-done.13 = bf16[2,18432]{1,0:T(2,128)(2,1)S(1)} collective-permute-done((bf16[2,18432]{1,0:T(2,128)(2,1)S(1)}, bf16[2,18432]{1,0:T(2,128)(2,1)S(1)}, u32[]{:S(2)}, u32[]{:S(2)}) %collective-permute-start.13) | collective-permute-done | bytes 73760 | tf_op jit(solution)/shard_map/ppermute | solution.py:403
  87.8 1.1 %collective-permute-done.14 = bf16[2,18432]{1,0:T(2,128)(2,1)S(1)} collective-permute-done((bf16[2,18432]{1,0:T(2,128)(2,1)S(1)}, bf16[2,18432]{1,0:T(2,128)(2,1)S(1)}, u32[]{:S(2)}, u32[]{:S(2)}) %collective-permute-start.14) | collective-permute-done | bytes 73760 | tf_op jit(solution)/shard_map/ppermute | solution.py:403
  88.9 0.9 fusion.9
  (37 shorter events, 0.2 us)
Async XLA Ops:
  0.0 52.8 %copy-start = (bf16[1,1024,256]{2,1,0:T(8,128)(2,1)S(1)}, bf16[1,1024,256]{2,1,0:T(8,128)(2,1)}, u32[]{:S(2)}) copy-start(bf16[1,1024,256]{2,1,0:T(8,128)(2,1)} %param.20) | copy-start | bytes 1572868
  0.0 22.0 %slice-start = ((s8[21233664]{0:T(1024)(128)(4,1)}), s8[4194304]{0:T(1024)(128)(4,1)S(1)}, s32[]{:S(2)}) async-start(s8[21233664]{0:T(1024)(128)(4,1)} %bitcast.64), calls=%async_computation.2 | async-start | bytes 8388608
  0.0 1.0 %copy-start.4 = (bf16[2,1,18432]{2,0,1:T(2,128)(2,1)S(1)}, bf16[2,1,18432]{2,0,1:T(2,128)(2,1)}, u32[]{:S(2)}) copy-start(bf16[2,1,18432]{2,0,1:T(2,128)(2,1)} %param.12) | copy-start | bytes 221188
  1.0 1.3 %copy-start.3 = (f32[18432]{0:T(1024)S(1)}, f32[18432]{0:T(1024)}, u32[]{:S(2)}) copy-start(f32[18432]{0:T(1024)} %param.13) | copy-start | bytes 221188
  1.0 21.0 %slice-start.1 = ((s8[21233664]{0:T(1024)(128)(4,1)}), s8[4194304]{0:T(1024)(128)(4,1)S(1)}, s32[]{:S(2)}) async-start(s8[21233664]{0:T(1024)(128)(4,1)} %bitcast.64), calls=%async_computation.3 | async-start | bytes 8388608
  1.0 21.0 %slice-start.2 = ((s8[21233664]{0:T(1024)(128)(4,1)}), s8[4194304]{0:T(1024)(128)(4,1)S(1)}, s32[]{:S(2)}) async-start(s8[21233664]{0:T(1024)(128)(4,1)} %bitcast.64), calls=%async_computation.4 | async-start | bytes 8388608
  1.0 21.0 %slice-start.3 = ((s8[21233664]{0:T(1024)(128)(4,1)}), s8[4194304]{0:T(1024)(128)(4,1)S(1)}, s32[]{:S(2)}) async-start(s8[21233664]{0:T(1024)(128)(4,1)} %bitcast.64), calls=%async_computation.5 | async-start | bytes 8388608
  1.1 21.0 %slice-start.4 = ((s8[21233664]{0:T(1024)(128)(4,1)}), s8[4194304]{0:T(1024)(128)(4,1)S(1)}, s32[]{:S(2)}) async-start(s8[21233664]{0:T(1024)(128)(4,1)} %bitcast.64), calls=%async_computation.6 | async-start | bytes 8388608
  1.1 21.0 %slice-start.5 = ((s8[21233664]{0:T(1024)(128)(4,1)}), s8[262144]{0:T(1024)(128)(4,1)S(1)}, s32[]{:S(2)}) async-start(s8[21233664]{0:T(1024)(128)(4,1)} %bitcast.64), calls=%async_computation.7 | async-start | bytes 524288
  1.1 21.0 %copy-start.1 = (bf16[384,18432]{1,0:T(8,128)(2,1)S(1)}, bf16[384,18432]{1,0:T(8,128)(2,1)}, u32[]{:S(2)}) copy-start(bf16[384,18432]{1,0:T(8,128)(2,1)} %wq_ref.1) | copy-start | bytes 42467332
  1.1 21.0 %copy-start.2 = (bf16[32,18432]{1,0:T(8,128)(2,1)S(1)}, bf16[32,18432]{1,0:T(8,128)(2,1)}, u32[]{:S(2)}) copy-start(bf16[32,18432]{1,0:T(8,128)(2,1)} %wk_ref.1) | copy-start | bytes 3538948
  2.4 7.9 %collective-permute-start.5 = (bf16[2,18432]{1,0:T(2,128)(2,1)S(1)}, bf16[2,18432]{1,0:T(2,128)(2,1)S(1)}, u32[]{:S(2)}, u32[]{:S(2)}) collective-permute-start(bf16[2,18432]{1,0:T(2,128)(2,1)S(1)} %shard_map.119), channel_id=1, source_target_pairs={{0,12},{1,13},{2,14},{3,15},{4,8},{5,9},{6,10},{7,11},{8,4},{9,5},... | collective-permute-start | bytes 221192 | tf_op jit(solution)/shard_map/ppermute | solution.py:403
  7.5 6.2 %collective-permute-start.3 = (bf16[2,18432]{1,0:T(2,128)(2,1)S(1)}, bf16[2,18432]{1,0:T(2,128)(2,1)S(1)}, u32[]{:S(2)}, u32[]{:S(2)}) collective-permute-start(bf16[2,18432]{1,0:T(2,128)(2,1)S(1)} %shard_map.119), channel_id=1, source_target_pairs={{0,8},{1,9},{2,10},{3,11},{4,12},{5,13},{6,14},{7,15},{8,0},{9,1},... | collective-permute-start | bytes 221192 | tf_op jit(solution)/shard_map/ppermute | solution.py:403
  7.6 7.7 %collective-permute-start.1 = (bf16[2,18432]{1,0:T(2,128)(2,1)S(1)}, bf16[2,18432]{1,0:T(2,128)(2,1)S(1)}, u32[]{:S(2)}, u32[]{:S(2)}) collective-permute-start(bf16[2,18432]{1,0:T(2,128)(2,1)S(1)} %shard_map.119), channel_id=1, source_target_pairs={{0,4},{1,5},{2,6},{3,7},{4,0},{5,1},{6,2},{7,3},{8,12},{9,13},{10,... | collective-permute-start | bytes 221192 | tf_op jit(solution)/shard_map/ppermute | solution.py:403
  8.2 7.6 %collective-permute-start = (bf16[2,18432]{1,0:T(2,128)(2,1)S(1)}, bf16[2,18432]{1,0:T(2,128)(2,1)S(1)}, u32[]{:S(2)}, u32[]{:S(2)}) collective-permute-start(bf16[2,18432]{1,0:T(2,128)(2,1)S(1)} %shard_map.119), channel_id=1, source_target_pairs={{0,2},{1,3},{2,0},{3,1},{4,6},{5,7},{6,4},{7,5},{8,10},{9,11},{10,... | collective-permute-start | bytes 221192 | tf_op jit(solution)/shard_map/ppermute | solution.py:403
  10.3 9.6 %collective-permute-start.6 = (bf16[2,18432]{1,0:T(2,128)(2,1)S(1)}, bf16[2,18432]{1,0:T(2,128)(2,1)S(1)}, u32[]{:S(2)}, u32[]{:S(2)}) collective-permute-start(bf16[2,18432]{1,0:T(2,128)(2,1)S(1)} %collective-permute-done.5), channel_id=1, source_target_pairs={{0,2},{1,3},{2,0},{3,1},{4,6},{5,7},{6,4},{7,5},{8,10},{9,11},{10,... | collective-permute-start | bytes 221192 | tf_op jit(solution)/shard_map/ppermute | solution.py:403
  13.8 6.0 %collective-permute-start.4 = (bf16[2,18432]{1,0:T(2,128)(2,1)S(1)}, bf16[2,18432]{1,0:T(2,128)(2,1)S(1)}, u32[]{:S(2)}, u32[]{:S(2)}) collective-permute-start(bf16[2,18432]{1,0:T(2,128)(2,1)S(1)} %collective-permute-done.3), channel_id=1, source_target_pairs={{0,2},{1,3},{2,0},{3,1},{4,6},{5,7},{6,4},{7,5},{8,10},{9,11},{10,... | collective-permute-start | bytes 221192 | tf_op jit(solution)/shard_map/ppermute | solution.py:403
  15.3 4.4 %collective-permute-start.2 = (bf16[2,18432]{1,0:T(2,128)(2,1)S(1)}, bf16[2,18432]{1,0:T(2,128)(2,1)S(1)}, u32[]{:S(2)}, u32[]{:S(2)}) collective-permute-start(bf16[2,18432]{1,0:T(2,128)(2,1)S(1)} %collective-permute-done.1), channel_id=1, source_target_pairs={{0,2},{1,3},{2,0},{3,1},{4,6},{5,7},{6,4},{7,5},{8,10},{9,11},{10,... | collective-permute-start | bytes 221192 | tf_op jit(solution)/shard_map/ppermute | solution.py:403
  20.0 2.1 %collective-permute-start.7 = (bf16[8,2,18432]{2,1,0:T(2,128)(2,1)S(1)}, bf16[8,2,18432]{2,1,0:T(2,128)(2,1)S(1)}, u32[]{:S(2)}, u32[]{:S(2)}) collective-permute-start(bf16[8,2,18432]{2,1,0:T(2,128)(2,1)S(1)} %bitcast_dynamic-update-slice_fusion.even_ref), channel_id=1, source_target_pairs={{0,1},{1,0},{2,3},{3,2},{4,5},{5,4},{6,7},{7,6},{8,9},{9,8},{10,11... | collective-permute-start | bytes 1769480 | tf_op jit(solution)/shard_map/ppermute | solution.py:403
  41.1 12.4 %copy-start.6 = (bf16[1,1024,256]{2,1,0:T(8,128)(2,1)S(1)}, bf16[1,1024,256]{2,1,0:T(8,128)(2,1)}, u32[]{:S(2)}) copy-start(bf16[1,1024,256]{2,1,0:T(8,128)(2,1)} %param.21) | copy-start | bytes 1572868
  41.1 11.4 %all-to-all-start = ((f32[16,2,416]{2,1,0:T(2,128)}), f32[16,2,416]{2,1,0:T(2,128)S(1)}, u32[]{:S(2)}, u32[]{:S(2)}) async-start(f32[16,2,416]{2,1,0:T(2,128)} %get-tuple-element.21), calls=%async_computation | async-start | bytes 131072 | tf_op jit(solution)/shard_map/all_to_all | solution.py:458
  54.7 10.5 %all-to-all-start.1 = ((bf16[16,2,384]{2,1,0:T(2,128)(2,1)}), bf16[16,2,384]{2,1,0:T(2,128)(2,1)S(1)}, u32[]{:S(2)}, u32[]{:S(2)}) async-start(bf16[16,2,384]{2,1,0:T(2,128)(2,1)} %bitcast.61), calls=%async_computation.1 | async-start | bytes 49152 | tf_op jit(solution)/shard_map/all_to_all | solution.py:471
  63.4 25.5 %copy-start.5 = (bf16[2,1,18432]{2,0,1:T(2,128)(2,1)S(1)}, bf16[2,1,18432]{2,0,1:T(2,128)(2,1)}, u32[]{:S(2)}) copy-start(bf16[2,1,18432]{2,0,1:T(2,128)(2,1)} %param.12) | copy-start | bytes 221188
  71.4 2.1 %collective-permute-start.8 = (bf16[16,18432]{1,0:T(8,128)(2,1)S(1)}, bf16[16,18432]{1,0:T(8,128)(2,1)S(1)}, u32[]{:S(2)}, u32[]{:S(2)}) collective-permute-start(bf16[16,18432]{1,0:T(8,128)(2,1)S(1)} %get-tuple-element.28), channel_id=1, source_target_pairs={{0,1},{1,0},{2,3},{3,2},{4,5},{5,4},{6,7},{7,6},{8,9},{9,8},{10,11... | collective-permute-start | bytes 1769480 | tf_op jit(solution)/shard_map/ppermute | solution.py:403
  73.9 8.3 %collective-permute-start.12 = (bf16[2,2,18432]{2,1,0:T(2,128)(2,1)S(1)}, bf16[2,2,18432]{2,1,0:T(2,128)(2,1)S(1)}, u32[]{:S(2)}, u32[]{:S(2)}) collective-permute-start(bf16[2,2,18432]{2,1,0:T(2,128)(2,1)S(1)} %get-tuple-element.34), channel_id=1, source_target_pairs={{0,2},{1,3},{2,0},{3,1},{4,6},{5,7},{6,4},{7,5},{8,10},{9,11},{10,... | collective-permute-start | bytes 442376 | tf_op jit(solution)/shard_map/ppermute | solution.py:403
  74.4 9.8 %collective-permute-start.9 = (bf16[2,18432]{1,0:T(2,128)(2,1)S(1)}, bf16[2,18432]{1,0:T(2,128)(2,1)S(1)}, u32[]{:S(2)}, u32[]{:S(2)}) collective-permute-start(bf16[2,18432]{1,0:T(2,128)(2,1)S(1)} %get-tuple-element.30), channel_id=1, source_target_pairs={{0,2},{1,3},{2,0},{3,1},{4,6},{5,7},{6,4},{7,5},{8,10},{9,11},{10,... | collective-permute-start | bytes 221192 | tf_op jit(solution)/shard_map/ppermute | solution.py:403
  76.0 8.1 %collective-permute-start.10 = (bf16[2,18432]{1,0:T(2,128)(2,1)S(1)}, bf16[2,18432]{1,0:T(2,128)(2,1)S(1)}, u32[]{:S(2)}, u32[]{:S(2)}) collective-permute-start(bf16[2,18432]{1,0:T(2,128)(2,1)S(1)} %get-tuple-element.31), channel_id=1, source_target_pairs={{0,4},{1,5},{2,6},{3,7},{4,0},{5,1},{6,2},{7,3},{8,12},{9,13},{10,... | collective-permute-start | bytes 221192 | tf_op jit(solution)/shard_map/ppermute | solution.py:403
  76.4 7.7 %collective-permute-start.11 = (bf16[2,18432]{1,0:T(2,128)(2,1)S(1)}, bf16[2,18432]{1,0:T(2,128)(2,1)S(1)}, u32[]{:S(2)}, u32[]{:S(2)}) collective-permute-start(bf16[2,18432]{1,0:T(2,128)(2,1)S(1)} %get-tuple-element.32), channel_id=1, source_target_pairs={{0,6},{1,7},{2,4},{3,5},{4,2},{5,3},{6,0},{7,1},{8,14},{9,15},{10,... | collective-permute-start | bytes 221192 | tf_op jit(solution)/shard_map/ppermute | solution.py:403
  82.5 5.3 %collective-permute-start.13 = (bf16[2,18432]{1,0:T(2,128)(2,1)S(1)}, bf16[2,18432]{1,0:T(2,128)(2,1)S(1)}, u32[]{:S(2)}, u32[]{:S(2)}) collective-permute-start(bf16[2,18432]{1,0:T(2,128)(2,1)S(1)} %get-tuple-element.35), channel_id=1, source_target_pairs={{0,8},{1,9},{2,10},{3,11},{4,12},{5,13},{6,14},{7,15},{8,0},{9,1},... | collective-permute-start | bytes 221192 | tf_op jit(solution)/shard_map/ppermute | solution.py:403
  82.6 6.3 %collective-permute-start.14 = (bf16[2,18432]{1,0:T(2,128)(2,1)S(1)}, bf16[2,18432]{1,0:T(2,128)(2,1)S(1)}, u32[]{:S(2)}, u32[]{:S(2)}) collective-permute-start(bf16[2,18432]{1,0:T(2,128)(2,1)S(1)} %get-tuple-element.36), channel_id=1, source_target_pairs={{0,12},{1,13},{2,14},{3,15},{4,8},{5,9},{6,10},{7,11},{8,4},{9,5},... | collective-permute-start | bytes 221192 | tf_op jit(solution)/shard_map/ppermute | solution.py:403

commit v8 on v7

--- a/solution.py
+++ b/solution.py
@@ -406,9 +406,17 @@
 def gather_rows(piece, devices):
     outer = min(4, devices // 2)
     inner = devices // (2 * outer)
-    near = [piece] + [swap(piece, 2 * inner * a, devices) for a in range(1, outer)]
-    far = [near] + [[swap(p, 2 * b, devices) for p in near] for b in range(1, inner)]
-    even = jnp.stack([far[b][a] for a in range(outer) for b in range(inner)])
+    middle = outer // 2
+    stride = 2 * inner
+    far = [swap(piece, stride * a, devices) for a in reversed(range(middle, outer))][::-1]
+    pieces = {(a, 0): far[a - middle] for a in range(middle, outer)}
+    for b in range(inner):
+        for a in range(middle):
+            pieces[a, b] = swap(piece, stride * a + 2 * b, devices) if a or b else piece
+    for b in range(1, inner):
+        passed = swap(jnp.stack(far), 2 * b, devices)
+        pieces.update({(a, b): passed[a - middle] for a in range(middle, outer)})
+    even = jnp.stack([pieces[a, b] for a in range(outer) for b in range(inner)])
     return even, swap(even, 1, devices)
 
 

time: 90 us -> 90.2 us (level)
    ppermute x15 -> x14, starting transfers between devices: 17 us -> 15.9 us  [swap(): return lax.ppermute(value, 'gx', [(i, i ^ bits) for i in range(devices)])]
    ppermute x15 -> x14, waiting for transfers between devices: 17.4 us -> 17.8 us  [swap(): return lax.ppermute(value, 'gx', [(i, i ^ bits) for i in range(devices)])]
  transfers between devices with their start and end apart: 17 -> 16, of which waited for: 10 -> 9; matrix products, arithmetic and copies ran while one was open for 1% -> 1% of each run, Pallas kernels for 11% -> 11%
where the time goes in v8:
time: 90.2 us; the launch traced here: 89.9 us
  Pallas kernels  36 us (40%)
  starting transfers between devices  24.9 us (28%)
  waiting for transfers between devices  21.7 us (24%)
  local copies, waits for them, and re-layouts  3.14 us (3%)
  between operations  1.64 us (2%)
  other arithmetic  1.58 us (2%)
  matrix products  0.98 us (1%)
    pallas_call x1, Pallas kernels, project(): pl.pallas_call(functools.partial(project_kernel, chunks), in_specs=[VMEM,...  19 us
    ppermute x14, waiting for transfers between devices, swap(): return lax.ppermute(value, 'gx', [(i, i ^ bits) for i in range(devices)])  17.8 us
    ppermute x14, starting transfers between devices, swap(): return lax.ppermute(value, 'gx', [(i, i ^ bits) for i in range(devices)])  15.9 us
    pallas_call x2, Pallas kernels, down_part(): pl.pallas_call(functools.partial(down_kernel, chunks, first * step), in_s...  9.56 us
    pallas_call x1, Pallas kernels, branch_parts(): pl.pallas_call(functools.partial(branch_kernel, chunks), in_specs=[VMEM,...  6.15 us
    all_to_all x1, starting transfers between devices, local(): lax.all_to_all(projected, 'gx', split_axis=0, concat_axis=0, tiled=True)  5.07 us
    all_to_all x1, starting transfers between devices, local(): lax.all_to_all(attended, 'gx', split_axis=0, concat_axis=0, tiled=True)  3.93 us
    unnamed x33, local copies, waits for them, and re-layouts  2.29 us
  transfers between devices with their start and end apart: 16, of which 9 were waited for; matrix products, arithmetic and copies ran while one was open for 1% of the time, Pallas kernels for 11%

profile of v8, /device:TPU:0, one launch (start us, length us, event | category | flops | bytes accessed | tf_op | source)
XLA Modules:
  0.0 89.9 jit_solution(16423487375754492343)
XLA Ops:
  0.0 1.0 %copy-done.4 = bf16[2,1,18432]{2,0,1:T(2,128)(2,1)S(1)} copy-done((bf16[2,1,18432]{2,0,1:T(2,128)(2,1)S(1)}, bf16[2,1,18432]{2,0,1:T(2,128)(2,1)}, u32[]{:S(2)}) %copy-start.4) | copy-done | bytes 73752
  1.1 0.0 slice-start.4
  1.1 0.0 slice-start.5
  1.1 0.5 shard_map.118.values_ref
  1.6 0.8 copy-done.3
  2.3 0.1 shard_map.119
  2.4 5.1 %collective-permute-start.4 = (bf16[2,18432]{1,0:T(2,128)(2,1)S(1)}, bf16[2,18432]{1,0:T(2,128)(2,1)S(1)}, u32[]{:S(2)}, u32[]{:S(2)}) collective-permute-start(bf16[2,18432]{1,0:T(2,128)(2,1)S(1)} %shard_map.119), channel_id=1, source_target_pairs={{0,12},{1,13},{2,14},{3,15},{4,8},{5,9},{6,10},{7,11},{8,4},{9,5},... | collective-permute-start | bytes 221192 | tf_op jit(solution)/shard_map/ppermute | solution.py:403
  7.5 0.0 collective-permute-start.3
  7.6 1.7 %collective-permute-start.2 = (bf16[2,18432]{1,0:T(2,128)(2,1)S(1)}, bf16[2,18432]{1,0:T(2,128)(2,1)S(1)}, u32[]{:S(2)}, u32[]{:S(2)}) collective-permute-start(bf16[2,18432]{1,0:T(2,128)(2,1)S(1)} %shard_map.119), channel_id=1, source_target_pairs={{0,6},{1,7},{2,4},{3,5},{4,2},{5,3},{6,0},{7,1},{8,14},{9,15},{10,... | collective-permute-start | bytes 221192 | tf_op jit(solution)/shard_map/ppermute | solution.py:403
  9.3 1.2 %collective-permute-start.1 = (bf16[2,18432]{1,0:T(2,128)(2,1)S(1)}, bf16[2,18432]{1,0:T(2,128)(2,1)S(1)}, u32[]{:S(2)}, u32[]{:S(2)}) collective-permute-start(bf16[2,18432]{1,0:T(2,128)(2,1)S(1)} %shard_map.119), channel_id=1, source_target_pairs={{0,4},{1,5},{2,6},{3,7},{4,0},{5,1},{6,2},{7,3},{8,12},{9,13},{10,... | collective-permute-start | bytes 221192 | tf_op jit(solution)/shard_map/ppermute | solution.py:403
  10.5 0.5 collective-permute-start
  11.0 0.1 bitcast_dynamic-update-slice_fusion.3
  11.1 0.0 collective-permute-done.4
  11.1 2.8 %collective-permute-done.3 = bf16[2,18432]{1,0:T(2,128)(2,1)S(1)} collective-permute-done((bf16[2,18432]{1,0:T(2,128)(2,1)S(1)}, bf16[2,18432]{1,0:T(2,128)(2,1)S(1)}, u32[]{:S(2)}, u32[]{:S(2)}) %collective-permute-start.3) | collective-permute-done | bytes 73760 | tf_op jit(solution)/shard_map/ppermute | solution.py:403
  13.9 0.2 pad_maximum_fusion
  14.1 1.6 %collective-permute-start.5 = (bf16[2,2,18432]{2,1,0:T(2,128)(2,1)S(1)}, bf16[2,2,18432]{2,1,0:T(2,128)(2,1)S(1)}, u32[]{:S(2)}, u32[]{:S(2)}) collective-permute-start(bf16[2,2,18432]{2,1,0:T(2,128)(2,1)S(1)} %pad_maximum_fusion), channel_id=1, source_target_pairs={{0,2},{1,3},{2,0},{3,1},{4,6},{5,7},{6,4},{7,5},{8,10},{9,11},{10,... | collective-permute-start | bytes 442376 | tf_op jit(solution)/shard_map/ppermute | solution.py:403
  15.6 0.0 collective-permute-done
  15.6 0.1 bitcast_dynamic-update-slice_fusion.2
  15.7 0.0 collective-permute-done.1
  15.7 0.1 bitcast_dynamic-update-slice_fusion.1
  15.8 0.0 collective-permute-done.2
  15.8 0.1 bitcast_dynamic-update-slice_fusion
  15.9 0.1 constant_dynamic-update-slice_fusion.1
  15.9 3.4 %collective-permute-done.5 = bf16[2,2,18432]{2,1,0:T(2,128)(2,1)S(1)} collective-permute-done((bf16[2,2,18432]{2,1,0:T(2,128)(2,1)S(1)}, bf16[2,2,18432]{2,1,0:T(2,128)(2,1)S(1)}, u32[]{:S(2)}, u32[]{:S(2)}) %collective-permute-start.5) | collective-permute-done | bytes 147488 | tf_op jit(solution)/shard_map/ppermute | solution.py:403
  19.3 0.1 slice_dynamic-update-slice_fusion.1
  19.4 0.1 constant_dynamic-update-slice_fusion
  19.4 0.1 slice_dynamic-update-slice_fusion.even_ref
  19.5 0.1 collective-permute-start.6
  20.9 0.1 multiply_cosine_fusion.1
  21.0 0.5 collective-permute-done.6.odd_ref
  21.6 19.0 %shard_map.120 = (f32[16,2,416]{2,1,0:T(2,128)}, bf16[32,576]{1,0:T(8,128)(2,1)S(1)}) custom-call(bf16[8,2,18432]{2,1,0:T(2,128)(2,1)S(1)} %slice_dynamic-update-slice_fusion.even_ref, bf16[8,2,18432]{2,1,0:T(2,128)(2,1)S(1)} %collective-permute-done.6.odd_ref, bf16[384,18432]{1,0:T(8,128)(2,1)S(1)} %copy-done.1, bf16[576,18432]{1,0:T(8,128)(2,1)S(1)} %bitcast.61, ...), custom_call_target="tpu_custom_call" | custom-call | flops 1849688064 | bytes 57802752 | tf_op jit(solution)/shard_map/pallas_call | solution.py:143
  40.6 0.0 copy-start.6
  40.7 5.1 %all-to-all-start = ((f32[16,2,416]{2,1,0:T(2,128)}), f32[16,2,416]{2,1,0:T(2,128)S(1)}, u32[]{:S(2)}, u32[]{:S(2)}) async-start(f32[16,2,416]{2,1,0:T(2,128)} %get-tuple-element.21), calls=%async_computation | async-start | bytes 131072 | tf_op jit(solution)/shard_map/all_to_all | solution.py:466
  45.7 4.8 %shard_map.121.first_ref = f32[32,9216]{1,0:T(8,128)S(1)} custom-call(bf16[32,576]{1,0:T(8,128)(2,1)S(1)} %get-tuple-element.26.hidden_ref, bf16[576,18432]{1,0:T(8,128)(2,1)} %w_ref.4), custom_call_target="tpu_custom_call" | custom-call | flops 339738624 | bytes 10616832 | tf_op jit(solution)/shard_map/pallas_call | solution.py:196
  50.5 2.1 %all-to-all-done = f32[16,2,416]{2,1,0:T(2,128)S(1)} async-done(((f32[16,2,416]{2,1,0:T(2,128)}), f32[16,2,416]{2,1,0:T(2,128)S(1)}, u32[]{:S(2)}, u32[]{:S(2)}) %all-to-all-start) | async-done | bytes 53280 | tf_op jit(solution)/shard_map/all_to_all | solution.py:466
  52.7 0.1 reshape.338
  52.8 0.1 fusion.27
  52.9 0.4 fusion.31
  53.3 0.2 fusion.32
  53.5 0.2 fusion.6
  53.7 0.3 fusion.3
  53.9 0.2 fusion.1
  54.2 0.6 copy.17
  54.8 3.9 %all-to-all-start.1 = ((bf16[16,2,384]{2,1,0:T(2,128)(2,1)}), bf16[16,2,384]{2,1,0:T(2,128)(2,1)S(1)}, u32[]{:S(2)}, u32[]{:S(2)}) async-start(bf16[16,2,384]{2,1,0:T(2,128)(2,1)} %bitcast.57), calls=%async_computation.1 | async-start | bytes 49152 | tf_op jit(solution)/shard_map/all_to_all | solution.py:479
  58.7 4.8 %shard_map.122.second_ref = f32[32,9216]{1,0:T(8,128)S(1)} custom-call(bf16[32,576]{1,0:T(8,128)(2,1)S(1)} %get-tuple-element.26.hidden_ref, bf16[576,18432]{1,0:T(8,128)(2,1)} %w_ref.4), custom_call_target="tpu_custom_call" | custom-call | flops 339738624 | bytes 10616832 | tf_op jit(solution)/shard_map/pallas_call | solution.py:196
  63.5 0.0 copy-start.5
  63.5 1.8 %all-to-all-done.1.attended_ref = bf16[16,2,384]{2,1,0:T(2,128)(2,1)S(1)} async-done(((bf16[16,2,384]{2,1,0:T(2,128)(2,1)}), bf16[16,2,384]{2,1,0:T(2,128)(2,1)S(1)}, u32[]{:S(2)}, u32[]{:S(2)}) %all-to-all-start.1) | async-done | bytes 24608 | tf_op jit(solution)/shard_map/all_to_all | solution.py:479
  65.3 6.2 %shard_map.123 = (f32[16,18432]{1,0:T(8,128)S(1)}, bf16[16,18432]{1,0:T(8,128)(2,1)S(1)}) custom-call(bf16[16,2,384]{2,1,0:T(2,128)(2,1)S(1)} %all-to-all-done.1.attended_ref, f32[32,9216]{1,0:T(8,128)S(1)} %shard_map.121.first_ref, f32[32,9216]{1,0:T(8,128)S(1)} %shard_map.122.second_ref, bf16[384,18432]{1,0:T(8,128)(2,1)} %w_ref.5), custom_call_target="tpu_custom_call" | custom-call | flops 452984832 | bytes 14155776 | tf_op jit(solution)/shard_map/pallas_call | solution.py:270
  71.5 0.1 collective-permute-start.7
  71.5 2.0 %collective-permute-done.7.came_ref = bf16[16,18432]{1,0:T(8,128)(2,1)S(1)} collective-permute-done((bf16[16,18432]{1,0:T(8,128)(2,1)S(1)}, bf16[16,18432]{1,0:T(8,128)(2,1)S(1)}, u32[]{:S(2)}, u32[]{:S(2)}) %collective-permute-start.7) | collective-permute-done | bytes 589856 | tf_op jit(solution)/shard_map/ppermute | solution.py:403
  73.5 0.5 shard_map.124
  74.0 0.5 collective-permute-start.11
  74.5 1.6 %collective-permute-start.8 = (bf16[2,18432]{1,0:T(2,128)(2,1)S(1)}, bf16[2,18432]{1,0:T(2,128)(2,1)S(1)}, u32[]{:S(2)}, u32[]{:S(2)}) collective-permute-start(bf16[2,18432]{1,0:T(2,128)(2,1)S(1)} %get-tuple-element.30), channel_id=1, source_target_pairs={{0,2},{1,3},{2,0},{3,1},{4,6},{5,7},{6,4},{7,5},{8,10},{9,11},{10,... | collective-permute-start | bytes 221192 | tf_op jit(solution)/shard_map/ppermute | solution.py:403
  76.1 0.4 collective-permute-start.9
  76.5 1.5 %collective-permute-start.10 = (bf16[2,18432]{1,0:T(2,128)(2,1)S(1)}, bf16[2,18432]{1,0:T(2,128)(2,1)S(1)}, u32[]{:S(2)}, u32[]{:S(2)}) collective-permute-start(bf16[2,18432]{1,0:T(2,128)(2,1)S(1)} %get-tuple-element.32), channel_id=1, source_target_pairs={{0,6},{1,7},{2,4},{3,5},{4,2},{5,3},{6,0},{7,1},{8,14},{9,15},{10,... | collective-permute-start | bytes 221192 | tf_op jit(solution)/shard_map/ppermute | solution.py:403
  78.0 4.4 %collective-permute-done.11.refs_0_ = bf16[2,2,18432]{2,1,0:T(2,128)(2,1)S(1)} collective-permute-done((bf16[2,2,18432]{2,1,0:T(2,128)(2,1)S(1)}, bf16[2,2,18432]{2,1,0:T(2,128)(2,1)S(1)}, u32[]{:S(2)}, u32[]{:S(2)}) %collective-permute-start.11) | collective-permute-done | bytes 147488 | tf_op jit(solution)/shard_map/ppermute | solution.py:403
  82.3 0.2 shard_map.125
  82.6 0.2 collective-permute-start.12
  82.7 1.5 %collective-permute-start.13 = (bf16[2,18432]{1,0:T(2,128)(2,1)S(1)}, bf16[2,18432]{1,0:T(2,128)(2,1)S(1)}, u32[]{:S(2)}, u32[]{:S(2)}) collective-permute-start(bf16[2,18432]{1,0:T(2,128)(2,1)S(1)} %get-tuple-element.36), channel_id=1, source_target_pairs={{0,12},{1,13},{2,14},{3,15},{4,8},{5,9},{6,10},{7,11},{8,4},{9,5},... | collective-permute-start | bytes 221192 | tf_op jit(solution)/shard_map/ppermute | solution.py:403
  84.2 0.0 collective-permute-done.9
  84.2 0.0 collective-permute-done.10
  84.3 3.7 %collective-permute-done.12 = bf16[2,18432]{1,0:T(2,128)(2,1)S(1)} collective-permute-done((bf16[2,18432]{1,0:T(2,128)(2,1)S(1)}, bf16[2,18432]{1,0:T(2,128)(2,1)S(1)}, u32[]{:S(2)}, u32[]{:S(2)}) %collective-permute-start.12) | collective-permute-done | bytes 73760 | tf_op jit(solution)/shard_map/ppermute | solution.py:403
  87.9 1.1 %collective-permute-done.13 = bf16[2,18432]{1,0:T(2,128)(2,1)S(1)} collective-permute-done((bf16[2,18432]{1,0:T(2,128)(2,1)S(1)}, bf16[2,18432]{1,0:T(2,128)(2,1)S(1)}, u32[]{:S(2)}, u32[]{:S(2)}) %collective-permute-start.13) | collective-permute-done | bytes 73760 | tf_op jit(solution)/shard_map/ppermute | solution.py:403
  89.0 0.9 fusion.9
  (36 shorter events, 0.2 us)
Async XLA Ops:
  0.0 52.9 %copy-start = (bf16[1,1024,256]{2,1,0:T(8,128)(2,1)S(1)}, bf16[1,1024,256]{2,1,0:T(8,128)(2,1)}, u32[]{:S(2)}) copy-start(bf16[1,1024,256]{2,1,0:T(8,128)(2,1)} %param.20) | copy-start | bytes 1572868
  0.0 21.6 %slice-start = ((s8[21233664]{0:T(1024)(128)(4,1)}), s8[4194304]{0:T(1024)(128)(4,1)S(1)}, s32[]{:S(2)}) async-start(s8[21233664]{0:T(1024)(128)(4,1)} %bitcast.60), calls=%async_computation.2 | async-start | bytes 8388608
  0.0 1.0 %copy-start.4 = (bf16[2,1,18432]{2,0,1:T(2,128)(2,1)S(1)}, bf16[2,1,18432]{2,0,1:T(2,128)(2,1)}, u32[]{:S(2)}) copy-start(bf16[2,1,18432]{2,0,1:T(2,128)(2,1)} %param.12) | copy-start | bytes 221188
  1.0 1.3 %copy-start.3 = (f32[18432]{0:T(1024)S(1)}, f32[18432]{0:T(1024)}, u32[]{:S(2)}) copy-start(f32[18432]{0:T(1024)} %param.13) | copy-start | bytes 221188
  1.0 20.5 %slice-start.1 = ((s8[21233664]{0:T(1024)(128)(4,1)}), s8[4194304]{0:T(1024)(128)(4,1)S(1)}, s32[]{:S(2)}) async-start(s8[21233664]{0:T(1024)(128)(4,1)} %bitcast.60), calls=%async_computation.3 | async-start | bytes 8388608
  1.0 20.5 %slice-start.2 = ((s8[21233664]{0:T(1024)(128)(4,1)}), s8[4194304]{0:T(1024)(128)(4,1)S(1)}, s32[]{:S(2)}) async-start(s8[21233664]{0:T(1024)(128)(4,1)} %bitcast.60), calls=%async_computation.4 | async-start | bytes 8388608
  1.0 20.5 %slice-start.3 = ((s8[21233664]{0:T(1024)(128)(4,1)}), s8[4194304]{0:T(1024)(128)(4,1)S(1)}, s32[]{:S(2)}) async-start(s8[21233664]{0:T(1024)(128)(4,1)} %bitcast.60), calls=%async_computation.5 | async-start | bytes 8388608
  1.1 20.5 %slice-start.4 = ((s8[21233664]{0:T(1024)(128)(4,1)}), s8[4194304]{0:T(1024)(128)(4,1)S(1)}, s32[]{:S(2)}) async-start(s8[21233664]{0:T(1024)(128)(4,1)} %bitcast.60), calls=%async_computation.6 | async-start | bytes 8388608
  1.1 20.5 %slice-start.5 = ((s8[21233664]{0:T(1024)(128)(4,1)}), s8[262144]{0:T(1024)(128)(4,1)S(1)}, s32[]{:S(2)}) async-start(s8[21233664]{0:T(1024)(128)(4,1)} %bitcast.60), calls=%async_computation.7 | async-start | bytes 524288
  1.1 20.5 %copy-start.1 = (bf16[384,18432]{1,0:T(8,128)(2,1)S(1)}, bf16[384,18432]{1,0:T(8,128)(2,1)}, u32[]{:S(2)}) copy-start(bf16[384,18432]{1,0:T(8,128)(2,1)} %wq_ref.1) | copy-start | bytes 42467332
  1.1 20.5 %copy-start.2 = (bf16[32,18432]{1,0:T(8,128)(2,1)S(1)}, bf16[32,18432]{1,0:T(8,128)(2,1)}, u32[]{:S(2)}) copy-start(bf16[32,18432]{1,0:T(8,128)(2,1)} %wk_ref.1) | copy-start | bytes 3538948
  2.4 8.7 %collective-permute-start.4 = (bf16[2,18432]{1,0:T(2,128)(2,1)S(1)}, bf16[2,18432]{1,0:T(2,128)(2,1)S(1)}, u32[]{:S(2)}, u32[]{:S(2)}) collective-permute-start(bf16[2,18432]{1,0:T(2,128)(2,1)S(1)} %shard_map.119), channel_id=1, source_target_pairs={{0,12},{1,13},{2,14},{3,15},{4,8},{5,9},{6,10},{7,11},{8,4},{9,5},... | collective-permute-start | bytes 221192 | tf_op jit(solution)/shard_map/ppermute | solution.py:403
  7.5 6.3 %collective-permute-start.3 = (bf16[2,18432]{1,0:T(2,128)(2,1)S(1)}, bf16[2,18432]{1,0:T(2,128)(2,1)S(1)}, u32[]{:S(2)}, u32[]{:S(2)}) collective-permute-start(bf16[2,18432]{1,0:T(2,128)(2,1)S(1)} %shard_map.119), channel_id=1, source_target_pairs={{0,8},{1,9},{2,10},{3,11},{4,12},{5,13},{6,14},{7,15},{8,0},{9,1},... | collective-permute-start | bytes 221192 | tf_op jit(solution)/shard_map/ppermute | solution.py:403
  7.6 8.2 %collective-permute-start.2 = (bf16[2,18432]{1,0:T(2,128)(2,1)S(1)}, bf16[2,18432]{1,0:T(2,128)(2,1)S(1)}, u32[]{:S(2)}, u32[]{:S(2)}) collective-permute-start(bf16[2,18432]{1,0:T(2,128)(2,1)S(1)} %shard_map.119), channel_id=1, source_target_pairs={{0,6},{1,7},{2,4},{3,5},{4,2},{5,3},{6,0},{7,1},{8,14},{9,15},{10,... | collective-permute-start | bytes 221192 | tf_op jit(solution)/shard_map/ppermute | solution.py:403
  9.3 6.4 %collective-permute-start.1 = (bf16[2,18432]{1,0:T(2,128)(2,1)S(1)}, bf16[2,18432]{1,0:T(2,128)(2,1)S(1)}, u32[]{:S(2)}, u32[]{:S(2)}) collective-permute-start(bf16[2,18432]{1,0:T(2,128)(2,1)S(1)} %shard_map.119), channel_id=1, source_target_pairs={{0,4},{1,5},{2,6},{3,7},{4,0},{5,1},{6,2},{7,3},{8,12},{9,13},{10,... | collective-permute-start | bytes 221192 | tf_op jit(solution)/shard_map/ppermute | solution.py:403
  10.5 5.1 %collective-permute-start = (bf16[2,18432]{1,0:T(2,128)(2,1)S(1)}, bf16[2,18432]{1,0:T(2,128)(2,1)S(1)}, u32[]{:S(2)}, u32[]{:S(2)}) collective-permute-start(bf16[2,18432]{1,0:T(2,128)(2,1)S(1)} %shard_map.119), channel_id=1, source_target_pairs={{0,2},{1,3},{2,0},{3,1},{4,6},{5,7},{6,4},{7,5},{8,10},{9,11},{10,... | collective-permute-start | bytes 221192 | tf_op jit(solution)/shard_map/ppermute | solution.py:403
  14.1 5.2 %collective-permute-start.5 = (bf16[2,2,18432]{2,1,0:T(2,128)(2,1)S(1)}, bf16[2,2,18432]{2,1,0:T(2,128)(2,1)S(1)}, u32[]{:S(2)}, u32[]{:S(2)}) collective-permute-start(bf16[2,2,18432]{2,1,0:T(2,128)(2,1)S(1)} %pad_maximum_fusion), channel_id=1, source_target_pairs={{0,2},{1,3},{2,0},{3,1},{4,6},{5,7},{6,4},{7,5},{8,10},{9,11},{10,... | collective-permute-start | bytes 442376 | tf_op jit(solution)/shard_map/ppermute | solution.py:403
  19.5 2.1 %collective-permute-start.6 = (bf16[8,2,18432]{2,1,0:T(2,128)(2,1)S(1)}, bf16[8,2,18432]{2,1,0:T(2,128)(2,1)S(1)}, u32[]{:S(2)}, u32[]{:S(2)}) collective-permute-start(bf16[8,2,18432]{2,1,0:T(2,128)(2,1)S(1)} %slice_dynamic-update-slice_fusion.even_ref), channel_id=1, source_target_pairs={{0,1},{1,0},{2,3},{3,2},{4,5},{5,4},{6,7},{7,6},{8,9},{9,8},{10,11... | collective-permute-start | bytes 1769480 | tf_op jit(solution)/shard_map/ppermute | solution.py:403
  40.6 13.0 %copy-start.6 = (bf16[1,1024,256]{2,1,0:T(8,128)(2,1)S(1)}, bf16[1,1024,256]{2,1,0:T(8,128)(2,1)}, u32[]{:S(2)}) copy-start(bf16[1,1024,256]{2,1,0:T(8,128)(2,1)} %param.21) | copy-start | bytes 1572868
  40.7 12.0 %all-to-all-start = ((f32[16,2,416]{2,1,0:T(2,128)}), f32[16,2,416]{2,1,0:T(2,128)S(1)}, u32[]{:S(2)}, u32[]{:S(2)}) async-start(f32[16,2,416]{2,1,0:T(2,128)} %get-tuple-element.21), calls=%async_computation | async-start | bytes 131072 | tf_op jit(solution)/shard_map/all_to_all | solution.py:466
  54.8 10.5 %all-to-all-start.1 = ((bf16[16,2,384]{2,1,0:T(2,128)(2,1)}), bf16[16,2,384]{2,1,0:T(2,128)(2,1)S(1)}, u32[]{:S(2)}, u32[]{:S(2)}) async-start(bf16[16,2,384]{2,1,0:T(2,128)(2,1)} %bitcast.57), calls=%async_computation.1 | async-start | bytes 49152 | tf_op jit(solution)/shard_map/all_to_all | solution.py:479
  63.5 25.5 %copy-start.5 = (bf16[2,1,18432]{2,0,1:T(2,128)(2,1)S(1)}, bf16[2,1,18432]{2,0,1:T(2,128)(2,1)}, u32[]{:S(2)}) copy-start(bf16[2,1,18432]{2,0,1:T(2,128)(2,1)} %param.12) | copy-start | bytes 221188
  71.5 2.1 %collective-permute-start.7 = (bf16[16,18432]{1,0:T(8,128)(2,1)S(1)}, bf16[16,18432]{1,0:T(8,128)(2,1)S(1)}, u32[]{:S(2)}, u32[]{:S(2)}) collective-permute-start(bf16[16,18432]{1,0:T(8,128)(2,1)S(1)} %get-tuple-element.28), channel_id=1, source_target_pairs={{0,1},{1,0},{2,3},{3,2},{4,5},{5,4},{6,7},{7,6},{8,9},{9,8},{10,11... | collective-permute-start | bytes 1769480 | tf_op jit(solution)/shard_map/ppermute | solution.py:403
  74.0 8.3 %collective-permute-start.11 = (bf16[2,2,18432]{2,1,0:T(2,128)(2,1)S(1)}, bf16[2,2,18432]{2,1,0:T(2,128)(2,1)S(1)}, u32[]{:S(2)}, u32[]{:S(2)}) collective-permute-start(bf16[2,2,18432]{2,1,0:T(2,128)(2,1)S(1)} %get-tuple-element.34), channel_id=1, source_target_pairs={{0,2},{1,3},{2,0},{3,1},{4,6},{5,7},{6,4},{7,5},{8,10},{9,11},{10,... | collective-permute-start | bytes 442376 | tf_op jit(solution)/shard_map/ppermute | solution.py:403
  74.5 9.8 %collective-permute-start.8 = (bf16[2,18432]{1,0:T(2,128)(2,1)S(1)}, bf16[2,18432]{1,0:T(2,128)(2,1)S(1)}, u32[]{:S(2)}, u32[]{:S(2)}) collective-permute-start(bf16[2,18432]{1,0:T(2,128)(2,1)S(1)} %get-tuple-element.30), channel_id=1, source_target_pairs={{0,2},{1,3},{2,0},{3,1},{4,6},{5,7},{6,4},{7,5},{8,10},{9,11},{10,... | collective-permute-start | bytes 221192 | tf_op jit(solution)/shard_map/ppermute | solution.py:403
  76.1 8.1 %collective-permute-start.9 = (bf16[2,18432]{1,0:T(2,128)(2,1)S(1)}, bf16[2,18432]{1,0:T(2,128)(2,1)S(1)}, u32[]{:S(2)}, u32[]{:S(2)}) collective-permute-start(bf16[2,18432]{1,0:T(2,128)(2,1)S(1)} %get-tuple-element.31), channel_id=1, source_target_pairs={{0,4},{1,5},{2,6},{3,7},{4,0},{5,1},{6,2},{7,3},{8,12},{9,13},{10,... | collective-permute-start | bytes 221192 | tf_op jit(solution)/shard_map/ppermute | solution.py:403
  76.5 7.7 %collective-permute-start.10 = (bf16[2,18432]{1,0:T(2,128)(2,1)S(1)}, bf16[2,18432]{1,0:T(2,128)(2,1)S(1)}, u32[]{:S(2)}, u32[]{:S(2)}) collective-permute-start(bf16[2,18432]{1,0:T(2,128)(2,1)S(1)} %get-tuple-element.32), channel_id=1, source_target_pairs={{0,6},{1,7},{2,4},{3,5},{4,2},{5,3},{6,0},{7,1},{8,14},{9,15},{10,... | collective-permute-start | bytes 221192 | tf_op jit(solution)/shard_map/ppermute | solution.py:403
  82.6 5.3 %collective-permute-start.12 = (bf16[2,18432]{1,0:T(2,128)(2,1)S(1)}, bf16[2,18432]{1,0:T(2,128)(2,1)S(1)}, u32[]{:S(2)}, u32[]{:S(2)}) collective-permute-start(bf16[2,18432]{1,0:T(2,128)(2,1)S(1)} %get-tuple-element.35), channel_id=1, source_target_pairs={{0,8},{1,9},{2,10},{3,11},{4,12},{5,13},{6,14},{7,15},{8,0},{9,1},... | collective-permute-start | bytes 221192 | tf_op jit(solution)/shard_map/ppermute | solution.py:403
  82.7 6.3 %collective-permute-start.13 = (bf16[2,18432]{1,0:T(2,128)(2,1)S(1)}, bf16[2,18432]{1,0:T(2,128)(2,1)S(1)}, u32[]{:S(2)}, u32[]{:S(2)}) collective-permute-start(bf16[2,18432]{1,0:T(2,128)(2,1)S(1)} %get-tuple-element.36), channel_id=1, source_target_pairs={{0,12},{1,13},{2,14},{3,15},{4,8},{5,9},{6,10},{7,11},{8,4},{9,5},... | collective-permute-start | bytes 221192 | tf_op jit(solution)/shard_map/ppermute | solution.py:403
